TPU v7x, 768 devices: a whole 4x8x12 slice. The times are simulated.
768 devices in a mesh: proto: 24 (over z, core), batch: 32 (over y, x).
Axes of the slice: x: 4, y: 8, z: 12, core: 2. Of those that a mesh axis runs over, the one named last changes fastest.
Arguments:
- teacher: bfloat16 [8192, 256], P('batch'), may hold values from -6 to 6
- student: bfloat16 [8192, 256], P('batch'), may hold values from -6 to 6
- prototypes: bfloat16 [256, 67584], P(None, 'proto'), may hold values from -0.375 to 0.375
- gain: float32 [67584], P('proto'), may hold values from 1 to 2.5
Outputs:
- targets: bfloat16 [8192, 67584], P('batch', 'proto')
- prototype_grad: float32 [256, 67584], P('batch', 'proto')
All inputs are finite; a program needn't handle non-finite values.
Results may differ from a plain program's by a relative error of at most 0.01.
The roundings to bfloat16 on the way count: a program that leaves them out, or rounds other values in their place, can miss the bound.
Values sent between devices are 32-bit elements; how exact they have to be, the bound alone decides.
No kernel may reach another device: no remote copies, remote signals or barrier semaphores. Data moves between devices by JAX's collectives and lax.ppermute only.
A program may use at most 32 MiB of HBM per device.

v0:
```python
import jax
import jax.numpy as jnp
from jax import lax
from jax.sharding import PartitionSpec as P

ITERS = 3


teacher_temp = 0.04
student_temp = 0.1
eps = 1e-06


def unit_rows(x):
    xf = x.astype(jnp.float32)
    return (xf * lax.rsqrt(jnp.sum(xf * xf, 1, keepdims=True) + eps)).astype(jnp.bfloat16)


def row_total(partial_value):
    return lax.psum(partial_value, "proto")


def column_scale(partial_value):
    summed = lax.psum(partial_value, "batch")
    return 1.0 / summed


def local(teacher, student, prototypes, gain):
    wf = prototypes.astype(jnp.float32)
    proto_n = (wf * lax.rsqrt(jnp.sum(wf * wf, 0, keepdims=True) + eps) * gain[None, :]).astype(
        jnp.bfloat16
    )
    count = proto_n.shape[1] * lax.axis_size("proto")
    rows_all = teacher.shape[0] * lax.axis_size("batch")
    teacher_n = unit_rows(teacher)
    student_n = unit_rows(student)
    expo = jnp.exp(
        jnp.dot(teacher_n, proto_n, preferred_element_type=jnp.float32) / teacher_temp
    ).astype(jnp.bfloat16)
    expo_wide = lax.optimization_barrier(expo).astype(jnp.float32)
    logits = jnp.dot(student_n, proto_n, preferred_element_type=jnp.float32) / student_temp
    local_total = jnp.sum(jnp.exp(logits), 1)
    scale_v = jnp.ones((teacher.shape[0],), jnp.float32)
    for step in range(ITERS):
        scale_u = column_scale(jnp.dot(scale_v, expo_wide, precision=lax.Precision.HIGHEST))
        partial_r = jnp.dot(expo_wide, scale_u, precision=lax.Precision.HIGHEST)
        if step + 1 == ITERS:
            row_tot = row_total(partial_r)
        else:
            row_tot = row_total(partial_r)
        scale_v = 1.0 / row_tot
    total = lax.psum(local_total, "proto")
    assign = expo_wide * scale_u[None, :] * scale_v[:, None]
    targets = (count * assign).astype(jnp.bfloat16)
    prob = jnp.exp(logits - jnp.log(total)[:, None])
    diff = (count * (prob - assign)).astype(jnp.bfloat16)
    inv_root = 1.0 / jnp.sqrt(jnp.float32(rows_all))
    grad = lax.psum_scatter(
        jnp.dot(student_n.T, diff, preferred_element_type=jnp.float32) * inv_root,
        "batch",
        scatter_dimension=0,
        tiled=True,
    )
    return (targets, grad)


def solution(mesh):
    return jax.shard_map(
        local,
        mesh=mesh,
        in_specs=(P("batch", None), P("batch", None), P(None, "proto"), P("proto")),
        out_specs=(P("batch", "proto"), P("batch", "proto")),
        check_vma=False,
    )
```

profile of v0, /device:TPU:16, one launch (start us, length us, event | category | flops | bytes accessed | tf_op | source)
XLA Modules:
  0.0 785.0 jit_solution(7777108676039924743)
XLA Ops:
  7.2 0.0 reduce-scatter.2.cloned.1.call-start
  7.2 1.0 fusion.11
  8.2 1.0 fusion.13
  9.3 1.7 fusion.2
  11.0 2.2 fusion.1
  13.2 0.7 convolution_reduce_fusion.2
  13.9 134.4 %psum.49 = f32[2816]{0:T(1024)S(1)} all-reduce(f32[2816]{0:T(1024)S(1)} %convolution_reduce_fusion.2), channel_id=1, replica_groups=mesh['proto'=24,'batch'=32] {'batch'}, use_global_device_ids=true, to_apply=%region_2.0 | all-reduce | flops 2816 | bytes 22528 | tf_op jit(solution)/shard_map/psum | solution.py:24
  148.3 1.2 fusion.22
  149.5 40.7 %psum.50 = f32[256]{0:T(256)S(1)} all-reduce(f32[256]{0:T(256)S(1)} %bitcast.19), channel_id=1, replica_groups=mesh['proto'=24,'batch'=32] {'proto'}, use_global_device_ids=true, to_apply=%region_3.0 | all-reduce | flops 256 | bytes 2048 | tf_op jit(solution)/shard_map/psum | solution.py:20
  190.2 0.0 copy-start.2
  190.2 0.7 convolution_reduce_fusion.1
  190.9 137.7 %psum.51 = f32[2816]{0:T(1024)S(1)} all-reduce(f32[2816]{0:T(1024)S(1)} %convolution_reduce_fusion.1), channel_id=1, replica_groups=mesh['proto'=24,'batch'=32] {'batch'}, use_global_device_ids=true, to_apply=%region_4.0 | all-reduce | flops 2816 | bytes 22528 | tf_op jit(solution)/shard_map/psum | solution.py:24
  328.7 1.2 fusion.23
  329.8 34.7 %psum.52 = f32[256]{0:T(256)S(1)} all-reduce(f32[256]{0:T(256)S(1)} %bitcast.20), channel_id=1, replica_groups=mesh['proto'=24,'batch'=32] {'proto'}, use_global_device_ids=true, to_apply=%region_5.0 | all-reduce | flops 256 | bytes 2048 | tf_op jit(solution)/shard_map/psum | solution.py:20
  364.6 0.7 convolution_reduce_fusion
  365.3 137.7 %psum.53 = f32[2816]{0:T(1024)S(1)} all-reduce(f32[2816]{0:T(1024)S(1)} %convolution_reduce_fusion), channel_id=1, replica_groups=mesh['proto'=24,'batch'=32] {'batch'}, use_global_device_ids=true, to_apply=%region_6.0 | all-reduce | flops 2816 | bytes 22528 | tf_op jit(solution)/shard_map/psum | solution.py:24
  503.0 1.2 fusion.24
  504.2 0.1 copy-done.1
  504.3 2.4 exponential_reduce_fusion
  506.7 34.7 %all-reduce = (f32[256]{0:T(256)S(1)}, f32[256]{0:T(256)S(1)}) all-reduce(f32[256]{0:T(256)S(1)} %bitcast.18, f32[256]{0:T(256)S(1)} %get-tuple-element.4), channel_id=1, replica_groups=mesh['proto'=24,'batch'=32] {'proto'}, use_global_device_ids=true, to_apply=%region_7.0 | all-reduce | flops 512 | bytes 4096 | tf_op jit(solution)/shard_map/psum | solution.py:20
  541.4 4.7 convolution_multiply_fusion
  546.1 0.0 reduce-scatter.2.cloned.1.call-update
  546.2 1.5 multiply_convert_fusion.1
  547.7 230.4 %reduce-scatter.2.cloned.1.call-done = f32[8,2816]{1,0:T(8,128)} async-done(((f32[256,2816]{1,0:T(8,128)}), f32[8,2816]{1,0:T(8,128)}) %reduce-scatter.2.cloned.1.call-update) | async-done | bytes 90128 | tf_op jit(solution)/shard_map/reduce_scatter | solution.py:58
  (17 shorter events, 0.1 us)
Async XLA Ops:
  7.2 771.0 %reduce-scatter.2.cloned.1.call-start = ((), (), s32[]{:S(2)}) async-start(), calls=%async_computation.1 | async-start | bytes 2973696 | tf_op jit(solution)/shard_map/reduce_scatter | solution.py:58
  190.2 314.0 %copy-start = (bf16[256,2816]{1,0:T(8,128)(2,1)S(1)}, bf16[256,2816]{1,0:T(8,128)(2,1)}, u32[]{:S(2)}) copy-start(bf16[256,2816]{1,0:T(8,128)(2,1)} %param.6) | copy-start | bytes 4325380
  190.2 314.1 %copy-start.1 = (bf16[256,256]{1,0:T(8,128)(2,1)S(1)}, bf16[256,256]{1,0:T(8,128)(2,1)}, u32[]{:S(2)}) copy-start(bf16[256,256]{1,0:T(8,128)(2,1)} %param.5) | copy-start | bytes 393220
  190.2 314.1 %copy-start.2 = (f32[2816]{0:T(1024)S(1)}, f32[2816]{0:T(1024)}, u32[]{:S(2)}) copy-start(f32[2816]{0:T(1024)} %param.7) | copy-start | bytes 33796
Sparse Core Ops, SparseCore 0:
  546.3 231.8 reduce-scatter.1
where the time goes:
time: 785 us
  blocking collectives  520 us (66%)
  waiting for transfers between devices  230 us (29%)
  matrix products  15 us (2%)
  between operations  14.1 us (2%)
    psum x3, blocking collectives, column_scale(): summed = lax.psum(partial_value, 'batch')  410 us
    reduce_scatter x1, waiting for transfers between devices, local(): lax.psum_scatter(jnp.dot(student_n.T, diff, preferred_element_type=jnp.fl...  230 us
    psum x3, blocking collectives, row_total(): return lax.psum(partial_value, 'proto')  110 us
  transfers between devices with their start and end apart: 1, of which 1 were waited for; matrix products, arithmetic and copies ran while one was open for 0% of the time, Pallas kernels for 0%

commit v1 on v0

v1 whole, which is shorter than its diff:
```python
import jax
import jax.numpy as jnp
from jax import lax
from jax.sharding import PartitionSpec as P

ITERS = 3
NX = 4


teacher_temp = 0.04
student_temp = 0.1
eps = 1e-06


def unit_rows(x):
    xf = x.astype(jnp.float32)
    return (xf * lax.rsqrt(jnp.sum(xf * xf, 1, keepdims=True) + eps)).astype(jnp.bfloat16)


def spread_sum(value, axis):
    n = lax.axis_size(axis)
    sent = jnp.broadcast_to(value[None], (n,) + value.shape)
    return jnp.sum(lax.all_to_all(sent, axis, 0, 0, tiled=True), 0)


def local(teacher, student, prototypes, gain):
    rows, depth = teacher.shape
    nb, npr = lax.axis_size("batch"), lax.axis_size("proto")
    ny = nb // NX
    x_groups = [[y * NX + x for x in range(NX)] for y in range(ny)]
    xp_groups = [[b * npr + p for b in group for p in range(npr)] for group in x_groups]
    x_me = lax.axis_index("batch") % NX

    both = jnp.concatenate([teacher, student], 0).astype(jnp.float32)
    both = lax.optimization_barrier(both)
    gathered = lax.all_gather(both, "batch", axis_index_groups=x_groups)

    wf = prototypes.astype(jnp.float32)
    proto_n = (wf * lax.rsqrt(jnp.sum(wf * wf, 0, keepdims=True) + eps) * gain[None, :]).astype(
        jnp.bfloat16
    )
    cols = proto_n.shape[1]
    part = cols // NX
    count = cols * npr
    rows_all = rows * nb
    teacher_n = unit_rows(teacher)
    student_n = unit_rows(student)
    expo = jnp.exp(
        jnp.dot(teacher_n, proto_n, preferred_element_type=jnp.float32) / teacher_temp
    ).astype(jnp.bfloat16)
    expo_wide = lax.optimization_barrier(expo).astype(jnp.float32)
    logits = jnp.dot(student_n, proto_n, preferred_element_type=jnp.float32) / student_temp
    local_total = jnp.sum(jnp.exp(logits), 1)

    teacher_x = unit_rows(gathered[:, :rows].reshape(NX * rows, depth))
    student_x = unit_rows(gathered[:, rows:].reshape(NX * rows, depth))
    proto_x = lax.dynamic_slice_in_dim(proto_n, x_me * part, part, 1)
    expo_x = jnp.exp(
        jnp.dot(teacher_x, proto_x, preferred_element_type=jnp.float32) / teacher_temp
    ).astype(jnp.bfloat16)
    expo_x = lax.optimization_barrier(expo_x)
    logits_x = jnp.dot(student_x, proto_x, preferred_element_type=jnp.float32) / student_temp

    scale_v = jnp.ones((rows,), jnp.float32)
    for step in range(ITERS):
        scale_u = 1.0 / spread_sum(
            jnp.dot(scale_v, expo_wide, precision=lax.Precision.HIGHEST), "batch"
        )
        partial_r = jnp.dot(expo_wide, scale_u, precision=lax.Precision.HIGHEST)
        if step + 1 < ITERS:
            scale_v = 1.0 / spread_sum(partial_r, "proto")
    sent = jnp.stack([partial_r, local_total])
    sent = jnp.broadcast_to(sent[None], (NX * npr, 2, rows))
    came = lax.all_to_all(
        sent, ("batch", "proto"), 0, 0, tiled=True, axis_index_groups=xp_groups
    ).reshape(NX, npr, 2, rows)
    tot = jnp.sum(came, 1)
    scale_v_x = 1.0 / tot[:, 0].reshape(-1)
    total_x = tot[:, 1].reshape(-1)
    scale_v = lax.dynamic_index_in_dim(1.0 / tot[:, 0], x_me, 0, keepdims=False)
    scale_u_x = lax.dynamic_slice_in_dim(scale_u, x_me * part, part, 0)

    assign_x = expo_x.astype(jnp.float32) * scale_u_x[None, :] * scale_v_x[:, None]
    prob_x = jnp.exp(logits_x - jnp.log(total_x)[:, None])
    diff_x = (count * (prob_x - assign_x)).astype(jnp.bfloat16)
    inv_root = 1.0 / jnp.sqrt(jnp.float32(rows_all))
    grad_x = jnp.dot(student_x.T, diff_x, preferred_element_type=jnp.float32) * inv_root
    own = depth // nb
    parts = lax.all_to_all(grad_x.reshape(nb, own, part), "batch", 0, 0, tiled=True)
    grad = jnp.sum(parts.reshape(ny, NX, own, part), 0)
    grad = jnp.swapaxes(grad, 0, 1).reshape(own, cols)

    assign = expo_wide * scale_u[None, :] * scale_v[:, None]
    targets = (count * assign).astype(jnp.bfloat16)
    return (targets, grad)


def solution(mesh):
    return jax.shard_map(
        local,
        mesh=mesh,
        in_specs=(P("batch", None), P("batch", None), P(None, "proto"), P("proto")),
        out_specs=(P("batch", "proto"), P("batch", "proto")),
        check_vma=False,
    )
```

time: 785 us -> 190 us (0.24)
  the two profiles are of different devices: /device:TPU:16 before, /device:TPU:2 now
where the time goes in v1:
time: 190 us; the launch traced here: 189 us
  waiting for transfers between devices  62 us (33%)
  blocking collectives  61.5 us (32%)
  starting transfers between devices  22.9 us (12%)
  between operations  14.4 us (8%)
  matrix products  12.4 us (7%)
  other arithmetic  8.87 us (5%)
  local copies, waits for them, and re-layouts  6.75 us (4%)
    all_to_all x3, blocking collectives, spread_sum(): return jnp.sum(lax.all_to_all(sent, axis, 0, 0, tiled=True), 0)  61.5 us
    all_to_all x2, waiting for transfers between devices, spread_sum(): return jnp.sum(lax.all_to_all(sent, axis, 0, 0, tiled=True), 0)  25.5 us
    all_to_all x1, waiting for transfers between devices, local(): lax.all_to_all(grad_x.reshape(nb, own, part), 'batch', 0, 0, tiled=True)  20.2 us
    all_to_all x1, waiting for transfers between devices, local(): lax.all_to_all(sent, ('batch', 'proto'), 0, 0, tiled=True, axis_index_gro...  16.3 us
    all_to_all x2, starting transfers between devices, spread_sum(): return jnp.sum(lax.all_to_all(sent, axis, 0, 0, tiled=True), 0)  11.1 us
    all_to_all x1, starting transfers between devices, local(): lax.all_to_all(sent, ('batch', 'proto'), 0, 0, tiled=True, axis_index_gro...  6.92 us
    all_to_all x1, starting transfers between devices, local(): lax.all_to_all(grad_x.reshape(nb, own, part), 'batch', 0, 0, tiled=True)  4.86 us
  transfers between devices with their start and end apart: 5, of which 4 were waited for; matrix products, arithmetic and copies ran while one was open for 5% of the time, Pallas kernels for 0%

profile of v1, /device:TPU:2, one launch (start us, length us, event | category | flops | bytes accessed | tf_op | source)
XLA Modules:
  0.0 188.9 jit_solution(7370986973198642879)
XLA Ops:
  7.2 1.1 fusion.12
  8.3 1.7 fusion.3
  12.4 23.4 %all_to_all.40 = f32[32,1,2816]{2,1,0:T(1,128)S(1)} all-to-all(f32[32,1,2816]{2,1,0:T(1,128)S(1)} %broadcast_in_dim.12), channel_id=1, replica_groups=mesh['proto'=24,'batch'=32] {'batch'}, dimensions={0} | all-to-all | bytes 720896 | tf_op jit(solution)/shard_map/all_to_all | solution.py:23
  36.1 1.2 fusion.27
  37.3 25.3 %all_to_all.41 = f32[24,1,256]{2,1,0:T(1,128)S(1)} all-to-all(f32[24,1,256]{2,1,0:T(1,128)S(1)} %broadcast_in_dim.13), channel_id=1, replica_groups=mesh['proto'=24,'batch'=32] {'proto'}, dimensions={0} | all-to-all | bytes 49152 | tf_op jit(solution)/shard_map/all_to_all | solution.py:23
  63.4 0.9 broadcast_in_dim.14
  64.3 5.6 %all-to-all-start.2 = ((f32[32,1,2816]{2,1,0:T(1,128)}), f32[32,1,2816]{2,1,0:T(1,128)S(1)}, u32[]{:S(2)}, u32[]{:S(2)}) async-start(f32[32,1,2816]{2,1,0:T(1,128)} %broadcast_in_dim.14), calls=%async_computation.2 | async-start | bytes 720896 | tf_op jit(solution)/shard_map/all_to_all | solution.py:23
  70.0 0.8 maximum_convert_fusion
  70.8 12.7 %all-to-all-done.2 = f32[32,1,2816]{2,1,0:T(1,128)S(1)} async-done(((f32[32,1,2816]{2,1,0:T(1,128)}), f32[32,1,2816]{2,1,0:T(1,128)S(1)}, u32[]{:S(2)}, u32[]{:S(2)}) %all-to-all-start.2) | async-done | bytes 360480 | tf_op jit(solution)/shard_map/all_to_all | solution.py:23
  83.8 1.2 fusion.28
  85.0 12.9 %all_to_all.42 = f32[24,1,256]{2,1,0:T(1,128)S(1)} all-to-all(f32[24,1,256]{2,1,0:T(1,128)S(1)} %broadcast_in_dim.15), channel_id=1, replica_groups=mesh['proto'=24,'batch'=32] {'proto'}, dimensions={0} | all-to-all | bytes 49152 | tf_op jit(solution)/shard_map/all_to_all | solution.py:23
  98.7 0.9 broadcast_in_dim.16
  99.6 5.6 %all-to-all-start.4 = ((f32[32,1,2816]{2,1,0:T(1,128)}), f32[32,1,2816]{2,1,0:T(1,128)S(1)}, u32[]{:S(2)}, u32[]{:S(2)}) async-start(f32[32,1,2816]{2,1,0:T(1,128)} %broadcast_in_dim.16), calls=%async_computation.4 | async-start | bytes 720896 | tf_op jit(solution)/shard_map/all_to_all | solution.py:23
  106.0 12.8 %all-to-all-done.4 = f32[32,1,2816]{2,1,0:T(1,128)S(1)} async-done(((f32[32,1,2816]{2,1,0:T(1,128)}), f32[32,1,2816]{2,1,0:T(1,128)S(1)}, u32[]{:S(2)}, u32[]{:S(2)}) %all-to-all-start.4) | async-done | bytes 360480 | tf_op jit(solution)/shard_map/all_to_all | solution.py:23
  119.0 1.2 fusion.29
  121.0 6.9 %all-to-all-start.5 = ((f32[96,2,256]{2,1,0:T(2,128)}), f32[96,2,256]{2,1,0:T(2,128)S(1)}, u32[]{:S(2)}, u32[]{:S(2)}) async-start(f32[96,2,256]{2,1,0:T(2,128)} %broadcast_in_dim.17), calls=%async_computation.5 | async-start | bytes 393216 | tf_op jit(solution)/shard_map/all_to_all | solution.py:74
  128.1 16.3 %all-to-all-done.5 = f32[96,2,256]{2,1,0:T(2,128)S(1)} async-done(((f32[96,2,256]{2,1,0:T(2,128)}), f32[96,2,256]{2,1,0:T(2,128)S(1)}, u32[]{:S(2)}, u32[]{:S(2)}) %all-to-all-start.5) | async-done | bytes 196640 | tf_op jit(solution)/shard_map/all_to_all | solution.py:74
  144.5 1.9 %multiply_reduce_fusion = (f32[4,256]{1,0:T(4,128)S(1)}, f32[4,256]{1,0:T(4,128)S(1)}, f32[4,256,256]{2,1,0:T(8,128)S(1)}, f32[4,256,256]{2,1,0:T(8,128)S(1)}) fusion(f32[4,512,256]{2,1,0:T(8,128)} %bitcast.45), kind=kLoop, calls=%fused_computation.22 | loop fusion | flops 1046528 | bytes 4202496 | tf_op jit(solution)/shard_map/reduce_sum | solution.py:17
  146.8 1.9 exponential_convert_fusion
  148.7 3.6 %convolution_multiply_fusion.2 = f32[256,704]{0,1:T(8,128)} fusion(bf16[1024,256]{1,0:T(8,128)(2,1)S(1)} %get-tuple-element.9, bf16[1024,704]{0,1:T(8,128)(2,1)} %exponential_convert_fusion, f32[1024]{0:T(1024)S(1)} %bitcast.50, f32[704]{0:T(1024)S(1)} %dynamic_slice.12, f32[1024]{0:T(1024)S(1)} %bitcast.54, bf16[256,2816]{1,0:T(8,128)(2,1)S(1)} %fusion.5, ...), kind=kOutput, calls=%fused_computation.14 | convolution fusion | flops 744144896 | bytes 3616772 | tf_op jit(solution)/shard_map/dot_general | solution.py:87
  152.3 2.3 %copy.22 = f32[256,704]{1,0:T(8,128)} copy(f32[256,704]{0,1:T(8,128)} %convolution_multiply_fusion.2) | data formatting | bytes 1441792 | tf_op jit(solution)/shard_map/mul | solution.py:87
  154.6 4.9 %all-to-all-start.6 = ((f32[32,8,704]{2,1,0:T(8,128)}), f32[32,8,704]{2,1,0:T(8,128)S(1)}, u32[]{:S(2)}, u32[]{:S(2)}) async-start(f32[32,8,704]{2,1,0:T(8,128)} %bitcast.13), calls=%async_computation.6 | async-start | bytes 1572864 | tf_op jit(solution)/shard_map/all_to_all | solution.py:89
  159.5 1.5 multiply_convert_fusion.1
  161.0 20.2 %all-to-all-done.6 = f32[32,8,704]{2,1,0:T(8,128)S(1)} async-done(((f32[32,8,704]{2,1,0:T(8,128)}), f32[32,8,704]{2,1,0:T(8,128)S(1)}, u32[]{:S(2)}, u32[]{:S(2)}) %all-to-all-start.6) | async-done | bytes 720928 | tf_op jit(solution)/shard_map/all_to_all | solution.py:89
  (51 shorter events, 7.8 us)
Async XLA Ops:
  7.2 2.9 %copy-start = (bf16[256,2816]{1,0:T(8,128)(2,1)S(1)}, bf16[256,2816]{1,0:T(8,128)(2,1)}, u32[]{:S(2)}) copy-start(bf16[256,2816]{1,0:T(8,128)(2,1)} %param.6) | copy-start | bytes 4325380
  7.2 2.8 %copy-start.3 = (f32[2816]{0:T(1024)S(1)}, f32[2816]{0:T(1024)}, u32[]{:S(2)}) copy-start(f32[2816]{0:T(1024)} %param.7) | copy-start | bytes 33796
  10.0 0.9 copy-start.1
  37.2 32.7 %copy-start.2 = (bf16[256,256]{1,0:T(8,128)(2,1)S(1)}, bf16[256,256]{1,0:T(8,128)(2,1)}, u32[]{:S(2)}) copy-start(bf16[256,256]{1,0:T(8,128)(2,1)} %param.5) | copy-start | bytes 393220
  64.3 19.2 %all-to-all-start.2 = ((f32[32,1,2816]{2,1,0:T(1,128)}), f32[32,1,2816]{2,1,0:T(1,128)S(1)}, u32[]{:S(2)}, u32[]{:S(2)}) async-start(f32[32,1,2816]{2,1,0:T(1,128)} %broadcast_in_dim.14), calls=%async_computation.2 | async-start | bytes 720896 | tf_op jit(solution)/shard_map/all_to_all | solution.py:23
  69.9 74.6 %all-gather.3.cloned.1.call-start = ((), (), s32[]{:S(2)}) async-start(), calls=%async_computation.7 | async-start | bytes 2621440 | tf_op jit(solution)/shard_map/all_gather | solution.py:36
  99.6 19.2 %all-to-all-start.4 = ((f32[32,1,2816]{2,1,0:T(1,128)}), f32[32,1,2816]{2,1,0:T(1,128)S(1)}, u32[]{:S(2)}, u32[]{:S(2)}) async-start(f32[32,1,2816]{2,1,0:T(1,128)} %broadcast_in_dim.16), calls=%async_computation.4 | async-start | bytes 720896 | tf_op jit(solution)/shard_map/all_to_all | solution.py:23
  121.0 23.3 %all-to-all-start.5 = ((f32[96,2,256]{2,1,0:T(2,128)}), f32[96,2,256]{2,1,0:T(2,128)S(1)}, u32[]{:S(2)}, u32[]{:S(2)}) async-start(f32[96,2,256]{2,1,0:T(2,128)} %broadcast_in_dim.17), calls=%async_computation.5 | async-start | bytes 393216 | tf_op jit(solution)/shard_map/all_to_all | solution.py:74
  154.6 26.6 %all-to-all-start.6 = ((f32[32,8,704]{2,1,0:T(8,128)}), f32[32,8,704]{2,1,0:T(8,128)S(1)}, u32[]{:S(2)}, u32[]{:S(2)}) async-start(f32[32,8,704]{2,1,0:T(8,128)} %bitcast.13), calls=%async_computation.6 | async-start | bytes 1572864 | tf_op jit(solution)/shard_map/all_to_all | solution.py:89
Sparse Core Ops, SparseCore 0:
  73.7 31.6 all-gather.2

commit v2 on v0

v2 whole, which is shorter than its diff:
```python
import functools

import jax
import jax.numpy as jnp
from jax import lax
from jax.experimental import pallas as pl
from jax.experimental.pallas import tpu as pltpu
from jax.sharding import PartitionSpec as P

ITERS = 3
TEAM = 8


teacher_temp = 0.04
student_temp = 0.1
eps = 1e-06


def unit_rows(x):
    xf = x.astype(jnp.float32)
    return (xf * lax.rsqrt(jnp.sum(xf * xf, 1, keepdims=True) + eps)).astype(jnp.bfloat16)


def spread(value, axis, size, groups=None):
    sent = jnp.broadcast_to(value[None], (size,) + value.shape)
    return lax.all_to_all(sent, axis, 0, 0, tiled=True, axis_index_groups=groups)


def grad_kernel(count, scale, expo_ref, student_exp_ref, student_ref, u_ref, rows_ref, out_ref, acc):
    step = pl.program_id(0)

    @pl.when(step == 0)
    def _():
        acc[...] = jnp.zeros_like(acc)

    rows = rows_ref.shape[2]
    u = u_ref[...]
    for s in range(rows_ref.shape[0]):
        span = slice(s * rows, (s + 1) * rows)
        v = rows_ref[s, 0:1, :]
        inv_total = rows_ref[s, 1:2, :]
        assign = expo_ref[:, span].astype(jnp.float32) * u * v
        diff = (count * (student_exp_ref[:, span] * inv_total - assign)).astype(jnp.bfloat16)
        acc[...] += jnp.dot(diff, student_ref[span, :], preferred_element_type=jnp.float32)

    @pl.when(step == pl.num_programs(0) - 1)
    def _():
        out_ref[...] = (acc[...].T * scale).reshape(out_ref.shape)


def partial_grad(expo_t, student_exp_t, student, u, by_sender, count, scale, owners):
    part, crops = expo_t.shape
    depth = student.shape[1]
    senders, _, rows = by_sender.shape
    steps = 4
    chunk = crops // steps
    return pl.pallas_call(
        functools.partial(grad_kernel, count, scale),
        grid=(steps,),
        in_specs=[
            pl.BlockSpec((part, chunk), lambda i: (0, i)),
            pl.BlockSpec((part, chunk), lambda i: (0, i)),
            pl.BlockSpec((chunk, depth), lambda i: (i, 0)),
            pl.BlockSpec((part, 1), lambda i: (0, 0)),
            pl.BlockSpec((senders // steps, 2, rows), lambda i: (i, 0, 0)),
        ],
        out_specs=pl.BlockSpec((owners, depth // owners, part), lambda i: (0, 0, 0)),
        out_shape=jax.ShapeDtypeStruct((owners, depth // owners, part), jnp.float32),
        scratch_shapes=[pltpu.VMEM((part, depth), jnp.float32)],
        compiler_params=pltpu.CompilerParams(vmem_limit_bytes=24 * 1024 * 1024),
        cost_estimate=pl.CostEstimate(
            flops=2 * part * crops * depth, bytes_accessed=6 * part * crops, transcendentals=0
        ),
    )(expo_t, student_exp_t, student, u, by_sender)


def local(teacher, student, prototypes, gain):
    rows, depth = teacher.shape
    nb, npr = lax.axis_size("batch"), lax.axis_size("proto")
    teams = [[t * TEAM + i for i in range(TEAM)] for t in range(nb // TEAM)]
    me = lax.axis_index("batch") % TEAM

    both = jnp.concatenate([teacher, student], 0).astype(jnp.float32)
    both = lax.optimization_barrier(both)
    gathered = lax.all_gather(both, "batch", axis_index_groups=teams)

    wf = prototypes.astype(jnp.float32)
    proto_n = (wf * lax.rsqrt(jnp.sum(wf * wf, 0, keepdims=True) + eps) * gain[None, :]).astype(
        jnp.bfloat16
    )
    cols = proto_n.shape[1]
    part = cols // TEAM
    count = cols * npr
    rows_all = rows * nb
    teacher_n = unit_rows(teacher)
    expo = jnp.exp(
        jnp.dot(teacher_n, proto_n, preferred_element_type=jnp.float32) / teacher_temp
    ).astype(jnp.bfloat16)
    expo_wide = lax.optimization_barrier(expo).astype(jnp.float32)

    scale_v = jnp.ones((rows,), jnp.float32)
    for step in range(ITERS):
        last = step + 1 == ITERS
        if last:
            scale_v, gathered, student, proto_n = lax.optimization_barrier(
                (scale_v, gathered, student, proto_n)
            )
        c = jnp.dot(scale_v, expo_wide, precision=lax.Precision.HIGHEST)
        scale_u = 1.0 / jnp.sum(spread(c, "batch", nb), 0)
        partial_r = jnp.dot(expo_wide, scale_u, precision=lax.Precision.HIGHEST)
        if not last:
            scale_v = 1.0 / jnp.sum(spread(partial_r, "proto", npr), 0)

    logits = jnp.dot(unit_rows(student), proto_n, preferred_element_type=jnp.float32)
    local_total = jnp.sum(jnp.exp(logits / student_temp), 1)
    teacher_t = unit_rows(gathered[:, :rows].reshape(TEAM * rows, depth))
    student_t = unit_rows(gathered[:, rows:].reshape(TEAM * rows, depth))
    proto_t = lax.dynamic_slice_in_dim(proto_n, me * part, part, 1)
    across = (((0,), (1,)), ((), ()))
    expo_t = jnp.exp(
        lax.dot_general(proto_t, teacher_t, across, preferred_element_type=jnp.float32)
        / teacher_temp
    ).astype(jnp.bfloat16)
    student_exp_t = jnp.exp(
        lax.dot_general(proto_t, student_t, across, preferred_element_type=jnp.float32)
        / student_temp
    )
    u_t = lax.dynamic_slice_in_dim(scale_u, me * part, part, 0)[:, None]
    sent = jnp.stack([partial_r, local_total])
    sent, expo_t, student_exp_t, student_t, u_t = lax.optimization_barrier(
        (sent, expo_t, student_exp_t, student_t, u_t)
    )
    inverse = 1.0 / jnp.sum(spread(sent, "proto", npr), 0)
    scale_v = inverse[0]
    by_sender = spread(inverse, "batch", TEAM, teams)

    inv_root = 1.0 / rows_all**0.5
    grad_t = partial_grad(
        expo_t, student_exp_t, student_t, u_t, by_sender, float(count), inv_root, nb
    )
    parts = lax.all_to_all(grad_t, "batch", 0, 0, tiled=True)
    own = depth // nb
    grad = jnp.sum(parts.reshape(nb // TEAM, TEAM, own, part), 0)
    grad = jnp.swapaxes(grad, 0, 1).reshape(own, cols)

    assign = expo_wide * scale_u[None, :] * scale_v[:, None]
    targets = (count * assign).astype(jnp.bfloat16)
    return (targets, grad)


def solution(mesh):
    return jax.shard_map(
        local,
        mesh=mesh,
        in_specs=(P("batch", None), P("batch", None), P(None, "proto"), P("proto")),
        out_specs=(P("batch", "proto"), P("batch", "proto")),
        check_vma=False,
    )
```

time: 785 us -> 190 us (0.24)
  the two profiles are of different devices: /device:TPU:16 before, /device:TPU:8 now
where the time goes in v2:
time: 190 us; the launch traced here: 189 us
  blocking collectives  85.3 us (45%)
  waiting for transfers between devices  33.9 us (18%)
  starting transfers between devices  18.8 us (10%)
  other arithmetic  16.2 us (9%)
  between operations  14.4 us (8%)
  matrix products  10.9 us (6%)
  local copies, waits for them, and re-layouts  6.59 us (3%)
  Pallas kernels  2.68 us (1%)
    all_to_all x4, blocking collectives, spread(): lax.all_to_all(sent, axis, 0, 0, tiled=True, axis_index_groups=groups)  85.3 us
    all_to_all x3, waiting for transfers between devices, spread(): lax.all_to_all(sent, axis, 0, 0, tiled=True, axis_index_groups=groups)  22.7 us
    all_to_all x3, starting transfers between devices, spread(): lax.all_to_all(sent, axis, 0, 0, tiled=True, axis_index_groups=groups)  13.7 us
    all_to_all x1, waiting for transfers between devices, local(): parts = lax.all_to_all(grad_t, 'batch', 0, 0, tiled=True)  11.2 us
    reduce_sum x3, other arithmetic, unit_rows(): jnp.sum(xf * xf, 1, keepdims=True) + eps  6.11 us
    all_to_all x1, starting transfers between devices, local(): parts = lax.all_to_all(grad_t, 'batch', 0, 0, tiled=True)  5.07 us
    dot_general x3, matrix products, local(): partial_r = jnp.dot(expo_wide, scale_u, precision=lax.Precision.HIGHEST)  4.93 us
  transfers between devices with their start and end apart: 5, of which 4 were waited for; matrix products, arithmetic and copies ran while one was open for 9% of the time, Pallas kernels for 0%

profile of v2, /device:TPU:8, one launch (start us, length us, event | category | flops | bytes accessed | tf_op | source)
XLA Modules:
  0.0 188.8 jit_solution(3674634926749062502)
XLA Ops:
  7.2 1.9 %maximum_convert_fusion = f32[512,256]{1,0:T(8,128)} fusion(bf16[256,256]{1,0:T(8,128)(2,1)} %param.5, bf16[256,256]{1,0:T(8,128)(2,1)} %param.4), kind=kLoop, calls=%fused_computation.34 | loop fusion | flops 524288 | bytes 786432 | tf_op jit(solution)/shard_map/convert_element_type | solution.py:83
  12.6 24.1 %all_to_all.45 = f32[32,1,2816]{2,1,0:T(1,128)S(1)} all-to-all(f32[32,1,2816]{2,1,0:T(1,128)S(1)} %broadcast_in_dim.16), channel_id=1, replica_groups=mesh['proto'=24,'batch'=32] {'batch'}, dimensions={0} | all-to-all | bytes 720896 | tf_op jit(solution)/shard_map/all_to_all | solution.py:26
  37.0 1.2 fusion.26
  38.2 26.2 %all_to_all.46 = f32[24,1,256]{2,1,0:T(1,128)S(1)} all-to-all(f32[24,1,256]{2,1,0:T(1,128)S(1)} %broadcast_in_dim.17), channel_id=1, replica_groups=mesh['proto'=24,'batch'=32] {'proto'}, dimensions={0} | all-to-all | bytes 49152 | tf_op jit(solution)/shard_map/all_to_all | solution.py:26
  65.4 21.8 %all_to_all.47 = f32[32,1,2816]{2,1,0:T(1,128)S(1)} all-to-all(f32[32,1,2816]{2,1,0:T(1,128)S(1)} %broadcast_in_dim.18), channel_id=1, replica_groups=mesh['proto'=24,'batch'=32] {'batch'}, dimensions={0} | all-to-all | bytes 720896 | tf_op jit(solution)/shard_map/all_to_all | solution.py:26
  87.4 1.2 fusion.27
  89.3 3.8 %all-to-all-start.3 = ((f32[24,1,256]{2,1,0:T(1,128)}), f32[24,1,256]{2,1,0:T(1,128)S(1)}, u32[]{:S(2)}, u32[]{:S(2)}) async-start(f32[24,1,256]{2,1,0:T(1,128)} %broadcast_in_dim.19), calls=%async_computation.3 | async-start | bytes 49152 | tf_op jit(solution)/shard_map/all_to_all | solution.py:26
  93.1 9.9 %all-to-all-done.3 = f32[24,1,256]{2,1,0:T(1,128)S(1)} async-done(((f32[24,1,256]{2,1,0:T(1,128)}), f32[24,1,256]{2,1,0:T(1,128)S(1)}, u32[]{:S(2)}, u32[]{:S(2)}) %all-to-all-start.3) | async-done | bytes 24608 | tf_op jit(solution)/shard_map/all_to_all | solution.py:26
  103.6 4.1 %multiply_reduce_fusion = (f32[8,256]{1,0:T(8,128)S(1)}, f32[8,256]{1,0:T(8,128)S(1)}, f32[8,256,256]{2,1,0:T(8,128)S(1)}, f32[8,256,256]{2,1,0:T(8,128)}) fusion(f32[8,512,256]{2,1,0:T(8,128)} %bitcast.39), kind=kLoop, calls=%fused_computation.20 | loop fusion | flops 2093056 | bytes 8404992 | tf_op jit(solution)/shard_map/reduce_sum | solution.py:21
  109.4 5.5 %all-to-all-start.4 = ((f32[32,1,2816]{2,1,0:T(1,128)}), f32[32,1,2816]{2,1,0:T(1,128)}, u32[]{:S(2)}, u32[]{:S(2)}) async-start(f32[32,1,2816]{2,1,0:T(1,128)} %broadcast_in_dim.20), calls=%async_computation.4 | async-start | bytes 720896 | tf_op jit(solution)/shard_map/all_to_all | solution.py:26
  116.0 2.1 %fusion.9 = (bf16[2048,256]{1,0:T(8,128)(2,1)S(1)}, bf16[2048,256]{1,0:T(8,128)(2,1)S(1)}) fusion(f32[8,256,256]{2,1,0:T(8,128)S(1)} %get-tuple-element.22, f32[2048]{0:T(1024)S(1)} %bitcast.43, f32[2048]{0:T(1024)S(1)} %bitcast.42, f32[8,256,256]{2,1,0:T(8,128)} %get-tuple-element.23), kind=kLoop, calls=%fused_computation.17 | loop fusion | flops 2097152 | bytes 6307840 | tf_op jit(solution)/shard_map/convert_element_type | solution.py:21
  118.8 1.9 fusion.8.expo_ref
  121.5 8.2 %all-to-all-done.4 = f32[32,1,2816]{2,1,0:T(1,128)} async-done(((f32[32,1,2816]{2,1,0:T(1,128)}), f32[32,1,2816]{2,1,0:T(1,128)}, u32[]{:S(2)}, u32[]{:S(2)}) %all-to-all-start.4) | async-done | bytes 360480 | tf_op jit(solution)/shard_map/all_to_all | solution.py:26
  129.6 1.2 reduce_sum.123
  131.0 2.6 %fusion.28 = f32[1,256]{1,0:T(1,128)S(1)} fusion(bf16[256,2816]{1,0:T(8,128)(2,1)} %copy-done.3, f32[2816,1]{0,1:T(1,128)S(1)} %reshape.114), kind=kOutput, calls=%fused_computation.57 | convolution fusion | flops 8650752 | bytes 1454080 | tf_op jit(solution)/shard_map/dot_general | solution.py:110
  133.6 13.3 %all_to_all.48 = f32[24,2,256]{2,1,0:T(2,128)S(1)} all-to-all(f32[24,2,256]{2,1,0:T(2,128)S(1)} %broadcast_in_dim.22), channel_id=1, replica_groups=mesh['proto'=24,'batch'=32] {'proto'}, dimensions={0} | all-to-all | bytes 98304 | tf_op jit(solution)/shard_map/all_to_all | solution.py:26
  147.6 4.3 %all-to-all-start.6 = ((f32[8,2,256]{2,1,0:T(2,128)}), f32[8,2,256]{2,1,0:T(2,128)S(1)}, u32[]{:S(2)}, u32[]{:S(2)}) async-start(f32[8,2,256]{2,1,0:T(2,128)} %broadcast_in_dim.23), calls=%async_computation.6 | async-start | bytes 32768 | tf_op jit(solution)/shard_map/all_to_all | solution.py:26
  152.0 4.6 %all-to-all-done.6.rows_ref = f32[8,2,256]{2,1,0:T(2,128)S(1)} async-done(((f32[8,2,256]{2,1,0:T(2,128)}), f32[8,2,256]{2,1,0:T(2,128)S(1)}, u32[]{:S(2)}, u32[]{:S(2)}) %all-to-all-start.6) | async-done | bytes 16416 | tf_op jit(solution)/shard_map/all_to_all | solution.py:26
  156.7 1.2 copy-done.1
  157.9 1.4 copy-done.2
  159.3 2.7 %shard_map.59 = f32[32,8,352]{2,1,0:T(8,128)} custom-call(bf16[352,2048]{1,0:T(8,128)(2,1)S(1)} %copy-done.2, f32[352,2048]{1,0:T(8,128)S(1)} %fusion.4.student_exp_ref, bf16[2048,256]{1,0:T(8,128)(2,1)S(1)} %copy-done.1, f32[352,1]{1,0:T(8,128)S(1)} %copy.18.u_ref, f32[8,2,256]{2,1,0:T(2,128)S(1)} %all-to-all-done.6.rows_ref), custom_call_target="tpu_custom_call" | custom-call | flops 369098752 | bytes 4325376 | tf_op jit(solution)/shard_map/pallas_call | solution.py:57
  161.9 5.1 %all-to-all-start.7 = ((f32[32,8,352]{2,1,0:T(8,128)}), f32[32,8,352]{2,1,0:T(8,128)S(1)}, u32[]{:S(2)}, u32[]{:S(2)}) async-start(f32[32,8,352]{2,1,0:T(8,128)} %shard_map.59), calls=%async_computation.7 | async-start | bytes 786432 | tf_op jit(solution)/shard_map/all_to_all | solution.py:141
  167.0 2.9 %multiply_convert_fusion = bf16[256,2816]{1,0:T(8,128)(2,1)} fusion(bf16[256,2816]{1,0:T(8,128)(2,1)} %copy-done.3, f32[256]{0:T(256)S(1)} %bitcast.45, f32[2816]{0:T(1024)S(1)} %broadcast_divide_fusion), kind=kLoop, calls=%fused_computation.14 | loop fusion | flops 3604480 | bytes 2895872 | tf_op jit(solution)/shard_map/convert_element_type | solution.py:147
  169.9 11.2 %all-to-all-done.7 = f32[32,8,352]{2,1,0:T(8,128)S(1)} async-done(((f32[32,8,352]{2,1,0:T(8,128)}), f32[32,8,352]{2,1,0:T(8,128)S(1)}, u32[]{:S(2)}, u32[]{:S(2)}) %all-to-all-start.7) | async-done | bytes 360480 | tf_op jit(solution)/shard_map/all_to_all | solution.py:141
  (69 shorter events, 12.1 us)
Async XLA Ops:
  7.2 3.0 %copy-start.4 = (bf16[256,2816]{1,0:T(8,128)(2,1)S(1)}, bf16[256,2816]{1,0:T(8,128)(2,1)}, u32[]{:S(2)}) copy-start(bf16[256,2816]{1,0:T(8,128)(2,1)} %param.6) | copy-start | bytes 4325380
  7.2 3.4 %copy-start.9 = (f32[2816]{0:T(1024)S(1)}, f32[2816]{0:T(1024)}, u32[]{:S(2)}) copy-start(f32[2816]{0:T(1024)} %param.7) | copy-start | bytes 33796
  7.2 96.4 %all-gather.3.cloned.1.call-start = ((), (), s32[]{:S(2)}) async-start(), calls=%async_computation.8 | async-start | bytes 4718592 | tf_op jit(solution)/shard_map/all_gather | solution.py:85
  10.2 0.9 copy-start.7
  11.1 1.3 copy-start.5
  11.7 96.0 %copy-start.3 = (bf16[256,2816]{1,0:T(8,128)(2,1)}, bf16[256,2816]{1,0:T(8,128)(2,1)S(1)}, u32[]{:S(2)}) copy-start(bf16[256,2816]{1,0:T(8,128)(2,1)S(1)} %fusion.2) | copy-start | bytes 4325380
  89.3 13.7 %all-to-all-start.3 = ((f32[24,1,256]{2,1,0:T(1,128)}), f32[24,1,256]{2,1,0:T(1,128)S(1)}, u32[]{:S(2)}, u32[]{:S(2)}) async-start(f32[24,1,256]{2,1,0:T(1,128)} %broadcast_in_dim.19), calls=%async_computation.3 | async-start | bytes 49152 | tf_op jit(solution)/shard_map/all_to_all | solution.py:26
  103.6 4.1 %copy-start.10 = (f32[256]{0:T(256)S(1)}, f32[256]{0:T(256)}, u32[]{:S(2)}) copy-start(f32[256]{0:T(256)} %broadcast_divide_fusion.5) | copy-start | bytes 3076
  109.4 20.2 %all-to-all-start.4 = ((f32[32,1,2816]{2,1,0:T(1,128)}), f32[32,1,2816]{2,1,0:T(1,128)}, u32[]{:S(2)}, u32[]{:S(2)}) async-start(f32[32,1,2816]{2,1,0:T(1,128)} %broadcast_in_dim.20), calls=%async_computation.4 | async-start | bytes 720896 | tf_op jit(solution)/shard_map/all_to_all | solution.py:26
  116.0 2.1 %copy-start.6 = (bf16[256,2816]{1,0:T(8,128)(2,1)S(1)}, bf16[256,2816]{1,0:T(8,128)(2,1)}, u32[]{:S(2)}) copy-start(bf16[256,2816]{1,0:T(8,128)(2,1)} %copy-done.5) | copy-start | bytes 4325380
  116.0 2.1 %copy-start.8 = (bf16[256,256]{1,0:T(8,128)(2,1)S(1)}, bf16[256,256]{1,0:T(8,128)(2,1)}, u32[]{:S(2)}) copy-start(bf16[256,256]{1,0:T(8,128)(2,1)} %param.5) | copy-start | bytes 393220
  118.1 2.6 %copy-start = (bf16[2048,256]{1,0:T(8,128)(2,1)}, bf16[2048,256]{1,0:T(8,128)(2,1)S(1)}, u32[]{:S(2)}) copy-start(bf16[2048,256]{1,0:T(8,128)(2,1)S(1)} %get-tuple-element.18.student_ref) | copy-start | bytes 3145732
  147.6 9.1 %all-to-all-start.6 = ((f32[8,2,256]{2,1,0:T(2,128)}), f32[8,2,256]{2,1,0:T(2,128)S(1)}, u32[]{:S(2)}, u32[]{:S(2)}) async-start(f32[8,2,256]{2,1,0:T(2,128)} %broadcast_in_dim.23), calls=%async_computation.6 | async-start | bytes 32768 | tf_op jit(solution)/shard_map/all_to_all | solution.py:26
  156.7 1.2 copy-start.1
  157.9 1.4 copy-start.2
  161.9 19.2 %all-to-all-start.7 = ((f32[32,8,352]{2,1,0:T(8,128)}), f32[32,8,352]{2,1,0:T(8,128)S(1)}, u32[]{:S(2)}, u32[]{:S(2)}) async-start(f32[32,8,352]{2,1,0:T(8,128)} %shard_map.59), calls=%async_computation.7 | async-start | bytes 786432 | tf_op jit(solution)/shard_map/all_to_all | solution.py:141
Sparse Core Ops, SparseCore 0:
  10.4 71.7 all-gather.2

commit v3 on v2

v3 whole, which is shorter than its diff:
```python
import functools

import jax
import jax.numpy as jnp
from jax import lax
from jax.experimental import pallas as pl
from jax.experimental.pallas import tpu as pltpu
from jax.sharding import PartitionSpec as P

ITERS = 3
SMALL, PASSING, VMEM = 16 * 2**20, 121 * 2**19, 61 * 2**20
LANES = 128
HELD = 3
TEAM = 8


teacher_temp = 0.04
student_temp = 0.1
eps = 1e-06


def unit_rows(x):
    xf = x.astype(jnp.float32)
    return (xf * lax.rsqrt(jnp.sum(xf * xf, 1, keepdims=True) + eps)).astype(jnp.bfloat16)


def spread(value, axis, size, groups=None):
    sent = jnp.broadcast_to(value[None], (size,) + value.shape)
    return lax.all_to_all(sent, axis, 0, 0, tiled=True, axis_index_groups=groups)


def first_group(groups):
    return jnp.minimum(lax.axis_index("batch") % TEAM * HELD, groups - HELD)


def grad_kernel(count, scale, expo_ref, student_exp_ref, student_ref, u_ref, rows_ref, out_ref, acc, u_wide):
    step = pl.program_id(0)

    @pl.when(step == 0)
    def _():
        acc[...] = jnp.zeros_like(acc)
        u = u_ref[pl.ds(first_group(u_ref.shape[0]), HELD), :]
        for g in range(HELD):
            wide = jnp.broadcast_to(u[g : g + 1, :], (LANES, LANES)).T
            u_wide[g * LANES : (g + 1) * LANES, :] = wide

    rows = rows_ref.shape[2]
    u = u_wide[...]
    for s in range(rows_ref.shape[0]):
        for start in range(0, rows, LANES):
            v = rows_ref[s, 0:1, start : start + LANES]
            inv_total = rows_ref[s, 1:2, start : start + LANES]
            span = slice(s * rows + start, s * rows + start + LANES)
            assign = expo_ref[:, span].astype(jnp.float32) * u * v
            diff = count * (student_exp_ref[:, span] * inv_total - assign)
            acc[...] += jnp.dot(
                diff.astype(jnp.bfloat16), student_ref[span, :], preferred_element_type=jnp.float32
            )

    @pl.when(step == pl.num_programs(0) - 1)
    def _():
        out_ref[...] = (acc[...].T * scale).reshape(out_ref.shape)


def partial_grad(expo_t, student_exp_t, student, u, by_sender, count, scale, owners):
    part, crops = expo_t.shape
    depth = student.shape[1]
    senders, _, rows = by_sender.shape
    steps = 4
    chunk = crops // steps
    return pl.pallas_call(
        functools.partial(grad_kernel, count, scale),
        grid=(steps,),
        in_specs=[
            pl.BlockSpec((part, chunk), lambda i: (0, i)),
            pl.BlockSpec((part, chunk), lambda i: (0, i)),
            pl.BlockSpec((chunk, depth), lambda i: (i, 0)),
            pl.BlockSpec(u.shape, lambda i: (0, 0)),
            pl.BlockSpec((senders // steps, 2, rows), lambda i: (i, 0, 0)),
        ],
        out_specs=pl.BlockSpec((owners, depth // owners, part), lambda i: (0, 0, 0)),
        out_shape=jax.ShapeDtypeStruct((owners, depth // owners, part), jnp.float32),
        scratch_shapes=[
            pltpu.VMEM((part, depth), jnp.float32),
            pltpu.VMEM((part, LANES), jnp.float32),
        ],
        compiler_params=pltpu.CompilerParams(vmem_limit_bytes=VMEM),
        cost_estimate=pl.CostEstimate(
            flops=2 * part * crops * depth, bytes_accessed=6 * part * crops, transcendentals=0
        ),
    )(expo_t, student_exp_t, student, u, by_sender)


def join_kernel(parts_ref, out_ref):
    teams = parts_ref.shape[0] // TEAM
    groups = out_ref.shape[1] // LANES
    for i in range(TEAM):
        start = min(i * HELD, groups - HELD) * LANES
        total = parts_ref[i]
        for t in range(1, teams):
            total += parts_ref[t * TEAM + i]
        out_ref[:, start : start + HELD * LANES] = total


def row_kernel(came_ref, expo_ref, *refs):
    total_ref, (sent_ref, u_ref) = (refs[0] if len(refs) == 3 else None), refs[-2:]
    u_ref[...] = 1.0 / jnp.sum(came_ref[...], 0)
    rows = expo_ref.shape[0]
    block = 64
    sums = []
    for start in range(0, rows, block):
        acc = jnp.zeros((block, LANES), jnp.float32)
        for j in range(u_ref.shape[0]):
            e = expo_ref[start : start + block, j * LANES : (j + 1) * LANES].astype(jnp.float32)
            acc += e * u_ref[j : j + 1, :]
        sums.append(acc)
    r = jnp.sum(jnp.concatenate(sums, 0).T, 0, keepdims=True)
    peers = sent_ref.shape[0]
    sent_ref[:, 0:1, :] = jnp.broadcast_to(r[None], (peers, 1, rows))
    if total_ref is not None:
        sent_ref[:, 1:2, :] = jnp.broadcast_to(total_ref[...][None], (peers, 1, rows))


def row_terms(came, expo, peers, total=None):
    more = () if total is None else (total,)
    _, groups, _ = came.shape
    rows = expo.shape[0]
    return pl.pallas_call(
        row_kernel,
        out_shape=(
            jax.ShapeDtypeStruct((peers, 1 + len(more), rows), jnp.float32),
            jax.ShapeDtypeStruct((groups, LANES), jnp.float32),
        ),
        compiler_params=pltpu.CompilerParams(vmem_limit_bytes=SMALL),
        cost_estimate=pl.CostEstimate(flops=2 * expo.size, bytes_accessed=2 * expo.size, transcendentals=0),
    )(came, expo, *more)


def column_kernel(came_ref, expo_ref, *refs):
    sent_ref = refs[len(refs) // 2]
    rows = expo_ref.shape[0]
    v = 1.0 / jnp.sum(came_ref[...], 0)
    v = jnp.broadcast_to(v, (LANES, rows)).T
    peers, groups, _ = sent_ref.shape
    for j in range(groups):
        e = expo_ref[:, j * LANES : (j + 1) * LANES].astype(jnp.float32)
        sent_ref[0, j : j + 1, :] = jnp.sum(e * v, 0, keepdims=True)
    sent_ref[1:] = jnp.broadcast_to(sent_ref[0:1], (peers - 1, groups, LANES))


def column_terms(came, expo, peers, passed=None):
    groups = expo.shape[1] // LANES
    more = () if passed is None else (passed,)
    out = pl.pallas_call(
        column_kernel,
        in_specs=[pl.BlockSpec(), pl.BlockSpec()] + [pl.BlockSpec(memory_space=pl.ANY)] * len(more),
        out_specs=[pl.BlockSpec()] + [pl.BlockSpec(memory_space=pl.ANY)] * len(more),
        out_shape=[jax.ShapeDtypeStruct((peers, groups, LANES), jnp.float32)]
        + [jax.ShapeDtypeStruct(m.shape, m.dtype) for m in more],
        input_output_aliases={2: 1} if more else {},
        compiler_params=pltpu.CompilerParams(vmem_limit_bytes=PASSING if more else SMALL),
        cost_estimate=pl.CostEstimate(flops=2 * expo.size, bytes_accessed=2 * expo.size, transcendentals=0),
    )(came, expo, *more)
    return out if more else out[0]


def team_kernel(rows_ref, proto_ref, after_ref, expo_ref, student_exp_ref, student_ref, proto_t):
    @pl.when(pl.program_id(0) == 0)
    def _():
        start = pl.multiple_of(first_group(proto_ref.shape[1] // LANES) * LANES, LANES)
        proto_t[...] = proto_ref[:, pl.ds(start, HELD * LANES)].astype(jnp.float32).T.astype(jnp.bfloat16)

    def unit(x):
        return (x * lax.rsqrt(jnp.sum(x * x, 1, keepdims=True) + eps)).astype(jnp.bfloat16)

    across = (((1,), (1,)), ((), ()))
    proto = proto_t[...]
    t = unit(rows_ref[0, 0])
    s = unit(rows_ref[1, 0])
    student_ref[...] = s
    lt = lax.dot_general(proto, t, across, preferred_element_type=jnp.float32)
    expo_ref[...] = jnp.exp(lt / teacher_temp).astype(jnp.bfloat16)
    ls = lax.dot_general(proto, s, across, preferred_element_type=jnp.float32)
    student_exp_ref[...] = jnp.exp(ls / student_temp)


def team_products(gathered, proto, after):
    _, senders, rows, depth = gathered.shape
    part = HELD * LANES
    return pl.pallas_call(
        team_kernel,
        grid=(senders,),
        in_specs=[
            pl.BlockSpec((2, 1, rows, depth), lambda i: (0, i, 0, 0)),
            pl.BlockSpec(proto.shape, lambda i: (0, 0)),
            pl.BlockSpec(memory_space=pl.ANY),
        ],
        out_specs=[
            pl.BlockSpec((part, rows), lambda i: (0, i)),
            pl.BlockSpec((part, rows), lambda i: (0, i)),
            pl.BlockSpec((rows, depth), lambda i: (i, 0)),
        ],
        out_shape=(
            jax.ShapeDtypeStruct((part, senders * rows), jnp.bfloat16),
            jax.ShapeDtypeStruct((part, senders * rows), jnp.float32),
            jax.ShapeDtypeStruct((senders * rows, depth), jnp.bfloat16),
        ),
        scratch_shapes=[pltpu.VMEM((part, depth), jnp.bfloat16)],
        compiler_params=pltpu.CompilerParams(vmem_limit_bytes=VMEM),
        cost_estimate=pl.CostEstimate(
            flops=4 * part * senders * rows * depth,
            bytes_accessed=10 * 2**20,
            transcendentals=2 * part * senders * rows,
        ),
    )(gathered, proto, after)


def local(teacher, student, prototypes, gain):
    rows, depth = teacher.shape
    nb, npr = lax.axis_size("batch"), lax.axis_size("proto")
    teams = [[t * TEAM + i for i in range(TEAM)] for t in range(nb // TEAM)]
    chips = [[2 * z, 2 * z + 1] for z in range(npr // 2)]
    core = lax.axis_index("proto") % 2

    mine = jnp.where(core == 0, teacher.astype(jnp.float32), student.astype(jnp.float32))
    mine = lax.optimization_barrier(mine)
    gathered = lax.all_gather(mine, "batch", axis_index_groups=teams)

    wf = prototypes.astype(jnp.float32)
    proto_n = (wf * lax.rsqrt(jnp.sum(wf * wf, 0, keepdims=True) + eps) * gain[None, :]).astype(
        jnp.bfloat16
    )
    cols = proto_n.shape[1]
    groups = cols // LANES
    count = cols * npr
    rows_all = rows * nb
    expo = jnp.exp(
        jnp.dot(unit_rows(teacher), proto_n, preferred_element_type=jnp.float32) / teacher_temp
    ).astype(jnp.bfloat16)
    expo = lax.optimization_barrier(expo)

    sent = jnp.sum(expo.astype(jnp.float32), 0).reshape(groups, LANES)
    sent = jnp.broadcast_to(sent[None], (nb, groups, LANES))
    for step in range(ITERS):
        last = step + 1 == ITERS
        if step == 1:
            sent, gathered = column_terms(came, expo, nb, gathered)
            gathered = lax.all_gather(gathered, "proto", axis_index_groups=chips)
        elif step:
            sent = column_terms(came, expo, nb)
        came = lax.all_to_all(sent, "batch", 0, 0, tiled=True)
        if not last:
            sent, _ = row_terms(came, expo, npr)
            came = lax.all_to_all(sent, "proto", 0, 0, tiled=True)

    logits = jnp.dot(unit_rows(student), proto_n, preferred_element_type=jnp.float32)
    local_total = jnp.sum(jnp.exp(logits / student_temp), 1)
    team_values = team_products(gathered, proto_n, sent)
    came, team_values, local_total = lax.optimization_barrier((came, team_values, local_total))
    expo_t, student_exp_t, student_t = team_values

    sent, scale_u = row_terms(came, expo, npr, local_total[None])
    came = lax.all_to_all(sent, "proto", 0, 0, tiled=True)
    inverse = 1.0 / jnp.sum(came, 0)
    scale_v = inverse[0]
    by_sender = spread(inverse, "batch", TEAM, teams)

    inv_root = 1.0 / rows_all**0.5
    grad_t = partial_grad(
        expo_t, student_exp_t, student_t, scale_u, by_sender, float(count), inv_root, nb
    )
    parts = lax.all_to_all(grad_t, "batch", 0, 0, tiled=True)
    grad = pl.pallas_call(
        join_kernel,
        out_shape=jax.ShapeDtypeStruct((depth // nb, cols), jnp.float32),
        compiler_params=pltpu.CompilerParams(vmem_limit_bytes=SMALL),
    )(parts)

    scale_u = scale_u.reshape(cols)
    assign = expo.astype(jnp.float32) * scale_u[None, :] * scale_v[:, None]
    targets = (count * assign).astype(jnp.bfloat16)
    return (targets, grad)


def solution(mesh):
    return jax.shard_map(
        local,
        mesh=mesh,
        in_specs=(P("batch", None), P("batch", None), P(None, "proto"), P("proto")),
        out_specs=(P("batch", "proto"), P("batch", "proto")),
        check_vma=False,
    )
```

time: 190 us -> 189 us (level)
  blocking collectives: 85.3 us -> 116 us
  Pallas kernels: 2.68 us -> 20.7 us
  waiting for transfers between devices: 33.9 us -> 17 us
  other arithmetic: 16.2 us -> 6.36 us
  starting transfers between devices: 18.8 us -> 10.3 us
  matrix products: 10.9 us -> 2.64 us
  local copies, waits for them, and re-layouts: 6.59 us -> 0.67 us
    all_to_all x0 -> x5, blocking collectives: none -> 107 us  [the longest x3 61.5 us: local(): came = lax.all_to_all(sent, 'proto', 0, 0, tiled=True)]
    all_to_all x4 -> x1, blocking collectives: 85.3 us -> 8.85 us  [spread(): lax.all_to_all(sent, axis, 0, 0, tiled=True, axis_index_groups=groups)]
    all_to_all x3 -> x1, waiting for transfers between devices: 22.7 us -> 4.2 us  [local(): came = lax.all_to_all(sent, 'batch', 0, 0, tiled=True)]
    pallas_call x0 -> x7, Pallas kernels: none -> 15.4 us  [the longest x1 8.77 us: team_products(): pl.pallas_call(team_kernel, grid=(senders,), in_specs=[pl.BlockSpec((2, 1...]
    dot_general x9 -> x1, matrix products: 10.2 us -> 0.6 us  [local(): jnp.dot(unit_rows(teacher), proto_n, preferred_element_type=jnp.float32)]
    all_to_all x3 -> x1, starting transfers between devices: 13.7 us -> 4.93 us  [local(): came = lax.all_to_all(sent, 'batch', 0, 0, tiled=True)]
    reduce_sum x3 -> x1, other arithmetic: 6.11 us -> 1.81 us  [unit_rows(): jnp.sum(xf * xf, 1, keepdims=True) + eps]
    convert_element_type x2 -> x0, other arithmetic: 4.01 us -> none  [the longest x1 2.12 us: unit_rows(): (xf * lax.rsqrt(jnp.sum(xf * xf, 1, keepdims=True) + eps)).astype(jnp.bfl...]
  transfers between devices with their start and end apart: 5 -> 4, of which waited for: 4 -> 3; matrix products, arithmetic and copies ran while one was open for 9% -> 4% of each run, Pallas kernels for 0% -> 6%
where the time goes in v3:
time: 189 us; the launch traced here: 188 us
  blocking collectives  116 us (61%)
  Pallas kernels  20.7 us (11%)
  waiting for transfers between devices  17 us (9%)
  between operations  14.2 us (8%)
  starting transfers between devices  10.3 us (5%)
  other arithmetic  6.36 us (3%)
  matrix products  2.64 us (1%)
    all_to_all x3, blocking collectives, local(): came = lax.all_to_all(sent, 'proto', 0, 0, tiled=True)  61.5 us
    all_to_all x2, blocking collectives, local(): came = lax.all_to_all(sent, 'batch', 0, 0, tiled=True)  45.5 us
    all_to_all x1, waiting for transfers between devices, local(): parts = lax.all_to_all(grad_t, 'batch', 0, 0, tiled=True)  12 us
    all_to_all x1, blocking collectives, spread(): lax.all_to_all(sent, axis, 0, 0, tiled=True, axis_index_groups=groups)  8.85 us
    pallas_call x1, Pallas kernels, team_products(): pl.pallas_call(team_kernel, grid=(senders,), in_specs=[pl.BlockSpec((2, 1...  8.77 us
    all_to_all x1, starting transfers between devices, local(): parts = lax.all_to_all(grad_t, 'batch', 0, 0, tiled=True)  5.32 us
    pallas_call x1, Pallas kernels, partial_grad(): pl.pallas_call(functools.partial(grad_kernel, count, scale), grid=(steps,...  5.27 us
    all_to_all x1, starting transfers between devices, local(): came = lax.all_to_all(sent, 'batch', 0, 0, tiled=True)  4.93 us
  transfers between devices with their start and end apart: 4, of which 3 were waited for; matrix products, arithmetic and copies ran while one was open for 4% of the time, Pallas kernels for 6%

profile of v3, /device:TPU:8, one launch (start us, length us, event | category | flops | bytes accessed | tf_op | source)
XLA Modules:
  0.0 187.8 jit_solution(9660930240656643948)
XLA Ops:
  7.2 1.8 fusion.12
  9.1 1.7 fusion.3
  10.8 1.0 fusion.5.proto_ref
  11.9 0.6 fusion.2.expo_ref
  12.8 24.8 %all_to_all.40.came_ref = f32[32,22,128]{2,1,0:T(8,128)S(1)} all-to-all(f32[32,22,128]{2,1,0:T(8,128)S(1)} %broadcast_in_dim.9), channel_id=1, replica_groups=mesh['proto'=24,'batch'=32] {'batch'}, dimensions={0} | all-to-all | bytes 720896 | tf_op jit(solution)/shard_map/all_to_all | solution.py:251
  37.6 0.9 shard_map.59
  38.6 26.5 %all_to_all.41.came_ref = f32[24,1,256]{2,1,0:T(1,128)} all-to-all(f32[24,1,256]{2,1,0:T(1,128)S(1)} %get-tuple-element.16), channel_id=1, replica_groups=mesh['proto'=24,'batch'=32] {'proto'}, dimensions={0} | all-to-all | bytes 49152 | tf_op jit(solution)/shard_map/all_to_all | solution.py:254
  65.1 0.8 all-gather.5.cloned.1.call-done
  65.8 2.5 %shard_map.60 = (f32[32,22,128]{2,1,0:T(8,128)}, f32[8,256,256]{2,1,0:T(8,128)}) custom-call(f32[24,1,256]{2,1,0:T(1,128)} %all_to_all.41.came_ref, bf16[256,2816]{1,0:T(8,128)(2,1)} %copy-done, f32[8,256,256]{2,1,0:T(8,128)} %bitcast.10), custom_call_target="tpu_custom_call", output_to_operand_aliasing={{1}: (2, {})} | custom-call | flops 1441792 | bytes 1441792 | tf_op jit(solution)/shard_map/pallas_call | solution.py:154
  68.4 20.7 %all_to_all.42.came_ref = f32[32,22,128]{2,1,0:T(8,128)S(1)} all-to-all(f32[32,22,128]{2,1,0:T(8,128)} %get-tuple-element.17), channel_id=1, replica_groups=mesh['proto'=24,'batch'=32] {'batch'}, dimensions={0} | all-to-all | bytes 720896 | tf_op jit(solution)/shard_map/all_to_all | solution.py:251
  89.1 0.9 shard_map.61
  90.0 21.7 %all_to_all.43.came_ref = f32[24,1,256]{2,1,0:T(1,128)S(1)} all-to-all(f32[24,1,256]{2,1,0:T(1,128)S(1)} %get-tuple-element.18), channel_id=1, replica_groups=mesh['proto'=24,'batch'=32] {'proto'}, dimensions={0} | all-to-all | bytes 49152 | tf_op jit(solution)/shard_map/all_to_all | solution.py:254
  111.7 1.2 shard_map.62.after_ref
  112.9 4.9 %all-to-all-start.4 = ((f32[32,22,128]{2,1,0:T(8,128)}), f32[32,22,128]{2,1,0:T(8,128)S(1)}, u32[]{:S(2)}, u32[]{:S(2)}) async-start(f32[32,22,128]{2,1,0:T(8,128)} %shard_map.62.after_ref), calls=%async_computation.4 | async-start | bytes 786432 | tf_op jit(solution)/shard_map/all_to_all | solution.py:251
  117.9 2.0 %fusion.9 = f32[256]{0:T(256)S(1)} fusion(bf16[256,2816]{1,0:T(8,128)(2,1)} %copy-done.5, bf16[256,256]{1,0:T(8,128)(2,1)S(1)} %copy-done.7, f32[256]{0:T(256)S(1)} %add_rsqrt_fusion.1), kind=kOutput, calls=%fused_computation.15 | convolution fusion | flops 370736896 | bytes 1574912 | tf_op jit(solution)/shard_map/dot_general | solution.py:256
  119.9 8.8 %shard_map.63 = (bf16[384,2048]{1,0:T(8,128)(2,1)}, f32[384,2048]{1,0:T(8,128)}, bf16[2048,256]{1,0:T(8,128)(2,1)}) custom-call(f32[2,8,256,256]{3,2,1,0:T(8,128)} %bitcast.11, bf16[256,2816]{1,0:T(8,128)(2,1)} %copy-done.5, f32[32,22,128]{2,1,0:T(8,128)} %shard_map.62.after_ref), custom_call_target="tpu_custom_call" | custom-call | flops 805306368 | bytes 10485760 | tf_op jit(solution)/shard_map/pallas_call | solution.py:190
  128.7 4.2 %all-to-all-done.4.came_ref = f32[32,22,128]{2,1,0:T(8,128)S(1)} async-done(((f32[32,22,128]{2,1,0:T(8,128)}), f32[32,22,128]{2,1,0:T(8,128)S(1)}, u32[]{:S(2)}, u32[]{:S(2)}) %all-to-all-start.4) | async-done | bytes 360480 | tf_op jit(solution)/shard_map/all_to_all | solution.py:251
  133.9 13.3 %all_to_all.44 = f32[24,2,256]{2,1,0:T(2,128)S(1)} all-to-all(f32[24,2,256]{2,1,0:T(2,128)S(1)} %get-tuple-element.26), channel_id=1, replica_groups=mesh['proto'=24,'batch'=32] {'proto'}, dimensions={0} | all-to-all | bytes 98304 | tf_op jit(solution)/shard_map/all_to_all | solution.py:263
  147.3 8.8 %all_to_all.45.rows_ref = f32[8,2,256]{2,1,0:T(2,128)} all-to-all(f32[8,2,256]{2,1,0:T(2,128)S(1)} %broadcast_in_dim.11), channel_id=1, replica_groups={{0,1,2,3,4,5,6,7},{8,9,10,11,12,13,14,15},{16,17,18,19,20,21,22,23},{24..., dimensions={0} | all-to-all | bytes 32768 | tf_op jit(solution)/shard_map/all_to_all | solution.py:29
  156.1 5.3 %shard_map.65 = f32[32,8,384]{2,1,0:T(8,128)} custom-call(bf16[384,2048]{1,0:T(8,128)(2,1)} %get-tuple-element.27.expo_ref, f32[384,2048]{1,0:T(8,128)} %get-tuple-element.28.student_exp_ref, bf16[2048,256]{1,0:T(8,128)(2,1)} %get-tuple-element.29.student_ref, f32[22,128]{1,0:T(8,128)} %copy-done.2, f32[8,2,256]{2,1,0:T(2,128)} %all_to_all.45.rows_ref), custom_call_target="tpu_custom_call" | custom-call | flops 402653184 | bytes 4718592 | tf_op jit(solution)/shard_map/pallas_call | solution.py:71
  161.4 5.3 %all-to-all-start.7 = ((f32[32,8,384]{2,1,0:T(8,128)}), f32[32,8,384]{2,1,0:T(8,128)S(1)}, u32[]{:S(2)}, u32[]{:S(2)}) async-start(f32[32,8,384]{2,1,0:T(8,128)} %shard_map.65), calls=%async_computation.7 | async-start | bytes 786432 | tf_op jit(solution)/shard_map/all_to_all | solution.py:272
  166.7 1.5 fusion.8
  168.3 12.0 %all-to-all-done.7.parts_ref = f32[32,8,384]{2,1,0:T(8,128)S(1)} async-done(((f32[32,8,384]{2,1,0:T(8,128)}), f32[32,8,384]{2,1,0:T(8,128)S(1)}, u32[]{:S(2)}, u32[]{:S(2)}) %all-to-all-start.7) | async-done | bytes 393248 | tf_op jit(solution)/shard_map/all_to_all | solution.py:272
  180.3 0.7 shard_map.66
  (31 shorter events, 1.5 us)
Async XLA Ops:
  7.2 4.7 %copy-start.6 = (bf16[256,256]{1,0:T(8,128)(2,1)S(1)}, bf16[256,256]{1,0:T(8,128)(2,1)}, u32[]{:S(2)}) copy-start(bf16[256,256]{1,0:T(8,128)(2,1)} %param.4) | copy-start | bytes 393220
  7.2 3.7 %copy-start.4 = (bf16[256,2816]{1,0:T(8,128)(2,1)S(1)}, bf16[256,2816]{1,0:T(8,128)(2,1)}, u32[]{:S(2)}) copy-start(bf16[256,2816]{1,0:T(8,128)(2,1)} %param.6) | copy-start | bytes 4325380
  7.2 58.6 %all-gather.5.cloned.1.call-start = ((), (), s32[]{:S(2)}) async-start(), calls=%async_computation.8 | async-start | bytes 2359296 | tf_op jit(solution)/shard_map/all_gather | solution.py:227
  9.1 110.9 %all-gather.7.cloned.1.call-start = ((), (), s32[]{:S(2)}) async-start(), calls=%async_computation.9 | async-start | bytes 6291456 | tf_op jit(solution)/shard_map/all_gather | solution.py:248
  11.9 25.7 %copy-start.5 = (bf16[256,2816]{1,0:T(8,128)(2,1)}, bf16[256,2816]{1,0:T(8,128)(2,1)S(1)}, u32[]{:S(2)}) copy-start(bf16[256,2816]{1,0:T(8,128)(2,1)S(1)} %fusion.5.proto_ref) | copy-start | bytes 4325380
  12.5 53.3 %copy-start = (bf16[256,2816]{1,0:T(8,128)(2,1)}, bf16[256,2816]{1,0:T(8,128)(2,1)S(1)}, u32[]{:S(2)}) copy-start(bf16[256,2816]{1,0:T(8,128)(2,1)S(1)} %fusion.2.expo_ref) | copy-start | bytes 4325380
  68.4 20.7 %copy-start.1 = (bf16[256,2816]{1,0:T(8,128)(2,1)S(1)}, bf16[256,2816]{1,0:T(8,128)(2,1)}, u32[]{:S(2)}) copy-start(bf16[256,2816]{1,0:T(8,128)(2,1)} %copy-done) | copy-start | bytes 4325380
  68.4 49.5 %copy-start.7 = (bf16[256,256]{1,0:T(8,128)(2,1)S(1)}, bf16[256,256]{1,0:T(8,128)(2,1)}, u32[]{:S(2)}) copy-start(bf16[256,256]{1,0:T(8,128)(2,1)} %param.5) | copy-start | bytes 393220
  112.9 20.0 %all-to-all-start.4 = ((f32[32,22,128]{2,1,0:T(8,128)}), f32[32,22,128]{2,1,0:T(8,128)S(1)}, u32[]{:S(2)}, u32[]{:S(2)}) async-start(f32[32,22,128]{2,1,0:T(8,128)} %shard_map.62.after_ref), calls=%async_computation.4 | async-start | bytes 786432 | tf_op jit(solution)/shard_map/all_to_all | solution.py:251
  133.3 0.6 copy-start.2
  156.1 10.6 %copy-start.3 = (f32[22,128]{1,0:T(8,128)S(1)}, f32[22,128]{1,0:T(8,128)}, u32[]{:S(2)}) copy-start(f32[22,128]{1,0:T(8,128)} %copy-done.2) | copy-start | bytes 33796
  161.4 18.9 %all-to-all-start.7 = ((f32[32,8,384]{2,1,0:T(8,128)}), f32[32,8,384]{2,1,0:T(8,128)S(1)}, u32[]{:S(2)}, u32[]{:S(2)}) async-start(f32[32,8,384]{2,1,0:T(8,128)} %shard_map.65), calls=%async_computation.7 | async-start | bytes 786432 | tf_op jit(solution)/shard_map/all_to_all | solution.py:272
Sparse Core Ops, SparseCore 0:
  10.4 55.3 all-gather.4
  68.5 26.2 all-gather.6

commit v4 on v3

--- a/solution.py
+++ b/solution.py
@@ -33,29 +33,40 @@
     return jnp.minimum(lax.axis_index("batch") % TEAM * HELD, groups - HELD)
 
 
-def grad_kernel(count, scale, expo_ref, student_exp_ref, student_ref, u_ref, rows_ref, out_ref, acc, u_wide):
+def grad_kernel(count, scale, expo_ref, student_exp_ref, student_ref, u_ref, rows_ref, out_ref, acc, u_wide, diff):
     step = pl.program_id(0)
+    rows = rows_ref.shape[2]
+    crops = diff.shape[1]
 
     @pl.when(step == 0)
     def _():
-        acc[...] = jnp.zeros_like(acc)
         u = u_ref[pl.ds(first_group(u_ref.shape[0]), HELD), :]
         for g in range(HELD):
             wide = jnp.broadcast_to(u[g : g + 1, :], (LANES, LANES)).T
             u_wide[g * LANES : (g + 1) * LANES, :] = wide
 
-    rows = rows_ref.shape[2]
-    u = u_wide[...]
-    for s in range(rows_ref.shape[0]):
+    me = lax.axis_index("batch") % TEAM
+    for s in range(crops // rows):
+        place = step * (crops // rows) + s
+        by = rows_ref[me ^ place ^ ((place >> 1) & 1)]
         for start in range(0, rows, LANES):
-            v = rows_ref[s, 0:1, start : start + LANES]
-            inv_total = rows_ref[s, 1:2, start : start + LANES]
+            v = by[0:1, start : start + LANES]
+            inv_total = by[1:2, start : start + LANES]
             span = slice(s * rows + start, s * rows + start + LANES)
-            assign = expo_ref[:, span].astype(jnp.float32) * u * v
-            diff = count * (student_exp_ref[:, span] * inv_total - assign)
-            acc[...] += jnp.dot(
-                diff.astype(jnp.bfloat16), student_ref[span, :], preferred_element_type=jnp.float32
-            )
+            for g in range(HELD):
+                part = slice(g * LANES, (g + 1) * LANES)
+                assign = expo_ref[part, span].astype(jnp.float32) * u_wide[part, :] * v
+                prob = student_exp_ref[part, span] * inv_total
+                diff[part, span] = (count * (prob - assign)).astype(jnp.bfloat16)
+    product = jnp.dot(diff[...], student_ref[...], preferred_element_type=jnp.float32)
+
+    @pl.when(step == 0)
+    def _():
+        acc[...] = product
+
+    @pl.when(step > 0)
+    def _():
+        acc[...] += product
 
     @pl.when(step == pl.num_programs(0) - 1)
     def _():
@@ -76,13 +87,14 @@
             pl.BlockSpec((part, chunk), lambda i: (0, i)),
             pl.BlockSpec((chunk, depth), lambda i: (i, 0)),
             pl.BlockSpec(u.shape, lambda i: (0, 0)),
-            pl.BlockSpec((senders // steps, 2, rows), lambda i: (i, 0, 0)),
+            pl.BlockSpec(by_sender.shape, lambda i: (0, 0, 0)),
         ],
         out_specs=pl.BlockSpec((owners, depth // owners, part), lambda i: (0, 0, 0)),
         out_shape=jax.ShapeDtypeStruct((owners, depth // owners, part), jnp.float32),
         scratch_shapes=[
             pltpu.VMEM((part, depth), jnp.float32),
             pltpu.VMEM((part, LANES), jnp.float32),
+            pltpu.VMEM((part, chunk), jnp.bfloat16),
         ],
         compiler_params=pltpu.CompilerParams(vmem_limit_bytes=VMEM),
         cost_estimate=pl.CostEstimate(
@@ -136,8 +148,7 @@
     )(came, expo, *more)
 
 
-def column_kernel(came_ref, expo_ref, *refs):
-    sent_ref = refs[len(refs) // 2]
+def column_kernel(came_ref, expo_ref, sent_ref):
     rows = expo_ref.shape[0]
     v = 1.0 / jnp.sum(came_ref[...], 0)
     v = jnp.broadcast_to(v, (LANES, rows)).T
@@ -148,23 +159,28 @@
     sent_ref[1:] = jnp.broadcast_to(sent_ref[0:1], (peers - 1, groups, LANES))
 
 
-def column_terms(came, expo, peers, passed=None):
+def column_terms(came, expo, peers):
     groups = expo.shape[1] // LANES
-    more = () if passed is None else (passed,)
-    out = pl.pallas_call(
+    return pl.pallas_call(
         column_kernel,
-        in_specs=[pl.BlockSpec(), pl.BlockSpec()] + [pl.BlockSpec(memory_space=pl.ANY)] * len(more),
-        out_specs=[pl.BlockSpec()] + [pl.BlockSpec(memory_space=pl.ANY)] * len(more),
-        out_shape=[jax.ShapeDtypeStruct((peers, groups, LANES), jnp.float32)]
-        + [jax.ShapeDtypeStruct(m.shape, m.dtype) for m in more],
-        input_output_aliases={2: 1} if more else {},
-        compiler_params=pltpu.CompilerParams(vmem_limit_bytes=PASSING if more else SMALL),
+        out_shape=jax.ShapeDtypeStruct((peers, groups, LANES), jnp.float32),
+        compiler_params=pltpu.CompilerParams(vmem_limit_bytes=SMALL),
         cost_estimate=pl.CostEstimate(flops=2 * expo.size, bytes_accessed=2 * expo.size, transcendentals=0),
-    )(came, expo, *more)
-    return out if more else out[0]
-
-
-def team_kernel(rows_ref, proto_ref, after_ref, expo_ref, student_exp_ref, student_ref, proto_t):
+    )(came, expo)
+
+
+def after(value, other):
+    return pl.pallas_call(
+        lambda value_ref, other_ref, out_ref: None,
+        in_specs=[pl.BlockSpec(memory_space=pl.ANY)] * 2,
+        out_specs=pl.BlockSpec(memory_space=pl.ANY),
+        out_shape=jax.ShapeDtypeStruct(value.shape, value.dtype),
+        input_output_aliases={0: 0},
+        compiler_params=pltpu.CompilerParams(vmem_limit_bytes=VMEM),
+    )(value, other)
+
+
+def team_kernel(own_ref, other_ref, proto_ref, after_ref, expo_ref, student_exp_ref, student_ref, proto_t):
     @pl.when(pl.program_id(0) == 0)
     def _():
         start = pl.multiple_of(first_group(proto_ref.shape[1] // LANES) * LANES, LANES)
@@ -174,9 +190,10 @@
         return (x * lax.rsqrt(jnp.sum(x * x, 1, keepdims=True) + eps)).astype(jnp.bfloat16)
 
     across = (((1,), (1,)), ((), ()))
+    first = lax.axis_index("proto") % 2 == 0
     proto = proto_t[...]
-    t = unit(rows_ref[0, 0])
-    s = unit(rows_ref[1, 0])
+    t = unit(jnp.where(first, own_ref[0], other_ref[0]))
+    s = unit(jnp.where(first, other_ref[0], own_ref[0]))
     student_ref[...] = s
     lt = lax.dot_general(proto, t, across, preferred_element_type=jnp.float32)
     expo_ref[...] = jnp.exp(lt / teacher_temp).astype(jnp.bfloat16)
@@ -184,14 +201,15 @@
     student_exp_ref[...] = jnp.exp(ls / student_temp)
 
 
-def team_products(gathered, proto, after):
-    _, senders, rows, depth = gathered.shape
+def team_products(own, other, proto, waited):
+    senders, rows, depth = own.shape
     part = HELD * LANES
     return pl.pallas_call(
         team_kernel,
         grid=(senders,),
         in_specs=[
-            pl.BlockSpec((2, 1, rows, depth), lambda i: (0, i, 0, 0)),
+            pl.BlockSpec((1, rows, depth), lambda i: (i, 0, 0)),
+            pl.BlockSpec((1, rows, depth), lambda i: (i, 0, 0)),
             pl.BlockSpec(proto.shape, lambda i: (0, 0)),
             pl.BlockSpec(memory_space=pl.ANY),
         ],
@@ -212,19 +230,20 @@
             bytes_accessed=10 * 2**20,
             transcendentals=2 * part * senders * rows,
         ),
-    )(gathered, proto, after)
+    )(own, other, proto, waited)
 
 
 def local(teacher, student, prototypes, gain):
     rows, depth = teacher.shape
     nb, npr = lax.axis_size("batch"), lax.axis_size("proto")
     teams = [[t * TEAM + i for i in range(TEAM)] for t in range(nb // TEAM)]
-    chips = [[2 * z, 2 * z + 1] for z in range(npr // 2)]
     core = lax.axis_index("proto") % 2
 
     mine = jnp.where(core == 0, teacher.astype(jnp.float32), student.astype(jnp.float32))
-    mine = lax.optimization_barrier(mine)
-    gathered = lax.all_gather(mine, "batch", axis_index_groups=teams)
+    held = lax.optimization_barrier(mine)[None]
+
+    def collect(held, flip):
+        return lax.ppermute(held, "batch", [(i, i ^ flip) for i in range(nb)])
 
     wf = prototypes.astype(jnp.float32)
     proto_n = (wf * lax.rsqrt(jnp.sum(wf * wf, 0, keepdims=True) + eps) * gain[None, :]).astype(
@@ -242,25 +261,23 @@
     sent = jnp.sum(expo.astype(jnp.float32), 0).reshape(groups, LANES)
     sent = jnp.broadcast_to(sent[None], (nb, groups, LANES))
     for step in range(ITERS):
-        last = step + 1 == ITERS
-        if step == 1:
-            sent, gathered = column_terms(came, expo, nb, gathered)
-            gathered = lax.all_gather(gathered, "proto", axis_index_groups=chips)
-        elif step:
+        if step:
             sent = column_terms(came, expo, nb)
         came = lax.all_to_all(sent, "batch", 0, 0, tiled=True)
-        if not last:
+        if step + 1 < ITERS:
+            held = jnp.concatenate([held, collect(held, 1 + 2 * step)])
             sent, _ = row_terms(came, expo, npr)
+            held = after(held, sent)
             came = lax.all_to_all(sent, "proto", 0, 0, tiled=True)
+    held = jnp.concatenate([held, collect(held, 4)])
+    held = after(held, sent)
+    other = lax.ppermute(held, "proto", [(i, i ^ 1) for i in range(npr)])
 
     logits = jnp.dot(unit_rows(student), proto_n, preferred_element_type=jnp.float32)
     local_total = jnp.sum(jnp.exp(logits / student_temp), 1)
-    team_values = team_products(gathered, proto_n, sent)
-    came, team_values, local_total = lax.optimization_barrier((came, team_values, local_total))
-    expo_t, student_exp_t, student_t = team_values
-
     sent, scale_u = row_terms(came, expo, npr, local_total[None])
     came = lax.all_to_all(sent, "proto", 0, 0, tiled=True)
+    expo_t, student_exp_t, student_t = team_products(held, other, proto_n, sent)
     inverse = 1.0 / jnp.sum(came, 0)
     scale_v = inverse[0]
     by_sender = spread(inverse, "batch", TEAM, teams)

time: 189 us -> 200 us (1.058)
  blocking collectives: 116 us -> 52 us
  waiting for transfers between devices: 17 us -> 59.5 us
  starting transfers between devices: 10.3 us -> 50.1 us
  between operations: 14.2 us -> 0.86 us
  other arithmetic: 6.36 us -> 11.5 us
  local copies, waits for them, and re-layouts: 0.67 us -> 4.3 us
    all_to_all x3 -> x0, blocking collectives: 54.4 us -> none  [the longest x2 45.5 us: local(): came = lax.all_to_all(sent, 'batch', 0, 0, tiled=True)]
    ppermute x0 -> x4, waiting for transfers between devices: none -> 23.3 us  [the longest x3 23.3 us: collect(): return lax.ppermute(held, 'batch', [(i, i ^ flip) for i in range(nb)])]
    all_to_all x1 -> x3, starting transfers between devices: 4.93 us -> 26.3 us  [local(): came = lax.all_to_all(sent, 'batch', 0, 0, tiled=True)]
    all_to_all x1 -> x3, waiting for transfers between devices: 4.2 us -> 23.2 us  [local(): came = lax.all_to_all(sent, 'batch', 0, 0, tiled=True)]
    ppermute x0 -> x4, starting transfers between devices: none -> 12.8 us  [the longest x3 10.8 us: collect(): return lax.ppermute(held, 'batch', [(i, i ^ flip) for i in range(nb)])]
    all_to_all x3, blocking collectives: 61.5 us -> 52 us  [local(): came = lax.all_to_all(sent, 'proto', 0, 0, tiled=True)]
    concatenate x0 -> x3, other arithmetic: none -> 5.75 us  [the longest x2 2.96 us: local(): held = jnp.concatenate([held, collect(held, 1 + 2 * step)])]
    all_to_all x0 -> x1, starting transfers between devices: none -> 4.26 us  [spread(): lax.all_to_all(sent, axis, 0, 0, tiled=True, axis_index_groups=groups)]
  transfers between devices with their start and end apart: 4 -> 9, of which waited for: 3 -> 5; matrix products, arithmetic and copies ran while one was open for 4% -> 3% of each run, Pallas kernels for 6% -> 6%
where the time goes in v4:
time: 200 us; the launch traced here: 199 us
  waiting for transfers between devices  59.5 us (30%)
  blocking collectives  52 us (26%)
  starting transfers between devices  50.1 us (25%)
  Pallas kernels  19.6 us (10%)
  other arithmetic  11.5 us (6%)
  local copies, waits for them, and re-layouts  4.3 us (2%)
    all_to_all x3, blocking collectives, local(): came = lax.all_to_all(sent, 'proto', 0, 0, tiled=True)  52 us
    all_to_all x3, starting transfers between devices, local(): came = lax.all_to_all(sent, 'batch', 0, 0, tiled=True)  26.3 us
    ppermute x3, waiting for transfers between devices, collect(): return lax.ppermute(held, 'batch', [(i, i ^ flip) for i in range(nb)])  23.3 us
    all_to_all x3, waiting for transfers between devices, local(): came = lax.all_to_all(sent, 'batch', 0, 0, tiled=True)  23.2 us
    all_to_all x1, waiting for transfers between devices, local(): parts = lax.all_to_all(grad_t, 'batch', 0, 0, tiled=True)  13.1 us
    ppermute x3, starting transfers between devices, collect(): return lax.ppermute(held, 'batch', [(i, i ^ flip) for i in range(nb)])  10.8 us
    pallas_call x1, Pallas kernels, team_products(): pl.pallas_call(team_kernel, grid=(senders,), in_specs=[pl.BlockSpec((1, r...  8.94 us
    all_to_all x1, starting transfers between devices, local(): parts = lax.all_to_all(grad_t, 'batch', 0, 0, tiled=True)  6.71 us
  transfers between devices with their start and end apart: 9, of which 5 were waited for; matrix products, arithmetic and copies ran while one was open for 3% of the time, Pallas kernels for 6%

profile of v4, /device:TPU:8, one launch (start us, length us, event | category | flops | bytes accessed | tf_op | source)
XLA Modules:
  0.0 199.1 jit_solution(14175679385379922467)
XLA Ops:
  0.7 1.8 fusion.3
  7.4 13.0 %all-to-all-start = ((f32[32,22,128]{2,1,0:T(8,128)}), f32[32,22,128]{2,1,0:T(8,128)S(1)}, u32[]{:S(2)}, u32[]{:S(2)}) async-start(f32[32,22,128]{2,1,0:T(8,128)} %broadcast_in_dim.11), calls=%async_computation | async-start | bytes 786432 | tf_op jit(solution)/shard_map/all_to_all | solution.py:266
  20.4 3.4 %collective-permute-start = (f32[1,256,256]{2,1,0:T(8,128)S(1)}, f32[1,256,256]{2,1,0:T(8,128)S(1)}, u32[]{:S(2)}, u32[]{:S(2)}) collective-permute-start(f32[1,256,256]{2,1,0:T(8,128)S(1)} %bitcast.9), channel_id=1, source_target_pairs={{0,1},{1,0},{2,3},{3,2},{4,5},{5,4},{6,7},{7,6},{8,9},{9,8},{10,11... | collective-permute-start | bytes 786440 | tf_op jit(solution)/shard_map/ppermute | solution.py:246
  23.8 8.6 %all-to-all-done.came_ref = f32[32,22,128]{2,1,0:T(8,128)S(1)} async-done(((f32[32,22,128]{2,1,0:T(8,128)}), f32[32,22,128]{2,1,0:T(8,128)S(1)}, u32[]{:S(2)}, u32[]{:S(2)}) %all-to-all-start) | async-done | bytes 360480 | tf_op jit(solution)/shard_map/all_to_all | solution.py:266
  33.3 25.0 %all_to_all.40.came_ref = f32[24,1,256]{2,1,0:T(1,128)S(1)} all-to-all(f32[24,1,256]{2,1,0:T(1,128)S(1)} %get-tuple-element.9.other_ref), channel_id=1, replica_groups=mesh['proto'=24,'batch'=32] {'proto'}, dimensions={0} | all-to-all | bytes 49152 | tf_op jit(solution)/shard_map/all_to_all | solution.py:271
  59.5 4.9 %all-to-all-start.2 = ((f32[32,22,128]{2,1,0:T(8,128)}), f32[32,22,128]{2,1,0:T(8,128)S(1)}, u32[]{:S(2)}, u32[]{:S(2)}) async-start(f32[32,22,128]{2,1,0:T(8,128)} %shard_map.60), calls=%async_computation.2 | async-start | bytes 786432 | tf_op jit(solution)/shard_map/all_to_all | solution.py:266
  65.2 4.6 %collective-permute-start.1 = (f32[2,256,256]{2,1,0:T(8,128)}, f32[2,256,256]{2,1,0:T(8,128)S(1)}, u32[]{:S(2)}, u32[]{:S(2)}) collective-permute-start(f32[2,256,256]{2,1,0:T(8,128)} %shard_map.64), channel_id=1, source_target_pairs={{0,3},{1,2},{2,1},{3,0},{4,7},{5,6},{6,5},{7,4},{8,11},{9,10},{10,... | collective-permute-start | bytes 1572872 | tf_op jit(solution)/shard_map/ppermute | solution.py:246
  69.8 15.0 %collective-permute-done.1 = f32[2,256,256]{2,1,0:T(8,128)S(1)} collective-permute-done((f32[2,256,256]{2,1,0:T(8,128)}, f32[2,256,256]{2,1,0:T(8,128)S(1)}, u32[]{:S(2)}, u32[]{:S(2)}) %collective-permute-start.1) | collective-permute-done | bytes 524320 | tf_op jit(solution)/shard_map/ppermute | solution.py:246
  84.8 2.1 %pad_maximum_fusion.1.value_ref = f32[4,256,256]{2,1,0:T(8,128)} fusion(f32[2,256,256]{2,1,0:T(8,128)S(1)} %collective-permute-done.1, f32[2,256,256]{2,1,0:T(8,128)} %shard_map.64), kind=kLoop, calls=%fused_computation.17 | loop fusion | flops 262144 | bytes 2097152 | tf_op jit(solution)/shard_map/concatenate | solution.py:268
  88.4 2.8 %collective-permute-start.2 = (f32[4,256,256]{2,1,0:T(8,128)}, f32[4,256,256]{2,1,0:T(8,128)S(1)}, u32[]{:S(2)}, u32[]{:S(2)}) collective-permute-start(f32[4,256,256]{2,1,0:T(8,128)} %shard_map.65), channel_id=1, source_target_pairs={{0,4},{1,5},{2,6},{3,7},{4,0},{5,1},{6,2},{7,3},{8,12},{9,13},{10,... | collective-permute-start | bytes 3145736 | tf_op jit(solution)/shard_map/ppermute | solution.py:246
  91.3 13.8 %all_to_all.41.came_ref = f32[24,1,256]{2,1,0:T(1,128)S(1)} all-to-all(f32[24,1,256]{2,1,0:T(1,128)} %copy-done.1), channel_id=1, replica_groups=mesh['proto'=24,'batch'=32] {'proto'}, dimensions={0} | all-to-all | bytes 49152 | tf_op jit(solution)/shard_map/all_to_all | solution.py:271
  105.0 1.2 shard_map.62.other_ref
  106.2 8.3 %collective-permute-done.2 = f32[4,256,256]{2,1,0:T(8,128)S(1)} collective-permute-done((f32[4,256,256]{2,1,0:T(8,128)}, f32[4,256,256]{2,1,0:T(8,128)S(1)}, u32[]{:S(2)}, u32[]{:S(2)}) %collective-permute-start.2) | collective-permute-done | bytes 1048608 | tf_op jit(solution)/shard_map/ppermute | solution.py:246
  114.5 2.8 %pad_maximum_fusion.value_ref = f32[8,256,256]{2,1,0:T(8,128)} fusion(f32[4,256,256]{2,1,0:T(8,128)S(1)} %collective-permute-done.2, f32[4,256,256]{2,1,0:T(8,128)} %shard_map.65), kind=kLoop, calls=%fused_computation.15 | loop fusion | flops 524288 | bytes 4194304 | tf_op jit(solution)/shard_map/concatenate | solution.py:272
  117.3 2.0 %collective-permute-start.3 = (f32[8,256,256]{2,1,0:T(8,128)}, f32[8,256,256]{2,1,0:T(8,128)}, u32[]{:S(2)}, u32[]{:S(2)}) collective-permute-start(f32[8,256,256]{2,1,0:T(8,128)} %shard_map.66.own_ref), channel_id=1, source_target_pairs={{0,32},{32,0},{64,96},{96,64},{128,160},{160,128},{192,224},{224,1... | collective-permute-start | bytes 6291464 | tf_op jit(solution)/shard_map/ppermute | solution.py:274
  119.3 8.4 %all-to-all-start.4 = ((f32[32,22,128]{2,1,0:T(8,128)}), f32[32,22,128]{2,1,0:T(8,128)S(1)}, u32[]{:S(2)}, u32[]{:S(2)}) async-start(f32[32,22,128]{2,1,0:T(8,128)} %shard_map.62.other_ref), calls=%async_computation.4 | async-start | bytes 786432 | tf_op jit(solution)/shard_map/all_to_all | solution.py:266
  128.4 14.6 %all-to-all-done.4.came_ref = f32[32,22,128]{2,1,0:T(8,128)S(1)} async-done(((f32[32,22,128]{2,1,0:T(8,128)}), f32[32,22,128]{2,1,0:T(8,128)S(1)}, u32[]{:S(2)}, u32[]{:S(2)}) %all-to-all-start.4) | async-done | bytes 360480 | tf_op jit(solution)/shard_map/all_to_all | solution.py:266
  144.0 13.3 %all_to_all.42 = f32[24,2,256]{2,1,0:T(2,128)S(1)} all-to-all(f32[24,2,256]{2,1,0:T(2,128)S(1)} %get-tuple-element.12.after_ref), channel_id=1, replica_groups=mesh['proto'=24,'batch'=32] {'proto'}, dimensions={0} | all-to-all | bytes 98304 | tf_op jit(solution)/shard_map/all_to_all | solution.py:279
  157.9 4.3 %all-to-all-start.6 = ((f32[8,2,256]{2,1,0:T(2,128)}), f32[8,2,256]{2,1,0:T(2,128)S(1)}, u32[]{:S(2)}, u32[]{:S(2)}) async-start(f32[8,2,256]{2,1,0:T(2,128)} %broadcast_in_dim.27), calls=%async_computation.6 | async-start | bytes 32768 | tf_op jit(solution)/shard_map/all_to_all | solution.py:29
  162.2 8.9 %shard_map.67 = (bf16[384,2048]{1,0:T(8,128)(2,1)}, f32[384,2048]{1,0:T(8,128)}, bf16[2048,256]{1,0:T(8,128)(2,1)}) custom-call(f32[8,256,256]{2,1,0:T(8,128)} %shard_map.66.own_ref, f32[8,256,256]{2,1,0:T(8,128)} %collective-permute-done.3.other_ref, bf16[256,2816]{1,0:T(8,128)(2,1)} %copy-done.6, f32[24,2,256]{2,1,0:T(2,128)} %copy-done), custom_call_target="tpu_custom_call" | custom-call | flops 805306368 | bytes 10485760 | tf_op jit(solution)/shard_map/pallas_call | solution.py:207
  171.7 5.4 %shard_map.68 = f32[32,8,384]{2,1,0:T(8,128)} custom-call(bf16[384,2048]{1,0:T(8,128)(2,1)} %get-tuple-element.13.expo_ref, f32[384,2048]{1,0:T(8,128)} %get-tuple-element.14.student_exp_ref, bf16[2048,256]{1,0:T(8,128)(2,1)} %get-tuple-element.15.student_ref, f32[22,128]{1,0:T(8,128)} %copy-done.3, f32[8,2,256]{2,1,0:T(2,128)} %copy-done.10), custom_call_target="tpu_custom_call" | custom-call | flops 402653184 | bytes 4718592 | tf_op jit(solution)/shard_map/pallas_call | solution.py:82
  177.1 6.7 %all-to-all-start.7 = ((f32[32,8,384]{2,1,0:T(8,128)}), f32[32,8,384]{2,1,0:T(8,128)S(1)}, u32[]{:S(2)}, u32[]{:S(2)}) async-start(f32[32,8,384]{2,1,0:T(8,128)} %shard_map.68), calls=%async_computation.7 | async-start | bytes 786432 | tf_op jit(solution)/shard_map/all_to_all | solution.py:289
  183.9 1.5 fusion.8
  185.4 13.1 %all-to-all-done.7.parts_ref = f32[32,8,384]{2,1,0:T(8,128)S(1)} async-done(((f32[32,8,384]{2,1,0:T(8,128)}), f32[32,8,384]{2,1,0:T(8,128)S(1)}, u32[]{:S(2)}, u32[]{:S(2)}) %all-to-all-start.7) | async-done | bytes 393248 | tf_op jit(solution)/shard_map/all_to_all | solution.py:289
  (47 shorter events, 13.0 us)
Async XLA Ops:
  0.6 3.0 %copy-start.5 = (bf16[256,2816]{1,0:T(8,128)(2,1)S(1)}, bf16[256,2816]{1,0:T(8,128)(2,1)}, u32[]{:S(2)}) copy-start(bf16[256,2816]{1,0:T(8,128)(2,1)} %param.6) | copy-start | bytes 4325380
  0.6 5.1 %copy-start.8 = (bf16[256,256]{1,0:T(8,128)(2,1)S(1)}, bf16[256,256]{1,0:T(8,128)(2,1)}, u32[]{:S(2)}) copy-start(bf16[256,256]{1,0:T(8,128)(2,1)} %param.4) | copy-start | bytes 393220
  4.7 1.1 copy-start.6
  7.4 25.0 %all-to-all-start = ((f32[32,22,128]{2,1,0:T(8,128)}), f32[32,22,128]{2,1,0:T(8,128)S(1)}, u32[]{:S(2)}, u32[]{:S(2)}) async-start(f32[32,22,128]{2,1,0:T(8,128)} %broadcast_in_dim.11), calls=%async_computation | async-start | bytes 786432 | tf_op jit(solution)/shard_map/all_to_all | solution.py:266
  20.4 44.0 %collective-permute-start = (f32[1,256,256]{2,1,0:T(8,128)S(1)}, f32[1,256,256]{2,1,0:T(8,128)S(1)}, u32[]{:S(2)}, u32[]{:S(2)}) collective-permute-start(f32[1,256,256]{2,1,0:T(8,128)S(1)} %bitcast.9), channel_id=1, source_target_pairs={{0,1},{1,0},{2,3},{3,2},{4,5},{5,4},{6,7},{7,6},{8,9},{9,8},{10,11... | collective-permute-start | bytes 786440 | tf_op jit(solution)/shard_map/ppermute | solution.py:246
  33.3 31.9 %copy-start.2 = (f32[24,1,256]{2,1,0:T(1,128)}, f32[24,1,256]{2,1,0:T(1,128)S(1)}, u32[]{:S(2)}) copy-start(f32[24,1,256]{2,1,0:T(1,128)S(1)} %get-tuple-element.9.other_ref) | copy-start | bytes 73732
  59.5 27.4 %all-to-all-start.2 = ((f32[32,22,128]{2,1,0:T(8,128)}), f32[32,22,128]{2,1,0:T(8,128)S(1)}, u32[]{:S(2)}, u32[]{:S(2)}) async-start(f32[32,22,128]{2,1,0:T(8,128)} %shard_map.60), calls=%async_computation.2 | async-start | bytes 786432 | tf_op jit(solution)/shard_map/all_to_all | solution.py:266
  65.2 19.6 %collective-permute-start.1 = (f32[2,256,256]{2,1,0:T(8,128)}, f32[2,256,256]{2,1,0:T(8,128)S(1)}, u32[]{:S(2)}, u32[]{:S(2)}) collective-permute-start(f32[2,256,256]{2,1,0:T(8,128)} %shard_map.64), channel_id=1, source_target_pairs={{0,3},{1,2},{2,1},{3,0},{4,7},{5,6},{6,5},{7,4},{8,11},{9,10},{10,... | collective-permute-start | bytes 1572872 | tf_op jit(solution)/shard_map/ppermute | solution.py:246
  87.8 0.6 copy-start.1
  88.4 26.0 %collective-permute-start.2 = (f32[4,256,256]{2,1,0:T(8,128)}, f32[4,256,256]{2,1,0:T(8,128)S(1)}, u32[]{:S(2)}, u32[]{:S(2)}) collective-permute-start(f32[4,256,256]{2,1,0:T(8,128)} %shard_map.65), channel_id=1, source_target_pairs={{0,4},{1,5},{2,6},{3,7},{4,0},{5,1},{6,2},{7,3},{8,12},{9,13},{10,... | collective-permute-start | bytes 3145736 | tf_op jit(solution)/shard_map/ppermute | solution.py:246
  117.3 10.5 %copy-start.7 = (bf16[256,2816]{1,0:T(8,128)(2,1)S(1)}, bf16[256,2816]{1,0:T(8,128)(2,1)}, u32[]{:S(2)}) copy-start(bf16[256,2816]{1,0:T(8,128)(2,1)} %copy-done.6) | copy-start | bytes 4325380
  117.3 10.5 %copy-start.9 = (bf16[256,256]{1,0:T(8,128)(2,1)S(1)}, bf16[256,256]{1,0:T(8,128)(2,1)}, u32[]{:S(2)}) copy-start(bf16[256,256]{1,0:T(8,128)(2,1)} %param.5) | copy-start | bytes 393220
  117.3 44.9 %collective-permute-start.3 = (f32[8,256,256]{2,1,0:T(8,128)}, f32[8,256,256]{2,1,0:T(8,128)}, u32[]{:S(2)}, u32[]{:S(2)}) collective-permute-start(f32[8,256,256]{2,1,0:T(8,128)} %shard_map.66.own_ref), channel_id=1, source_target_pairs={{0,32},{32,0},{64,96},{96,64},{128,160},{160,128},{192,224},{224,1... | collective-permute-start | bytes 6291464 | tf_op jit(solution)/shard_map/ppermute | solution.py:274
  119.3 23.7 %all-to-all-start.4 = ((f32[32,22,128]{2,1,0:T(8,128)}), f32[32,22,128]{2,1,0:T(8,128)S(1)}, u32[]{:S(2)}, u32[]{:S(2)}) async-start(f32[32,22,128]{2,1,0:T(8,128)} %shard_map.62.other_ref), calls=%async_computation.4 | async-start | bytes 786432 | tf_op jit(solution)/shard_map/all_to_all | solution.py:266
  143.4 0.6 copy-start.3
  144.0 18.2 %copy-start = (f32[24,2,256]{2,1,0:T(2,128)}, f32[24,2,256]{2,1,0:T(2,128)S(1)}, u32[]{:S(2)}) copy-start(f32[24,2,256]{2,1,0:T(2,128)S(1)} %get-tuple-element.12.after_ref) | copy-start | bytes 147460
  157.9 13.2 %all-to-all-start.6 = ((f32[8,2,256]{2,1,0:T(2,128)}), f32[8,2,256]{2,1,0:T(2,128)S(1)}, u32[]{:S(2)}, u32[]{:S(2)}) async-start(f32[8,2,256]{2,1,0:T(2,128)} %broadcast_in_dim.27), calls=%async_computation.6 | async-start | bytes 32768 | tf_op jit(solution)/shard_map/all_to_all | solution.py:29
  171.1 0.6 copy-start.10
  171.7 12.1 %copy-start.4 = (f32[22,128]{1,0:T(8,128)S(1)}, f32[22,128]{1,0:T(8,128)}, u32[]{:S(2)}) copy-start(f32[22,128]{1,0:T(8,128)} %copy-done.3) | copy-start | bytes 33796
  177.1 21.3 %all-to-all-start.7 = ((f32[32,8,384]{2,1,0:T(8,128)}), f32[32,8,384]{2,1,0:T(8,128)S(1)}, u32[]{:S(2)}, u32[]{:S(2)}) async-start(f32[32,8,384]{2,1,0:T(8,128)} %shard_map.68), calls=%async_computation.7 | async-start | bytes 786432 | tf_op jit(solution)/shard_map/all_to_all | solution.py:289

commit v5 on v4

v5 whole, which is shorter than its diff:
```python
import functools

import jax
import jax.numpy as jnp
from jax import lax
from jax.experimental import pallas as pl
from jax.experimental.pallas import tpu as pltpu
from jax.sharding import PartitionSpec as P

ITERS = 3
SMALL, PASSING, VMEM = 16 * 2**20, 121 * 2**19, 61 * 2**20
LANES = 128
HELD = 6
TEAM = 4


teacher_temp = 0.04
student_temp = 0.1
eps = 1e-06


def unit_rows(x):
    xf = x.astype(jnp.float32)
    return (xf * lax.rsqrt(jnp.sum(xf * xf, 1, keepdims=True) + eps)).astype(jnp.bfloat16)


def first_group(groups):
    return jnp.minimum(lax.axis_index("batch") % TEAM * HELD, groups - HELD)


def grad_kernel(count, scale, expo_ref, student_exp_ref, student_ref, u_ref, rows_ref, out_ref, acc, diff):
    step = pl.program_id(0)
    rows = rows_ref.shape[2]
    crops = diff.shape[1]

    me = lax.axis_index("batch") % TEAM
    for s in range(crops // rows):
        place = step * (crops // rows) + s
        by = rows_ref[me ^ place]
        for start in range(0, rows, LANES):
            v = count * by[0:1, start : start + LANES]
            inv_total = count * by[1:2, start : start + LANES]
            span = slice(s * rows + start, s * rows + start + LANES)
            for g in range(HELD):
                part = slice(g * LANES, (g + 1) * LANES)
                assign = expo_ref[part, span].astype(jnp.float32) * u_ref[part, :] * v
                prob = student_exp_ref[part, span] * inv_total
                diff[part, span] = (prob - assign).astype(jnp.bfloat16)
    product = jnp.dot(diff[...], student_ref[...], preferred_element_type=jnp.float32)

    @pl.when(step == 0)
    def _():
        acc[...] = product

    @pl.when(step > 0)
    def _():
        acc[...] += product

    @pl.when(step == pl.num_programs(0) - 1)
    def _():
        out_ref[...] = (acc[...].T * scale).reshape(out_ref.shape)


def partial_grad(expo_t, student_exp_t, student, u, by_sender, count, scale, owners):
    part, crops = expo_t.shape
    depth = student.shape[1]
    senders, _, rows = by_sender.shape
    steps = 4
    chunk = crops // steps
    return pl.pallas_call(
        functools.partial(grad_kernel, count, scale),
        grid=(steps,),
        in_specs=[
            pl.BlockSpec((part, chunk), lambda i: (0, i)),
            pl.BlockSpec((part, chunk), lambda i: (0, i)),
            pl.BlockSpec((chunk, depth), lambda i: (i, 0)),
            pl.BlockSpec(u.shape, lambda i: (0, 0)),
            pl.BlockSpec(by_sender.shape, lambda i: (0, 0, 0)),
        ],
        out_specs=pl.BlockSpec((owners, depth // owners, part), lambda i: (0, 0, 0)),
        out_shape=jax.ShapeDtypeStruct((owners, depth // owners, part), jnp.float32),
        scratch_shapes=[
            pltpu.VMEM((part, depth), jnp.float32),
            pltpu.VMEM((part, chunk), jnp.bfloat16),
        ],
        compiler_params=pltpu.CompilerParams(vmem_limit_bytes=VMEM),
        cost_estimate=pl.CostEstimate(
            flops=2 * part * crops * depth, bytes_accessed=6 * part * crops, transcendentals=0
        ),
    )(expo_t, student_exp_t, student, u, by_sender)


def join_kernel(parts_ref, out_ref):
    teams = parts_ref.shape[0] // TEAM
    groups = out_ref.shape[1] // LANES
    for i in range(TEAM):
        start = min(i * HELD, groups - HELD) * LANES
        total = parts_ref[i]
        for t in range(1, teams):
            total += parts_ref[t * TEAM + i]
        out_ref[:, start : start + HELD * LANES] = total


def start_kernel(teacher_ref, student_ref, proto_ref, gain_ref, mine_ref, proto_n_ref, expo_ref, sent_ref):
    t = teacher_ref[...].astype(jnp.float32)
    first = lax.axis_index("proto") % 2 == 0
    mine_ref[0] = jnp.where(first, t, student_ref[...].astype(jnp.float32))
    t = (t * lax.rsqrt(jnp.sum(t * t, 1, keepdims=True) + eps)).astype(jnp.bfloat16)
    peers, groups, _ = sent_ref.shape
    for j in range(0, groups, 2):
        span = slice(j * LANES, (j + 2) * LANES)
        w = proto_ref[:, span].astype(jnp.float32)
        gains = jnp.concatenate([gain_ref[j : j + 1, :], gain_ref[j + 1 : j + 2, :]], 1)
        w = (w * lax.rsqrt(jnp.sum(w * w, 0, keepdims=True) + eps) * gains).astype(jnp.bfloat16)
        proto_n_ref[:, span] = w
        e = jnp.exp(jnp.dot(t, w, preferred_element_type=jnp.float32) / teacher_temp)
        e = e.astype(jnp.bfloat16)
        expo_ref[:, span] = e
        c = jnp.sum(e.astype(jnp.float32), 0, keepdims=True)
        sent_ref[0, j : j + 1, :] = c[:, :LANES]
        sent_ref[0, j + 1 : j + 2, :] = c[:, LANES:]
    sent_ref[1:] = jnp.broadcast_to(sent_ref[0:1], (peers - 1, groups, LANES))


def start(teacher, student, prototypes, gain, peers):
    rows, depth = teacher.shape
    cols = prototypes.shape[1]
    groups = cols // LANES
    return pl.pallas_call(
        start_kernel,
        out_shape=(
            jax.ShapeDtypeStruct((1, rows, depth), jnp.float32),
            jax.ShapeDtypeStruct((depth, cols), jnp.bfloat16),
            jax.ShapeDtypeStruct((rows, cols), jnp.bfloat16),
            jax.ShapeDtypeStruct((peers, groups, LANES), jnp.float32),
        ),
        compiler_params=pltpu.CompilerParams(vmem_limit_bytes=VMEM),
        cost_estimate=pl.CostEstimate(
            flops=2 * rows * depth * cols, bytes_accessed=6 * depth * cols, transcendentals=rows * cols
        ),
    )(teacher, student, prototypes, gain.reshape(groups, LANES))


def local_call(kernel, operands, waited, out_shape, flops):
    n = len(operands)

    def body(*refs):
        kernel(*refs[:n], *refs[n + len(waited) :])

    return pl.pallas_call(
        body,
        in_specs=[pl.BlockSpec()] * n + [pl.BlockSpec(memory_space=pl.ANY)] * len(waited),
        out_shape=out_shape,
        compiler_params=pltpu.CompilerParams(vmem_limit_bytes=SMALL),
        cost_estimate=pl.CostEstimate(flops=flops, bytes_accessed=flops, transcendentals=0),
    )(*operands, *waited)


def row_kernel(came_ref, expo_ref, *refs):
    total_ref, (sent_ref, u_ref) = (refs[0] if len(refs) == 3 else None), refs[-2:]
    u_ref[...] = 1.0 / jnp.sum(came_ref[...], 0)
    rows = expo_ref.shape[0]
    block = 64
    sums = []
    for first in range(0, rows, block):
        acc = jnp.zeros((block, LANES), jnp.float32)
        for j in range(u_ref.shape[0]):
            e = expo_ref[first : first + block, j * LANES : (j + 1) * LANES].astype(jnp.float32)
            acc += e * u_ref[j : j + 1, :]
        sums.append(acc)
    r = jnp.sum(jnp.concatenate(sums, 0).T, 0, keepdims=True)
    peers = sent_ref.shape[0]
    sent_ref[:, 0:1, :] = jnp.broadcast_to(r[None], (peers, 1, rows))
    if total_ref is not None:
        sent_ref[:, 1:2, :] = jnp.broadcast_to(total_ref[...][None], (peers, 1, rows))


def row_terms(came, expo, peers, *waited, total=None):
    more = () if total is None else (total,)
    rows = expo.shape[0]
    out_shape = (
        jax.ShapeDtypeStruct((peers, 1 + len(more), rows), jnp.float32),
        jax.ShapeDtypeStruct(came.shape[1:], jnp.float32),
    )
    return local_call(row_kernel, (came, expo, *more), waited, out_shape, 2 * expo.size)


def column_kernel(came_ref, expo_ref, sent_ref):
    rows = expo_ref.shape[0]
    v = 1.0 / jnp.sum(came_ref[...], 0)
    v = jnp.broadcast_to(v, (LANES, rows)).T
    peers, groups, _ = sent_ref.shape
    for j in range(groups):
        e = expo_ref[:, j * LANES : (j + 1) * LANES].astype(jnp.float32)
        sent_ref[0, j : j + 1, :] = jnp.sum(e * v, 0, keepdims=True)
    sent_ref[1:] = jnp.broadcast_to(sent_ref[0:1], (peers - 1, groups, LANES))


def column_terms(came, expo, peers, *waited):
    out_shape = jax.ShapeDtypeStruct((peers, expo.shape[1] // LANES, LANES), jnp.float32)
    return local_call(column_kernel, (came, expo), waited, out_shape, 2 * expo.size)


def team_rows_kernel(came_ref, sent_ref, own_ref):
    own_ref[...] = 1.0 / jnp.sum(came_ref[...], 0)
    sent_ref[...] = jnp.broadcast_to(own_ref[...][None], sent_ref.shape)


def team_rows(came, *waited):
    out_shape = (
        jax.ShapeDtypeStruct((TEAM,) + came.shape[1:], jnp.float32),
        jax.ShapeDtypeStruct(came.shape[1:], jnp.float32),
    )
    return local_call(team_rows_kernel, (came,), waited, out_shape, came.size)


def after(value, other):
    return pl.pallas_call(
        lambda value_ref, other_ref, out_ref: None,
        in_specs=[pl.BlockSpec(memory_space=pl.ANY)] * 2,
        out_specs=pl.BlockSpec(memory_space=pl.ANY),
        out_shape=jax.ShapeDtypeStruct(value.shape, value.dtype),
        input_output_aliases={0: 0},
        compiler_params=pltpu.CompilerParams(vmem_limit_bytes=VMEM),
    )(value, other)


def team_kernel(own_ref, other_ref, proto_ref, u_ref, after_ref, expo_ref, student_exp_ref, student_ref, u_wide_ref, done_ref, proto_t):
    @pl.when(pl.program_id(0) == 0)
    def _():
        start = pl.multiple_of(first_group(proto_ref.shape[1] // LANES) * LANES, LANES)
        proto_t[...] = proto_ref[:, pl.ds(start, HELD * LANES)].astype(jnp.float32).T.astype(jnp.bfloat16)
        u = u_ref[pl.ds(first_group(u_ref.shape[0]), HELD), :]
        for g in range(HELD):
            wide = jnp.broadcast_to(u[g : g + 1, :], (LANES, LANES)).T
            u_wide_ref[g * LANES : (g + 1) * LANES, :] = wide
        done_ref[...] = jnp.zeros_like(done_ref)

    def unit(x):
        return (x * lax.rsqrt(jnp.sum(x * x, 1, keepdims=True) + eps)).astype(jnp.bfloat16)

    across = (((1,), (1,)), ((), ()))
    first = lax.axis_index("proto") % 2 == 0
    proto = proto_t[...]
    t = unit(jnp.where(first, own_ref[0], other_ref[0]))
    s = unit(jnp.where(first, other_ref[0], own_ref[0]))
    student_ref[...] = s
    lt = lax.dot_general(proto, t, across, preferred_element_type=jnp.float32)
    expo_ref[...] = jnp.exp(lt / teacher_temp).astype(jnp.bfloat16)
    ls = lax.dot_general(proto, s, across, preferred_element_type=jnp.float32)
    student_exp_ref[...] = jnp.exp(ls / student_temp)


def team_products(own, other, proto, u, waited):
    senders, rows, depth = own.shape
    part = HELD * LANES
    return pl.pallas_call(
        team_kernel,
        grid=(senders,),
        in_specs=[
            pl.BlockSpec((1, rows, depth), lambda i: (i, 0, 0)),
            pl.BlockSpec((1, rows, depth), lambda i: (i, 0, 0)),
            pl.BlockSpec(proto.shape, lambda i: (0, 0)),
            pl.BlockSpec(u.shape, lambda i: (0, 0)),
            pl.BlockSpec(memory_space=pl.ANY),
        ],
        out_specs=[
            pl.BlockSpec((part, rows), lambda i: (0, i)),
            pl.BlockSpec((part, rows), lambda i: (0, i)),
            pl.BlockSpec((rows, depth), lambda i: (i, 0)),
            pl.BlockSpec((part, LANES), lambda i: (0, 0)),
            pl.BlockSpec((8, LANES), lambda i: (0, 0)),
        ],
        out_shape=(
            jax.ShapeDtypeStruct((part, senders * rows), jnp.bfloat16),
            jax.ShapeDtypeStruct((part, senders * rows), jnp.float32),
            jax.ShapeDtypeStruct((senders * rows, depth), jnp.bfloat16),
            jax.ShapeDtypeStruct((part, LANES), jnp.float32),
            jax.ShapeDtypeStruct((8, LANES), jnp.float32),
        ),
        scratch_shapes=[pltpu.VMEM((part, depth), jnp.bfloat16)],
        compiler_params=pltpu.CompilerParams(vmem_limit_bytes=VMEM),
        cost_estimate=pl.CostEstimate(
            flops=4 * part * senders * rows * depth,
            bytes_accessed=10 * 2**20,
            transcendentals=2 * part * senders * rows,
        ),
    )(own, other, proto, u, waited)


def local(teacher, student, prototypes, gain):
    rows, depth = teacher.shape
    nb, npr = lax.axis_size("batch"), lax.axis_size("proto")
    teams = [[t * TEAM + i for i in range(TEAM)] for t in range(nb // TEAM)]
    cols = prototypes.shape[1]
    count = cols * npr
    rows_all = rows * nb

    mine, proto_n, expo, sent = start(teacher, student, prototypes, gain, nb)

    def member(rows, flip):
        return lax.ppermute(rows, "batch", [(i, i ^ flip) for i in range(nb)])

    held = [mine, member(mine, 1), None, member(mine, 3)]
    came = lax.all_to_all(sent, "batch", 0, 0, tiled=True)
    sent, _ = row_terms(came, expo, npr, held[1], held[3])
    came = lax.all_to_all(sent, "proto", 0, 0, tiled=True)
    sent = column_terms(came, expo, nb)
    held[2] = member(after(mine, sent), 2)
    came = lax.all_to_all(sent, "batch", 0, 0, tiled=True)
    sent, _ = row_terms(came, expo, npr, held[2])
    own = jnp.concatenate(held)
    came = lax.all_to_all(sent, "proto", 0, 0, tiled=True)
    sent = column_terms(came, expo, nb)
    other = lax.ppermute(own, "proto", [(i, i ^ 1) for i in range(npr)])
    came = lax.all_to_all(sent, "batch", 0, 0, tiled=True)

    logits = jnp.dot(unit_rows(student), proto_n, preferred_element_type=jnp.float32)
    local_total = jnp.sum(jnp.exp(logits / student_temp), 1)
    sent, scale_u = row_terms(came, expo, npr, other, total=local_total[None])
    came = lax.all_to_all(sent, "proto", 0, 0, tiled=True)
    *team_values, done = team_products(own, other, proto_n, scale_u, sent)
    sent, inverse = team_rows(came, done)
    scale_v = inverse[0]
    by_sender = lax.all_to_all(sent, "batch", 0, 0, tiled=True, axis_index_groups=teams)

    inv_root = 1.0 / rows_all**0.5
    grad_t = partial_grad(*team_values, by_sender, float(count), inv_root, nb)
    parts = lax.all_to_all(grad_t, "batch", 0, 0, tiled=True)
    grad = pl.pallas_call(
        join_kernel,
        out_shape=jax.ShapeDtypeStruct((depth // nb, cols), jnp.float32),
        compiler_params=pltpu.CompilerParams(vmem_limit_bytes=SMALL),
    )(parts)

    scale_u = scale_u.reshape(cols)
    assign = expo.astype(jnp.float32) * scale_u[None, :] * scale_v[:, None]
    targets = (count * assign).astype(jnp.bfloat16)
    return (targets, grad)


def solution(mesh):
    return jax.shard_map(
        local,
        mesh=mesh,
        in_specs=(P("batch", None), P("batch", None), P(None, "proto"), P("proto")),
        out_specs=(P("batch", "proto"), P("batch", "proto")),
        check_vma=False,
    )
```

time: 200 us -> 180 us (0.900)
  the two profiles are of different devices: /device:TPU:8 before, /device:TPU:2 now
where the time goes in v5:
time: 180 us; the launch traced here: 179 us
  starting transfers between devices  64.2 us (36%)
  waiting for transfers between devices  61.1 us (34%)
  blocking collectives  21.4 us (12%)
  Pallas kernels  21.1 us (12%)
  local copies, waits for them, and re-layouts  6.29 us (3%)
  matrix products  2.04 us (1%)
    all_to_all x3, starting transfers between devices, local(): came = lax.all_to_all(sent, 'batch', 0, 0, tiled=True)  27.7 us
    all_to_all x3, waiting for transfers between devices, local(): came = lax.all_to_all(sent, 'batch', 0, 0, tiled=True)  22 us
    all_to_all x1, waiting for transfers between devices, local(): parts = lax.all_to_all(grad_t, 'batch', 0, 0, tiled=True)  20.1 us
    all_to_all x2, starting transfers between devices, local(): came = lax.all_to_all(sent, 'proto', 0, 0, tiled=True)  19 us
    all_to_all x2, waiting for transfers between devices, local(): came = lax.all_to_all(sent, 'proto', 0, 0, tiled=True)  13.4 us
    all_to_all x1, blocking collectives, local(): came = lax.all_to_all(sent, 'proto', 0, 0, tiled=True)  12.8 us
    ppermute x3, starting transfers between devices, member(): return lax.ppermute(rows, 'batch', [(i, i ^ flip) for i in range(nb)])  10.5 us
    all_to_all x1, blocking collectives, local(): lax.all_to_all(sent, 'batch', 0, 0, tiled=True, axis_index_groups=teams)  8.55 us
  transfers between devices with their start and end apart: 10, of which 7 were waited for; matrix products, arithmetic and copies ran while one was open for 4% of the time, Pallas kernels for 5%

profile of v5, /device:TPU:2, one launch (start us, length us, event | category | flops | bytes accessed | tf_op | source)
XLA Modules:
  0.0 178.6 jit_solution(14943049000100947820)
XLA Ops:
  0.6 4.3 %shard_map.59 = (f32[1,256,256]{2,1,0:T(8,128)}, bf16[256,2816]{1,0:T(8,128)(2,1)}, bf16[256,2816]{1,0:T(8,128)(2,1)}, f32[32,22,128]{2,1,0:T(8,128)}) custom-call(bf16[256,256]{1,0:T(8,128)(2,1)} %teacher_ref.1, bf16[256,256]{1,0:T(8,128)(2,1)} %student_ref.1, bf16[256,2816]{1,0:T(8,128)(2,1)} %proto_ref.1, f32[22,128]{1,0:T(8,128)} %bitcast.7), custom_call_target="tpu_custom_call" | custom-call | flops 369098752 | bytes 4325376 | tf_op jit(solution)/shard_map/pallas_call | solution.py:129
  4.9 13.2 %all-to-all-start = ((f32[32,22,128]{2,1,0:T(8,128)}), f32[32,22,128]{2,1,0:T(8,128)S(1)}, u32[]{:S(2)}, u32[]{:S(2)}) async-start(f32[32,22,128]{2,1,0:T(8,128)} %get-tuple-element.18), calls=%async_computation | async-start | bytes 786432 | tf_op jit(solution)/shard_map/all_to_all | solution.py:305
  18.1 2.3 %collective-permute-start = (f32[1,256,256]{2,1,0:T(8,128)}, f32[1,256,256]{2,1,0:T(8,128)S(1)}, u32[]{:S(2)}, u32[]{:S(2)}) collective-permute-start(f32[1,256,256]{2,1,0:T(8,128)} %get-tuple-element.19.value_ref), channel_id=1, source_target_pairs={{0,1},{1,0},{2,3},{3,2},{4,5},{5,4},{6,7},{7,6},{8,9},{9,8},{10,11... | collective-permute-start | bytes 786440 | tf_op jit(solution)/shard_map/ppermute | solution.py:302
  20.4 4.2 %collective-permute-start.1 = (f32[1,256,256]{2,1,0:T(8,128)}, f32[1,256,256]{2,1,0:T(8,128)S(1)}, u32[]{:S(2)}, u32[]{:S(2)}) collective-permute-start(f32[1,256,256]{2,1,0:T(8,128)} %get-tuple-element.19.value_ref), channel_id=1, source_target_pairs={{0,3},{1,2},{2,1},{3,0},{4,7},{5,6},{6,5},{7,4},{8,11},{9,10},{10,... | collective-permute-start | bytes 786440 | tf_op jit(solution)/shard_map/ppermute | solution.py:302
  24.6 3.6 %collective-permute-done.refs_2_ = f32[1,256,256]{2,1,0:T(8,128)S(1)} collective-permute-done((f32[1,256,256]{2,1,0:T(8,128)}, f32[1,256,256]{2,1,0:T(8,128)S(1)}, u32[]{:S(2)}, u32[]{:S(2)}) %collective-permute-start) | collective-permute-done | bytes 262176 | tf_op jit(solution)/shard_map/ppermute | solution.py:302
  28.2 2.0 %collective-permute-done.1.refs_3_ = f32[1,256,256]{2,1,0:T(8,128)S(1)} collective-permute-done((f32[1,256,256]{2,1,0:T(8,128)}, f32[1,256,256]{2,1,0:T(8,128)S(1)}, u32[]{:S(2)}, u32[]{:S(2)}) %collective-permute-start.1) | collective-permute-done | bytes 262176 | tf_op jit(solution)/shard_map/ppermute | solution.py:302
  32.5 15.2 %all-to-all-start.1 = ((f32[24,1,256]{2,1,0:T(1,128)}), f32[24,1,256]{2,1,0:T(1,128)S(1)}, u32[]{:S(2)}, u32[]{:S(2)}) async-start(f32[24,1,256]{2,1,0:T(1,128)} %get-tuple-element.20), calls=%async_computation.1 | async-start | bytes 49152 | tf_op jit(solution)/shard_map/all_to_all | solution.py:307
  48.5 9.3 %all-to-all-done.1.refs_0_ = f32[24,1,256]{2,1,0:T(1,128)S(1)} async-done(((f32[24,1,256]{2,1,0:T(1,128)}), f32[24,1,256]{2,1,0:T(1,128)S(1)}, u32[]{:S(2)}, u32[]{:S(2)}) %all-to-all-start.1) | async-done | bytes 24608 | tf_op jit(solution)/shard_map/all_to_all | solution.py:307
  58.9 4.1 %collective-permute-start.2 = (f32[1,256,256]{2,1,0:T(8,128)}, f32[1,256,256]{2,1,0:T(8,128)S(1)}, u32[]{:S(2)}, u32[]{:S(2)}) collective-permute-start(f32[1,256,256]{2,1,0:T(8,128)} %shard_map.62), channel_id=1, source_target_pairs={{0,2},{1,3},{2,0},{3,1},{4,6},{5,7},{6,4},{7,5},{8,10},{9,11},{10,... | collective-permute-start | bytes 786440 | tf_op jit(solution)/shard_map/ppermute | solution.py:302
  63.0 8.9 %all-to-all-start.2 = ((f32[32,22,128]{2,1,0:T(8,128)}), f32[32,22,128]{2,1,0:T(8,128)S(1)}, u32[]{:S(2)}, u32[]{:S(2)}) async-start(f32[32,22,128]{2,1,0:T(8,128)} %copy-done.3), calls=%async_computation.2 | async-start | bytes 786432 | tf_op jit(solution)/shard_map/all_to_all | solution.py:310
  74.1 1.9 %collective-permute-start.3 = (f32[4,256,256]{2,1,0:T(8,128)}, f32[4,256,256]{2,1,0:T(8,128)S(1)}, u32[]{:S(2)}, u32[]{:S(2)}) collective-permute-start(f32[4,256,256]{2,1,0:T(8,128)} %constant_dynamic-update-slice_fusion.own_ref), channel_id=1, source_target_pairs={{0,32},{32,0},{64,96},{96,64},{128,160},{160,128},{192,224},{224,1... | collective-permute-start | bytes 3145736 | tf_op jit(solution)/shard_map/ppermute | solution.py:315
  76.0 9.9 %all-to-all-done.2.refs_0_ = f32[32,22,128]{2,1,0:T(8,128)S(1)} async-done(((f32[32,22,128]{2,1,0:T(8,128)}), f32[32,22,128]{2,1,0:T(8,128)S(1)}, u32[]{:S(2)}, u32[]{:S(2)}) %all-to-all-start.2) | async-done | bytes 360480 | tf_op jit(solution)/shard_map/all_to_all | solution.py:310
  86.8 12.8 %all_to_all.40.refs_0_ = f32[24,1,256]{2,1,0:T(1,128)S(1)} all-to-all(f32[24,1,256]{2,1,0:T(1,128)S(1)} %get-tuple-element.21), channel_id=1, replica_groups=mesh['proto'=24,'batch'=32] {'proto'}, dimensions={0} | all-to-all | bytes 49152 | tf_op jit(solution)/shard_map/all_to_all | solution.py:313
  100.9 5.6 %all-to-all-start.4 = ((f32[32,22,128]{2,1,0:T(8,128)}), f32[32,22,128]{2,1,0:T(8,128)S(1)}, u32[]{:S(2)}, u32[]{:S(2)}) async-start(f32[32,22,128]{2,1,0:T(8,128)} %shard_map.64), calls=%async_computation.4 | async-start | bytes 786432 | tf_op jit(solution)/shard_map/all_to_all | solution.py:316
  106.6 2.0 %fusion.1 = f32[256]{0:T(256)S(1)} fusion(bf16[256,2816]{1,0:T(8,128)(2,1)} %get-tuple-element.22.proto_ref, bf16[256,256]{1,0:T(8,128)(2,1)S(1)} %copy-done.8, f32[256]{0:T(256)S(1)} %add_rsqrt_fusion), kind=kOutput, calls=%fused_computation.3 | convolution fusion | flops 370736896 | bytes 1574912 | tf_op jit(solution)/shard_map/dot_general | solution.py:318
  108.6 12.1 %all-to-all-done.4.refs_0_ = f32[32,22,128]{2,1,0:T(8,128)S(1)} async-done(((f32[32,22,128]{2,1,0:T(8,128)}), f32[32,22,128]{2,1,0:T(8,128)S(1)}, u32[]{:S(2)}, u32[]{:S(2)}) %all-to-all-start.4) | async-done | bytes 360480 | tf_op jit(solution)/shard_map/all_to_all | solution.py:316
  122.4 3.8 %all-to-all-start.5 = ((f32[24,2,256]{2,1,0:T(2,128)}), f32[24,2,256]{2,1,0:T(2,128)S(1)}, u32[]{:S(2)}, u32[]{:S(2)}) async-start(f32[24,2,256]{2,1,0:T(2,128)} %get-tuple-element.24.after_ref), calls=%async_computation.5 | async-start | bytes 98304 | tf_op jit(solution)/shard_map/all_to_all | solution.py:321
  126.2 6.1 %shard_map.66 = (bf16[768,1024]{1,0:T(8,128)(2,1)}, f32[768,1024]{1,0:T(8,128)}, bf16[1024,256]{1,0:T(8,128)(2,1)}, f32[768,128]{1,0:T(8,128)}, f32[8,128]{1,0:T(8,128)}) custom-call(f32[4,256,256]{2,1,0:T(8,128)} %constant_dynamic-update-slice_fusion.own_ref, f32[4,256,256]{2,1,0:T(8,128)} %copy-done.2, bf16[256,2816]{1,0:T(8,128)(2,1)} %get-tuple-element.22.proto_ref, ...), custom_call_target="tpu_custom_call" | custom-call | flops 805306368 | bytes 10485760 | tf_op jit(solution)/shard_map/pallas_call | solution.py:257
  132.3 4.2 %all-to-all-done.5.refs_0_ = f32[24,2,256]{2,1,0:T(2,128)S(1)} async-done(((f32[24,2,256]{2,1,0:T(2,128)}), f32[24,2,256]{2,1,0:T(2,128)S(1)}, u32[]{:S(2)}, u32[]{:S(2)}) %all-to-all-start.5) | async-done | bytes 49184 | tf_op jit(solution)/shard_map/all_to_all | solution.py:321
  137.2 8.6 %all_to_all.41.rows_ref = f32[4,2,256]{2,1,0:T(2,128)} all-to-all(f32[4,2,256]{2,1,0:T(2,128)S(1)} %get-tuple-element.31), channel_id=1, replica_groups={{0,1,2,3},{4,5,6,7},{8,9,10,11},{12,13,14,15},{16,17,18,19},{20,21,22,2..., dimensions={0} | all-to-all | bytes 16384 | tf_op jit(solution)/shard_map/all_to_all | solution.py:325
  145.8 5.5 %shard_map.68 = f32[32,8,768]{2,1,0:T(8,128)} custom-call(bf16[768,1024]{1,0:T(8,128)(2,1)} %get-tuple-element.27.expo_ref, f32[768,1024]{1,0:T(8,128)} %get-tuple-element.28.student_exp_ref, bf16[1024,256]{1,0:T(8,128)(2,1)} %get-tuple-element.29.student_ref, f32[768,128]{1,0:T(8,128)} %get-tuple-element.30.u_ref, f32[4,2,256]{2,1,0:T(2,128)} %all_to_all.41.rows_ref), custom_call_target="tpu_custom_call" | custom-call | flops 402653184 | bytes 4718592 | tf_op jit(solution)/shard_map/pallas_call | solution.py:70
  151.3 5.0 %all-to-all-start.7 = ((f32[32,8,768]{2,1,0:T(8,128)}), f32[32,8,768]{2,1,0:T(8,128)S(1)}, u32[]{:S(2)}, u32[]{:S(2)}) async-start(f32[32,8,768]{2,1,0:T(8,128)} %shard_map.68), calls=%async_computation.7 | async-start | bytes 1572864 | tf_op jit(solution)/shard_map/all_to_all | solution.py:329
  156.4 1.5 multiply_convert_fusion
  157.9 20.1 %all-to-all-done.7.parts_ref = f32[32,8,768]{2,1,0:T(8,128)S(1)} async-done(((f32[32,8,768]{2,1,0:T(8,128)}), f32[32,8,768]{2,1,0:T(8,128)S(1)}, u32[]{:S(2)}, u32[]{:S(2)}) %all-to-all-start.7) | async-done | bytes 786464 | tf_op jit(solution)/shard_map/all_to_all | solution.py:329
  (36 shorter events, 11.7 us)
Async XLA Ops:
  4.9 42.9 %copy-start.7 = (f32[1,256,256]{2,1,0:T(8,128)S(1)}, f32[1,256,256]{2,1,0:T(8,128)}, u32[]{:S(2)}) copy-start(f32[1,256,256]{2,1,0:T(8,128)} %get-tuple-element.19.value_ref) | copy-start | bytes 786436
  4.9 25.3 %all-to-all-start = ((f32[32,22,128]{2,1,0:T(8,128)}), f32[32,22,128]{2,1,0:T(8,128)S(1)}, u32[]{:S(2)}, u32[]{:S(2)}) async-start(f32[32,22,128]{2,1,0:T(8,128)} %get-tuple-element.18), calls=%async_computation | async-start | bytes 786432 | tf_op jit(solution)/shard_map/all_to_all | solution.py:305
  18.1 10.1 %collective-permute-start = (f32[1,256,256]{2,1,0:T(8,128)}, f32[1,256,256]{2,1,0:T(8,128)S(1)}, u32[]{:S(2)}, u32[]{:S(2)}) collective-permute-start(f32[1,256,256]{2,1,0:T(8,128)} %get-tuple-element.19.value_ref), channel_id=1, source_target_pairs={{0,1},{1,0},{2,3},{3,2},{4,5},{5,4},{6,7},{7,6},{8,9},{9,8},{10,11... | collective-permute-start | bytes 786440 | tf_op jit(solution)/shard_map/ppermute | solution.py:302
  20.4 9.8 %collective-permute-start.1 = (f32[1,256,256]{2,1,0:T(8,128)}, f32[1,256,256]{2,1,0:T(8,128)S(1)}, u32[]{:S(2)}, u32[]{:S(2)}) collective-permute-start(f32[1,256,256]{2,1,0:T(8,128)} %get-tuple-element.19.value_ref), channel_id=1, source_target_pairs={{0,3},{1,2},{2,1},{3,0},{4,7},{5,6},{6,5},{7,4},{8,11},{9,10},{10,... | collective-permute-start | bytes 786440 | tf_op jit(solution)/shard_map/ppermute | solution.py:302
  30.1 1.4 copy-start
  31.5 26.2 %copy-start.1 = (bf16[256,2816]{1,0:T(8,128)(2,1)S(1)}, bf16[256,2816]{1,0:T(8,128)(2,1)}, u32[]{:S(2)}) copy-start(bf16[256,2816]{1,0:T(8,128)(2,1)} %get-tuple-element.17.refs_1_) | copy-start | bytes 4325380
  32.5 25.2 %all-to-all-start.1 = ((f32[24,1,256]{2,1,0:T(1,128)}), f32[24,1,256]{2,1,0:T(1,128)S(1)}, u32[]{:S(2)}, u32[]{:S(2)}) async-start(f32[24,1,256]{2,1,0:T(1,128)} %get-tuple-element.20), calls=%async_computation.1 | async-start | bytes 49152 | tf_op jit(solution)/shard_map/all_to_all | solution.py:307
  58.2 0.7 copy-start.3
  58.9 13.7 %collective-permute-start.2 = (f32[1,256,256]{2,1,0:T(8,128)}, f32[1,256,256]{2,1,0:T(8,128)S(1)}, u32[]{:S(2)}, u32[]{:S(2)}) collective-permute-start(f32[1,256,256]{2,1,0:T(8,128)} %shard_map.62), channel_id=1, source_target_pairs={{0,2},{1,3},{2,0},{3,1},{4,6},{5,7},{6,4},{7,5},{8,10},{9,11},{10,... | collective-permute-start | bytes 786440 | tf_op jit(solution)/shard_map/ppermute | solution.py:302
  63.0 22.9 %all-to-all-start.2 = ((f32[32,22,128]{2,1,0:T(8,128)}), f32[32,22,128]{2,1,0:T(8,128)S(1)}, u32[]{:S(2)}, u32[]{:S(2)}) async-start(f32[32,22,128]{2,1,0:T(8,128)} %copy-done.3), calls=%async_computation.2 | async-start | bytes 786432 | tf_op jit(solution)/shard_map/all_to_all | solution.py:310
  72.6 33.8 %copy-start.8 = (bf16[256,256]{1,0:T(8,128)(2,1)S(1)}, bf16[256,256]{1,0:T(8,128)(2,1)}, u32[]{:S(2)}) copy-start(bf16[256,256]{1,0:T(8,128)(2,1)} %student_ref.1) | copy-start | bytes 393220
  74.1 34.5 %collective-permute-start.3 = (f32[4,256,256]{2,1,0:T(8,128)}, f32[4,256,256]{2,1,0:T(8,128)S(1)}, u32[]{:S(2)}, u32[]{:S(2)}) collective-permute-start(f32[4,256,256]{2,1,0:T(8,128)} %constant_dynamic-update-slice_fusion.own_ref), channel_id=1, source_target_pairs={{0,32},{32,0},{64,96},{96,64},{128,160},{160,128},{192,224},{224,1... | collective-permute-start | bytes 3145736 | tf_op jit(solution)/shard_map/ppermute | solution.py:315
  100.9 19.9 %all-to-all-start.4 = ((f32[32,22,128]{2,1,0:T(8,128)}), f32[32,22,128]{2,1,0:T(8,128)S(1)}, u32[]{:S(2)}, u32[]{:S(2)}) async-start(f32[32,22,128]{2,1,0:T(8,128)} %shard_map.64), calls=%async_computation.4 | async-start | bytes 786432 | tf_op jit(solution)/shard_map/all_to_all | solution.py:316
  108.6 17.6 %copy-start.2 = (f32[4,256,256]{2,1,0:T(8,128)}, f32[4,256,256]{2,1,0:T(8,128)S(1)}, u32[]{:S(2)}) copy-start(f32[4,256,256]{2,1,0:T(8,128)S(1)} %collective-permute-done.3.refs_3_.other_ref) | copy-start | bytes 3145732
  121.8 0.6 copy-start.4
  122.4 14.1 %all-to-all-start.5 = ((f32[24,2,256]{2,1,0:T(2,128)}), f32[24,2,256]{2,1,0:T(2,128)S(1)}, u32[]{:S(2)}, u32[]{:S(2)}) async-start(f32[24,2,256]{2,1,0:T(2,128)} %get-tuple-element.24.after_ref), calls=%async_computation.5 | async-start | bytes 98304 | tf_op jit(solution)/shard_map/all_to_all | solution.py:321
  136.5 0.7 copy-start.6
  145.8 10.5 %copy-start.5 = (f32[22,128]{1,0:T(8,128)S(1)}, f32[22,128]{1,0:T(8,128)}, u32[]{:S(2)}) copy-start(f32[22,128]{1,0:T(8,128)} %copy-done.4) | copy-start | bytes 33796
  151.3 26.7 %all-to-all-start.7 = ((f32[32,8,768]{2,1,0:T(8,128)}), f32[32,8,768]{2,1,0:T(8,128)S(1)}, u32[]{:S(2)}, u32[]{:S(2)}) async-start(f32[32,8,768]{2,1,0:T(8,128)} %shard_map.68), calls=%async_computation.7 | async-start | bytes 1572864 | tf_op jit(solution)/shard_map/all_to_all | solution.py:329

commit v6 on v5

v6 whole, which is shorter than its diff:
```python
import functools

import jax
import jax.numpy as jnp
from jax import lax
from jax.experimental import pallas as pl
from jax.experimental.pallas import tpu as pltpu
from jax.sharding import PartitionSpec as P

ITERS = 3
SMALL, VMEM = 16 * 2**20, 61 * 2**20
TEAM_VMEM, GRAD_VMEM = 56 * 2**20, 61 * 2**20
LANES = 128
HELD = 6
SPLIT = 4
HALVES = 2
TEAM = 4


teacher_temp = 0.04
student_temp = 0.1
eps = 1e-06


def unit_rows(x):
    xf = x.astype(jnp.float32)
    return (xf * lax.rsqrt(jnp.sum(xf * xf, 1, keepdims=True) + eps)).astype(jnp.bfloat16)


def first_group(groups):
    return jnp.minimum(lax.axis_index("batch") % TEAM * HELD, groups - HELD)


def grad_kernel(count, scale, *refs):
    exps, student_exps = refs[:SPLIT], refs[SPLIT : 2 * SPLIT]
    student_ref, u_ref, rows_ref, out_ref, diff = refs[2 * SPLIT :]
    rows = rows_ref.shape[2]
    chunk = diff.shape[0]
    piece = chunk // SPLIT
    me = lax.axis_index("batch") % TEAM
    u = u_ref[pl.ds(first_group(u_ref.shape[0]) + pl.program_id(0) * (chunk // LANES), chunk // LANES), :]
    wide = [jnp.broadcast_to(u[g : g + 1, :], (LANES, LANES)).T for g in range(chunk // LANES)]
    wide = jnp.concatenate(wide, 0)
    for place in range(TEAM):
        by = rows_ref[me ^ place] * count
        for first in range(0, rows, LANES):
            v = by[0:1, first : first + LANES]
            inv_total = by[1:2, first : first + LANES]
            span = slice(place * rows + first, place * rows + first + LANES)
            for i in range(SPLIT):
                part = slice(i * piece, (i + 1) * piece)
                assign = exps[i][:, span].astype(jnp.float32) * wide[part, :] * v
                prob = student_exps[i][:, span] * inv_total
                diff[part, span] = (prob - assign).astype(jnp.bfloat16)
    product = jnp.dot(diff[...], student_ref[...], preferred_element_type=jnp.float32)
    out_ref[...] = (product.T * scale).reshape(out_ref.shape)


def partial_grad(expo_t, student_exp_t, student, u, by_sender, count, scale, owners):
    part, crops = expo_t.shape
    depth = student.shape[1]
    steps = 2
    chunk = part // steps
    piece = chunk // SPLIT

    def pieces():
        return [pl.BlockSpec((piece, crops), lambda i, k=k: (i * SPLIT + k, 0)) for k in range(SPLIT)]

    return pl.pallas_call(
        functools.partial(grad_kernel, count, scale),
        grid=(steps,),
        in_specs=[
            *pieces(),
            *pieces(),
            pl.BlockSpec(student.shape, lambda i: (0, 0)),
            pl.BlockSpec(u.shape, lambda i: (0, 0)),
            pl.BlockSpec(by_sender.shape, lambda i: (0, 0, 0)),
        ],
        out_specs=pl.BlockSpec((owners, depth // owners, chunk), lambda i: (0, 0, i)),
        out_shape=jax.ShapeDtypeStruct((owners, depth // owners, part), jnp.float32),
        scratch_shapes=[pltpu.VMEM((chunk, crops), jnp.bfloat16)],
        compiler_params=pltpu.CompilerParams(vmem_limit_bytes=GRAD_VMEM),
        cost_estimate=pl.CostEstimate(
            flops=2 * part * crops * depth, bytes_accessed=6 * part * crops, transcendentals=0
        ),
    )(*[expo_t] * SPLIT, *[student_exp_t] * SPLIT, student, u, by_sender)


def join_kernel(parts_ref, out_ref):
    teams = parts_ref.shape[0] // TEAM
    groups = out_ref.shape[1] // LANES
    for i in range(TEAM):
        start = min(i * HELD, groups - HELD) * LANES
        total = parts_ref[i]
        for t in range(1, teams):
            total += parts_ref[t * TEAM + i]
        out_ref[:, start : start + HELD * LANES] = total


def start_kernel(teacher_ref, student_ref, proto_ref, gain_ref, mine_ref, proto_n_ref, expo_ref, sent_ref, unit, terms):
    step = pl.program_id(0)
    here = proto_ref.shape[1] // LANES

    @pl.when(step == 0)
    def _():
        t = teacher_ref[...].astype(jnp.float32)
        first = lax.axis_index("proto") % 2 == 0
        mine_ref[0] = jnp.where(first, t, student_ref[...].astype(jnp.float32))
        unit[...] = (t * lax.rsqrt(jnp.sum(t * t, 1, keepdims=True) + eps)).astype(jnp.bfloat16)

    for j in range(here):
        span = slice(j * LANES, (j + 1) * LANES)
        w = proto_ref[:, span].astype(jnp.float32)
        gains = gain_ref[pl.ds(step * here + j, 1), :]
        w = (w * lax.rsqrt(jnp.sum(w * w, 0, keepdims=True) + eps) * gains).astype(jnp.bfloat16)
        proto_n_ref[:, span] = w
    e = jnp.exp(jnp.dot(unit[...], proto_n_ref[...], preferred_element_type=jnp.float32) / teacher_temp)
    e = e.astype(jnp.bfloat16)
    cols = proto_ref.shape[1]
    expo_ref[:, pl.ds(pl.multiple_of(step * cols, LANES), cols)] = e
    c = jnp.sum(e.astype(jnp.float32), 0, keepdims=True)
    terms[pl.ds(step, 1), :] = c

    @pl.when(step == pl.num_programs(0) - 1)
    def _():
        sent_ref[...] = jnp.broadcast_to(terms[...][None], sent_ref.shape)


def start(teacher, student, prototypes, gain, peers):
    rows, depth = teacher.shape
    cols = prototypes.shape[1]
    groups = cols // LANES
    steps = HALVES
    chunk = cols // steps
    return pl.pallas_call(
        start_kernel,
        grid=(steps,),
        in_specs=[
            pl.BlockSpec((rows, depth), lambda i: (0, 0)),
            pl.BlockSpec((rows, depth), lambda i: (0, 0)),
            pl.BlockSpec((depth, chunk), lambda i: (0, i)),
            pl.BlockSpec((groups, LANES), lambda i: (0, 0)),
        ],
        out_specs=[
            pl.BlockSpec((1, rows, depth), lambda i: (0, 0, 0)),
            pl.BlockSpec((depth, chunk), lambda i: (0, i)),
            pl.BlockSpec(memory_space=pltpu.VMEM),
            pl.BlockSpec(memory_space=pltpu.VMEM),
        ],
        out_shape=(
            jax.ShapeDtypeStruct((1, rows, depth), jnp.float32),
            jax.ShapeDtypeStruct((depth, cols), jnp.bfloat16),
            pltpu.VMEM((rows, cols), jnp.bfloat16),
            pltpu.VMEM((peers, steps, chunk), jnp.float32),
        ),
        scratch_shapes=[pltpu.VMEM((rows, depth), jnp.bfloat16), pltpu.VMEM((steps, chunk), jnp.float32)],
        compiler_params=pltpu.CompilerParams(vmem_limit_bytes=60 * 2**20),
        cost_estimate=pl.CostEstimate(
            flops=2 * rows * depth * cols, bytes_accessed=6 * depth * cols, transcendentals=rows * cols
        ),
    )(teacher, student, prototypes, gain.reshape(groups, LANES))


def local_call(kernel, operands, waited, out_shape, flops):
    n = len(operands)

    def body(*refs):
        kernel(*refs[:n], *refs[n + len(waited) :])

    return pl.pallas_call(
        body,
        in_specs=[pl.BlockSpec()] * n + [pl.BlockSpec(memory_space=pl.ANY)] * len(waited),
        out_shape=out_shape,
        compiler_params=pltpu.CompilerParams(vmem_limit_bytes=SMALL),
        cost_estimate=pl.CostEstimate(flops=flops, bytes_accessed=flops, transcendentals=0),
    )(*operands, *waited)


def row_kernel(came_ref, expo_ref, *refs):
    total_ref, (sent_ref, u_ref) = (refs[0] if len(refs) == 3 else None), refs[-2:]
    u = 1.0 / jnp.sum(came_ref[...], 0)
    half = u.shape[1] // LANES
    for j in range(u_ref.shape[0]):
        u_ref[j : j + 1, :] = u[j // half : j // half + 1, j % half * LANES : (j % half + 1) * LANES]
    rows = expo_ref.shape[0]
    block = 64
    sums = []
    for first in range(0, rows, block):
        acc = jnp.zeros((block, LANES), jnp.float32)
        for j in range(u_ref.shape[0]):
            e = expo_ref[first : first + block, j * LANES : (j + 1) * LANES].astype(jnp.float32)
            acc += e * u_ref[j : j + 1, :]
        sums.append(acc)
    r = jnp.sum(jnp.concatenate(sums, 0).T, 0, keepdims=True)
    peers = sent_ref.shape[0]
    sent_ref[:, 0:1, :] = jnp.broadcast_to(r[None], (peers, 1, rows))
    if total_ref is not None:
        sent_ref[:, 1:2, :] = jnp.broadcast_to(total_ref[...][None], (peers, 1, rows))


def row_terms(came, expo, peers, *waited, total=None):
    more = () if total is None else (total,)
    rows = expo.shape[0]
    out_shape = (
        jax.ShapeDtypeStruct((peers, 1 + len(more), rows), jnp.float32),
        jax.ShapeDtypeStruct((expo.shape[1] // LANES, LANES), jnp.float32),
    )
    return local_call(row_kernel, (came, expo, *more), waited, out_shape, 2 * expo.size)


def column_kernel(came_ref, expo_ref, sent_ref):
    rows = expo_ref.shape[0]
    v = 1.0 / jnp.sum(came_ref[...], 0)
    v = jnp.broadcast_to(v, (LANES, rows)).T
    peers, halves, cols = sent_ref.shape
    for h in range(halves):
        for first in range(0, cols, LANES):
            e = expo_ref[:, h * cols + first : h * cols + first + LANES].astype(jnp.float32)
            sent_ref[0, h : h + 1, first : first + LANES] = jnp.sum(e * v, 0, keepdims=True)
    sent_ref[1:] = jnp.broadcast_to(sent_ref[0:1], (peers - 1, halves, cols))


def column_terms(came, expo, peers, *waited):
    out_shape = jax.ShapeDtypeStruct((peers, HALVES, expo.shape[1] // HALVES), jnp.float32)
    return local_call(column_kernel, (came, expo), waited, out_shape, 2 * expo.size)


def team_rows_kernel(came_ref, sent_ref, own_ref):
    own_ref[...] = 1.0 / jnp.sum(came_ref[...], 0)
    sent_ref[...] = jnp.broadcast_to(own_ref[...][None], sent_ref.shape)


def team_rows(came, *waited):
    out_shape = (
        jax.ShapeDtypeStruct((TEAM,) + came.shape[1:], jnp.float32),
        jax.ShapeDtypeStruct(came.shape[1:], jnp.float32),
    )
    return local_call(team_rows_kernel, (came,), waited, out_shape, came.size)


def team_kernel(own_ref, other_ref, proto_ref, after_ref, expo_ref, student_exp_ref, student_ref, done_ref, proto_t):
    @pl.when(pl.program_id(0) == 0)
    def _():
        start = pl.multiple_of(first_group(proto_ref.shape[1] // LANES) * LANES, LANES)
        proto_t[...] = proto_ref[:, pl.ds(start, HELD * LANES)].astype(jnp.float32).T.astype(jnp.bfloat16)
        done_ref[...] = jnp.zeros_like(done_ref)

    def unit(x):
        return (x * lax.rsqrt(jnp.sum(x * x, 1, keepdims=True) + eps)).astype(jnp.bfloat16)

    across = (((1,), (1,)), ((), ()))
    first = lax.axis_index("proto") % 2 == 0
    proto = proto_t[...]
    t = unit(jnp.where(first, own_ref[0], other_ref[0]))
    s = unit(jnp.where(first, other_ref[0], own_ref[0]))
    student_ref[...] = s
    lt = lax.dot_general(proto, t, across, preferred_element_type=jnp.float32)
    expo_ref[...] = jnp.exp(lt / teacher_temp).astype(jnp.bfloat16)
    ls = lax.dot_general(proto, s, across, preferred_element_type=jnp.float32)
    student_exp_ref[...] = jnp.exp(ls / student_temp)


def team_products(own, other, proto, waited):
    senders, rows, depth = own.shape
    part = HELD * LANES
    return pl.pallas_call(
        team_kernel,
        grid=(senders,),
        in_specs=[
            pl.BlockSpec((1, rows, depth), lambda i: (i, 0, 0)),
            pl.BlockSpec((1, rows, depth), lambda i: (i, 0, 0)),
            pl.BlockSpec(proto.shape, lambda i: (0, 0)),
            pl.BlockSpec(memory_space=pl.ANY),
        ],
        out_specs=[
            pl.BlockSpec((part, rows), lambda i: (0, i)),
            pl.BlockSpec((part, rows), lambda i: (0, i)),
            pl.BlockSpec((rows, depth), lambda i: (i, 0)),
            pl.BlockSpec((8, LANES), lambda i: (0, 0)),
        ],
        out_shape=(
            jax.ShapeDtypeStruct((part, senders * rows), jnp.bfloat16),
            jax.ShapeDtypeStruct((part, senders * rows), jnp.float32),
            jax.ShapeDtypeStruct((senders * rows, depth), jnp.bfloat16),
            jax.ShapeDtypeStruct((8, LANES), jnp.float32),
        ),
        scratch_shapes=[pltpu.VMEM((part, depth), jnp.bfloat16)],
        compiler_params=pltpu.CompilerParams(vmem_limit_bytes=TEAM_VMEM),
        cost_estimate=pl.CostEstimate(
            flops=4 * part * senders * rows * depth,
            bytes_accessed=10 * 2**20,
            transcendentals=2 * part * senders * rows,
        ),
    )(own, other, proto, waited)


def local(teacher, student, prototypes, gain):
    rows, depth = teacher.shape
    nb, npr = lax.axis_size("batch"), lax.axis_size("proto")
    teams = [[t * TEAM + i for i in range(TEAM)] for t in range(nb // TEAM)]
    cols = prototypes.shape[1]
    count = cols * npr
    rows_all = rows * nb

    mine, proto_n, expo, sent = start(teacher, student, prototypes, gain, nb)

    def member(rows, flip):
        return lax.ppermute(rows, "batch", [(i, i ^ flip) for i in range(nb)])

    held = [mine, member(mine, 1), None, member(mine, 3)]
    came = lax.all_to_all(sent, "batch", 0, 0, tiled=True)
    sent, _ = row_terms(came, expo, npr, held[1], held[3])
    came = lax.all_to_all(sent, "proto", 0, 0, tiled=True)
    sent = column_terms(came, expo, nb)
    held[2] = member(mine, 2)
    came = lax.all_to_all(sent, "batch", 0, 0, tiled=True)
    sent, _ = row_terms(came, expo, npr, held[2])
    own = jnp.concatenate(held)
    came = lax.all_to_all(sent, "proto", 0, 0, tiled=True)
    sent = column_terms(came, expo, nb)
    other = lax.ppermute(own, "proto", [(i, i ^ 1) for i in range(npr)])
    came = lax.all_to_all(sent, "batch", 0, 0, tiled=True)

    logits = jnp.dot(unit_rows(student), proto_n, preferred_element_type=jnp.float32)
    local_total = jnp.sum(jnp.exp(logits / student_temp), 1)
    sent, scale_u = row_terms(came, expo, npr, other, total=local_total[None])
    came = lax.all_to_all(sent, "proto", 0, 0, tiled=True)
    *team_values, done = team_products(own, other, proto_n, sent)
    sent, inverse = team_rows(came, done)
    scale_v = inverse[0]
    by_sender = lax.all_to_all(sent, "batch", 0, 0, tiled=True, axis_index_groups=teams)

    inv_root = 1.0 / rows_all**0.5
    grad_t = partial_grad(*team_values, scale_u, by_sender, float(count), inv_root, nb)
    parts = lax.all_to_all(grad_t, "batch", 0, 0, tiled=True)
    grad = pl.pallas_call(
        join_kernel,
        out_shape=jax.ShapeDtypeStruct((depth // nb, cols), jnp.float32),
        compiler_params=pltpu.CompilerParams(vmem_limit_bytes=SMALL),
    )(parts)

    scale_u = scale_u.reshape(cols)
    assign = expo.astype(jnp.float32) * scale_u[None, :] * scale_v[:, None]
    targets = (count * assign).astype(jnp.bfloat16)
    return (targets, grad)


def solution(mesh):
    return jax.shard_map(
        local,
        mesh=mesh,
        in_specs=(P("batch", None), P("batch", None), P(None, "proto"), P("proto")),
        out_specs=(P("batch", "proto"), P("batch", "proto")),
        check_vma=False,
    )
```

time: 180 us -> 172 us (0.956)
  waiting for transfers between devices: 61.1 us -> 55.7 us
  local copies, waits for them, and re-layouts: 6.29 us -> 4.17 us
    all_to_all x2, waiting for transfers between devices: 13.4 us -> 10.1 us  [local(): came = lax.all_to_all(sent, 'proto', 0, 0, tiled=True)]
    unnamed x21 -> x15, local copies, waits for them, and re-layouts: 5.57 us -> 3.45 us
    all_to_all x3, waiting for transfers between devices: 22 us -> 20.2 us  [local(): came = lax.all_to_all(sent, 'batch', 0, 0, tiled=True)]
    pallas_call x2 -> x1, Pallas kernels: 4.26 us -> 3.91 us  [start(): pl.pallas_call(start_kernel, grid=(steps,), in_specs=[pl.BlockSpec((rows,...]
  transfers between devices with their start and end apart: 10 -> 10, of which waited for: 7 -> 7; matrix products, arithmetic and copies ran while one was open for 4% -> 4% of each run, Pallas kernels for 5% -> 6%
where the time goes in v6:
time: 172 us; the launch traced here: 171 us
  starting transfers between devices  64 us (37%)
  waiting for transfers between devices  55.7 us (32%)
  blocking collectives  22.1 us (13%)
  Pallas kernels  20.8 us (12%)
  local copies, waits for them, and re-layouts  4.17 us (2%)
  matrix products  2.04 us (1%)
    all_to_all x3, starting transfers between devices, local(): came = lax.all_to_all(sent, 'batch', 0, 0, tiled=True)  27.4 us
    all_to_all x1, waiting for transfers between devices, local(): parts = lax.all_to_all(grad_t, 'batch', 0, 0, tiled=True)  20.2 us
    all_to_all x3, waiting for transfers between devices, local(): came = lax.all_to_all(sent, 'batch', 0, 0, tiled=True)  20.2 us
    all_to_all x2, starting transfers between devices, local(): came = lax.all_to_all(sent, 'proto', 0, 0, tiled=True)  19.2 us
    all_to_all x1, blocking collectives, local(): came = lax.all_to_all(sent, 'proto', 0, 0, tiled=True)  13.5 us
    ppermute x3, starting transfers between devices, member(): return lax.ppermute(rows, 'batch', [(i, i ^ flip) for i in range(nb)])  10.5 us
    all_to_all x2, waiting for transfers between devices, local(): came = lax.all_to_all(sent, 'proto', 0, 0, tiled=True)  10.1 us
    all_to_all x1, blocking collectives, local(): lax.all_to_all(sent, 'batch', 0, 0, tiled=True, axis_index_groups=teams)  8.55 us
  transfers between devices with their start and end apart: 10, of which 7 were waited for; matrix products, arithmetic and copies ran while one was open for 4% of the time, Pallas kernels for 6%

profile of v6, /device:TPU:2, one launch (start us, length us, event | category | flops | bytes accessed | tf_op | source)
XLA Modules:
  0.0 171.2 jit_solution(2782441266598565786)
XLA Ops:
  0.6 3.9 %shard_map.59 = (f32[1,256,256]{2,1,0:T(8,128)}, bf16[256,2816]{1,0:T(8,128)(2,1)}, bf16[256,2816]{1,0:T(8,128)(2,1)S(1)}, f32[32,2,1408]{2,1,0:T(2,128)}) custom-call(bf16[256,256]{1,0:T(8,128)(2,1)} %teacher_ref.1, bf16[256,256]{1,0:T(8,128)(2,1)} %student_ref.1, bf16[256,2816]{1,0:T(8,128)(2,1)} %proto_ref.1, f32[22,128]{1,0:T(8,128)} %bitcast.7), custom_call_target="tpu_custom_call" | custom-call | flops 369098752 | bytes 4325376 | tf_op jit(solution)/shard_map/pallas_call | solution.py:135
  4.5 13.2 %all-to-all-start = ((f32[32,2,1408]{2,1,0:T(2,128)}), f32[32,2,1408]{2,1,0:T(2,128)S(1)}, u32[]{:S(2)}, u32[]{:S(2)}) async-start(f32[32,2,1408]{2,1,0:T(2,128)} %get-tuple-element.17), calls=%async_computation | async-start | bytes 720896 | tf_op jit(solution)/shard_map/all_to_all | solution.py:311
  17.8 2.3 %collective-permute-start = (f32[1,256,256]{2,1,0:T(8,128)}, f32[1,256,256]{2,1,0:T(8,128)S(1)}, u32[]{:S(2)}, u32[]{:S(2)}) collective-permute-start(f32[1,256,256]{2,1,0:T(8,128)} %get-tuple-element.18), channel_id=1, source_target_pairs={{0,1},{1,0},{2,3},{3,2},{4,5},{5,4},{6,7},{7,6},{8,9},{9,8},{10,11... | collective-permute-start | bytes 786440 | tf_op jit(solution)/shard_map/ppermute | solution.py:308
  20.0 4.2 %collective-permute-start.1 = (f32[1,256,256]{2,1,0:T(8,128)}, f32[1,256,256]{2,1,0:T(8,128)S(1)}, u32[]{:S(2)}, u32[]{:S(2)}) collective-permute-start(f32[1,256,256]{2,1,0:T(8,128)} %get-tuple-element.18), channel_id=1, source_target_pairs={{0,3},{1,2},{2,1},{3,0},{4,7},{5,6},{6,5},{7,4},{8,11},{9,10},{10,... | collective-permute-start | bytes 786440 | tf_op jit(solution)/shard_map/ppermute | solution.py:308
  24.3 3.3 %collective-permute-done.refs_2_ = f32[1,256,256]{2,1,0:T(8,128)S(1)} collective-permute-done((f32[1,256,256]{2,1,0:T(8,128)}, f32[1,256,256]{2,1,0:T(8,128)S(1)}, u32[]{:S(2)}, u32[]{:S(2)}) %collective-permute-start) | collective-permute-done | bytes 262176 | tf_op jit(solution)/shard_map/ppermute | solution.py:308
  27.5 1.8 %collective-permute-done.1.refs_3_ = f32[1,256,256]{2,1,0:T(8,128)S(1)} collective-permute-done((f32[1,256,256]{2,1,0:T(8,128)}, f32[1,256,256]{2,1,0:T(8,128)S(1)}, u32[]{:S(2)}, u32[]{:S(2)}) %collective-permute-start.1) | collective-permute-done | bytes 262176 | tf_op jit(solution)/shard_map/ppermute | solution.py:308
  30.5 15.4 %all-to-all-start.1 = ((f32[24,1,256]{2,1,0:T(1,128)}), f32[24,1,256]{2,1,0:T(1,128)S(1)}, u32[]{:S(2)}, u32[]{:S(2)}) async-start(f32[24,1,256]{2,1,0:T(1,128)} %get-tuple-element.19), calls=%async_computation.1 | async-start | bytes 49152 | tf_op jit(solution)/shard_map/all_to_all | solution.py:313
  45.9 4.0 %collective-permute-start.2 = (f32[1,256,256]{2,1,0:T(8,128)S(1)}, f32[1,256,256]{2,1,0:T(8,128)S(1)}, u32[]{:S(2)}, u32[]{:S(2)}) collective-permute-start(f32[1,256,256]{2,1,0:T(8,128)S(1)} %copy-done.5), channel_id=1, source_target_pairs={{0,2},{1,3},{2,0},{3,1},{4,6},{5,7},{6,4},{7,5},{8,10},{9,11},{10,... | collective-permute-start | bytes 786440 | tf_op jit(solution)/shard_map/ppermute | solution.py:308
  49.9 5.9 %all-to-all-done.1.refs_0_ = f32[24,1,256]{2,1,0:T(1,128)S(1)} async-done(((f32[24,1,256]{2,1,0:T(1,128)}), f32[24,1,256]{2,1,0:T(1,128)S(1)}, u32[]{:S(2)}, u32[]{:S(2)}) %all-to-all-start.1) | async-done | bytes 24608 | tf_op jit(solution)/shard_map/all_to_all | solution.py:313
  57.0 8.6 %all-to-all-start.2 = ((f32[32,2,1408]{2,1,0:T(2,128)}), f32[32,2,1408]{2,1,0:T(2,128)S(1)}, u32[]{:S(2)}, u32[]{:S(2)}) async-start(f32[32,2,1408]{2,1,0:T(2,128)} %shard_map.61), calls=%async_computation.2 | async-start | bytes 720896 | tf_op jit(solution)/shard_map/all_to_all | solution.py:316
  68.5 1.9 %collective-permute-start.3 = (f32[4,256,256]{2,1,0:T(8,128)}, f32[4,256,256]{2,1,0:T(8,128)S(1)}, u32[]{:S(2)}, u32[]{:S(2)}) collective-permute-start(f32[4,256,256]{2,1,0:T(8,128)} %constant_dynamic-update-slice_fusion.own_ref), channel_id=1, source_target_pairs={{0,32},{32,0},{64,96},{96,64},{128,160},{160,128},{192,224},{224,1... | collective-permute-start | bytes 3145736 | tf_op jit(solution)/shard_map/ppermute | solution.py:321
  70.4 8.8 %all-to-all-done.2.refs_0_ = f32[32,2,1408]{2,1,0:T(2,128)S(1)} async-done(((f32[32,2,1408]{2,1,0:T(2,128)}), f32[32,2,1408]{2,1,0:T(2,128)S(1)}, u32[]{:S(2)}, u32[]{:S(2)}) %all-to-all-start.2) | async-done | bytes 360480 | tf_op jit(solution)/shard_map/all_to_all | solution.py:316
  80.3 13.5 %all_to_all.40.refs_0_ = f32[24,1,256]{2,1,0:T(1,128)S(1)} all-to-all(f32[24,1,256]{2,1,0:T(1,128)S(1)} %get-tuple-element.20), channel_id=1, replica_groups=mesh['proto'=24,'batch'=32] {'proto'}, dimensions={0} | all-to-all | bytes 49152 | tf_op jit(solution)/shard_map/all_to_all | solution.py:319
  95.0 5.6 %all-to-all-start.4 = ((f32[32,2,1408]{2,1,0:T(2,128)}), f32[32,2,1408]{2,1,0:T(2,128)S(1)}, u32[]{:S(2)}, u32[]{:S(2)}) async-start(f32[32,2,1408]{2,1,0:T(2,128)} %shard_map.63), calls=%async_computation.4 | async-start | bytes 720896 | tf_op jit(solution)/shard_map/all_to_all | solution.py:322
  100.7 2.0 %fusion.1 = f32[256]{0:T(256)S(1)} fusion(bf16[256,2816]{1,0:T(8,128)(2,1)} %get-tuple-element.21.proto_ref, bf16[256,256]{1,0:T(8,128)(2,1)S(1)} %copy-done.4, f32[256]{0:T(256)S(1)} %add_rsqrt_fusion), kind=kOutput, calls=%fused_computation.3 | convolution fusion | flops 370736896 | bytes 1574912 | tf_op jit(solution)/shard_map/dot_general | solution.py:324
  102.7 11.4 %all-to-all-done.4.refs_0_ = f32[32,2,1408]{2,1,0:T(2,128)S(1)} async-done(((f32[32,2,1408]{2,1,0:T(2,128)}), f32[32,2,1408]{2,1,0:T(2,128)S(1)}, u32[]{:S(2)}, u32[]{:S(2)}) %all-to-all-start.4) | async-done | bytes 360480 | tf_op jit(solution)/shard_map/all_to_all | solution.py:322
  115.9 3.8 %all-to-all-start.5 = ((f32[24,2,256]{2,1,0:T(2,128)}), f32[24,2,256]{2,1,0:T(2,128)S(1)}, u32[]{:S(2)}, u32[]{:S(2)}) async-start(f32[24,2,256]{2,1,0:T(2,128)} %get-tuple-element.23.after_ref), calls=%async_computation.5 | async-start | bytes 98304 | tf_op jit(solution)/shard_map/all_to_all | solution.py:327
  119.7 6.1 %shard_map.65 = (bf16[768,1024]{1,0:T(8,128)(2,1)}, f32[768,1024]{1,0:T(8,128)}, bf16[1024,256]{1,0:T(8,128)(2,1)}, f32[8,128]{1,0:T(8,128)}) custom-call(f32[4,256,256]{2,1,0:T(8,128)} %constant_dynamic-update-slice_fusion.own_ref, f32[4,256,256]{2,1,0:T(8,128)} %copy-done, bf16[256,2816]{1,0:T(8,128)(2,1)} %get-tuple-element.21.proto_ref, ...), custom_call_target="tpu_custom_call" | custom-call | flops 805306368 | bytes 10485760 | tf_op jit(solution)/shard_map/pallas_call | solution.py:266
  125.8 4.2 %all-to-all-done.5.refs_0_ = f32[24,2,256]{2,1,0:T(2,128)S(1)} async-done(((f32[24,2,256]{2,1,0:T(2,128)}), f32[24,2,256]{2,1,0:T(2,128)S(1)}, u32[]{:S(2)}, u32[]{:S(2)}) %all-to-all-start.5) | async-done | bytes 49184 | tf_op jit(solution)/shard_map/all_to_all | solution.py:327
  130.7 8.6 %all_to_all.41.refs_10_ = f32[4,2,256]{2,1,0:T(2,128)} all-to-all(f32[4,2,256]{2,1,0:T(2,128)S(1)} %get-tuple-element.29), channel_id=1, replica_groups={{0,1,2,3},{4,5,6,7},{8,9,10,11},{12,13,14,15},{16,17,18,19},{20,21,22,2..., dimensions={0} | all-to-all | bytes 16384 | tf_op jit(solution)/shard_map/all_to_all | solution.py:331
  139.3 4.4 %shard_map.67 = f32[32,8,768]{2,1,0:T(8,128)} custom-call(bf16[768,1024]{1,0:T(8,128)(2,1)} %get-tuple-element.26.refs_0_.refs_1_.refs_2_.refs_3_, bf16[768,1024]{1,0:T(8,128)(2,1)} %get-tuple-element.26.refs_0_.refs_1_.refs_2_.refs_3_, bf16[768,1024]{1,0:T(8,128)(2,1)} %get-tuple-element.26.refs_0_.refs_1_.refs_2_.refs_3_, ...), custom_call_target="tpu_custom_call" | custom-call | flops 402653184 | bytes 4718592 | tf_op jit(solution)/shard_map/pallas_call | solution.py:69
  143.7 5.0 %all-to-all-start.7 = ((f32[32,8,768]{2,1,0:T(8,128)}), f32[32,8,768]{2,1,0:T(8,128)S(1)}, u32[]{:S(2)}, u32[]{:S(2)}) async-start(f32[32,8,768]{2,1,0:T(8,128)} %shard_map.67), calls=%async_computation.7 | async-start | bytes 1572864 | tf_op jit(solution)/shard_map/all_to_all | solution.py:335
  148.7 1.5 multiply_convert_fusion
  150.3 20.2 %all-to-all-done.7.parts_ref = f32[32,8,768]{2,1,0:T(8,128)S(1)} async-done(((f32[32,8,768]{2,1,0:T(8,128)}), f32[32,8,768]{2,1,0:T(8,128)S(1)}, u32[]{:S(2)}, u32[]{:S(2)}) %all-to-all-start.7) | async-done | bytes 786464 | tf_op jit(solution)/shard_map/all_to_all | solution.py:335
  (29 shorter events, 10.7 us)
Async XLA Ops:
  4.5 41.3 %copy-start.5 = (f32[1,256,256]{2,1,0:T(8,128)S(1)}, f32[1,256,256]{2,1,0:T(8,128)}, u32[]{:S(2)}) copy-start(f32[1,256,256]{2,1,0:T(8,128)} %get-tuple-element.18) | copy-start | bytes 786436
  4.5 24.8 %all-to-all-start = ((f32[32,2,1408]{2,1,0:T(2,128)}), f32[32,2,1408]{2,1,0:T(2,128)S(1)}, u32[]{:S(2)}, u32[]{:S(2)}) async-start(f32[32,2,1408]{2,1,0:T(2,128)} %get-tuple-element.17), calls=%async_computation | async-start | bytes 720896 | tf_op jit(solution)/shard_map/all_to_all | solution.py:311
  17.8 9.8 %collective-permute-start = (f32[1,256,256]{2,1,0:T(8,128)}, f32[1,256,256]{2,1,0:T(8,128)S(1)}, u32[]{:S(2)}, u32[]{:S(2)}) collective-permute-start(f32[1,256,256]{2,1,0:T(8,128)} %get-tuple-element.18), channel_id=1, source_target_pairs={{0,1},{1,0},{2,3},{3,2},{4,5},{5,4},{6,7},{7,6},{8,9},{9,8},{10,11... | collective-permute-start | bytes 786440 | tf_op jit(solution)/shard_map/ppermute | solution.py:308
  20.0 9.3 %collective-permute-start.1 = (f32[1,256,256]{2,1,0:T(8,128)}, f32[1,256,256]{2,1,0:T(8,128)S(1)}, u32[]{:S(2)}, u32[]{:S(2)}) collective-permute-start(f32[1,256,256]{2,1,0:T(8,128)} %get-tuple-element.18), channel_id=1, source_target_pairs={{0,3},{1,2},{2,1},{3,0},{4,7},{5,6},{6,5},{7,4},{8,11},{9,10},{10,... | collective-permute-start | bytes 786440 | tf_op jit(solution)/shard_map/ppermute | solution.py:308
  30.5 25.3 %all-to-all-start.1 = ((f32[24,1,256]{2,1,0:T(1,128)}), f32[24,1,256]{2,1,0:T(1,128)S(1)}, u32[]{:S(2)}, u32[]{:S(2)}) async-start(f32[24,1,256]{2,1,0:T(1,128)} %get-tuple-element.19), calls=%async_computation.1 | async-start | bytes 49152 | tf_op jit(solution)/shard_map/all_to_all | solution.py:313
  45.9 21.2 %collective-permute-start.2 = (f32[1,256,256]{2,1,0:T(8,128)S(1)}, f32[1,256,256]{2,1,0:T(8,128)S(1)}, u32[]{:S(2)}, u32[]{:S(2)}) collective-permute-start(f32[1,256,256]{2,1,0:T(8,128)S(1)} %copy-done.5), channel_id=1, source_target_pairs={{0,2},{1,3},{2,0},{3,1},{4,6},{5,7},{6,4},{7,5},{8,10},{9,11},{10,... | collective-permute-start | bytes 786440 | tf_op jit(solution)/shard_map/ppermute | solution.py:308
  57.0 22.2 %all-to-all-start.2 = ((f32[32,2,1408]{2,1,0:T(2,128)}), f32[32,2,1408]{2,1,0:T(2,128)S(1)}, u32[]{:S(2)}, u32[]{:S(2)}) async-start(f32[32,2,1408]{2,1,0:T(2,128)} %shard_map.61), calls=%async_computation.2 | async-start | bytes 720896 | tf_op jit(solution)/shard_map/all_to_all | solution.py:316
  67.1 33.5 %copy-start.4 = (bf16[256,256]{1,0:T(8,128)(2,1)S(1)}, bf16[256,256]{1,0:T(8,128)(2,1)}, u32[]{:S(2)}) copy-start(bf16[256,256]{1,0:T(8,128)(2,1)} %student_ref.1) | copy-start | bytes 393220
  68.5 34.2 %collective-permute-start.3 = (f32[4,256,256]{2,1,0:T(8,128)}, f32[4,256,256]{2,1,0:T(8,128)S(1)}, u32[]{:S(2)}, u32[]{:S(2)}) collective-permute-start(f32[4,256,256]{2,1,0:T(8,128)} %constant_dynamic-update-slice_fusion.own_ref), channel_id=1, source_target_pairs={{0,32},{32,0},{64,96},{96,64},{128,160},{160,128},{192,224},{224,1... | collective-permute-start | bytes 3145736 | tf_op jit(solution)/shard_map/ppermute | solution.py:321
  95.0 19.2 %all-to-all-start.4 = ((f32[32,2,1408]{2,1,0:T(2,128)}), f32[32,2,1408]{2,1,0:T(2,128)S(1)}, u32[]{:S(2)}, u32[]{:S(2)}) async-start(f32[32,2,1408]{2,1,0:T(2,128)} %shard_map.63), calls=%async_computation.4 | async-start | bytes 720896 | tf_op jit(solution)/shard_map/all_to_all | solution.py:322
  102.7 17.0 %copy-start = (f32[4,256,256]{2,1,0:T(8,128)}, f32[4,256,256]{2,1,0:T(8,128)S(1)}, u32[]{:S(2)}) copy-start(f32[4,256,256]{2,1,0:T(8,128)S(1)} %collective-permute-done.3.refs_3_.other_ref) | copy-start | bytes 3145732
  115.3 0.6 copy-start.1
  115.9 14.1 %all-to-all-start.5 = ((f32[24,2,256]{2,1,0:T(2,128)}), f32[24,2,256]{2,1,0:T(2,128)S(1)}, u32[]{:S(2)}, u32[]{:S(2)}) async-start(f32[24,2,256]{2,1,0:T(2,128)} %get-tuple-element.23.after_ref), calls=%async_computation.5 | async-start | bytes 98304 | tf_op jit(solution)/shard_map/all_to_all | solution.py:327
  130.0 0.7 copy-start.3
  139.3 9.4 %copy-start.2 = (f32[22,128]{1,0:T(8,128)S(1)}, f32[22,128]{1,0:T(8,128)}, u32[]{:S(2)}) copy-start(f32[22,128]{1,0:T(8,128)} %copy-done.1) | copy-start | bytes 33796
  143.7 26.8 %all-to-all-start.7 = ((f32[32,8,768]{2,1,0:T(8,128)}), f32[32,8,768]{2,1,0:T(8,128)S(1)}, u32[]{:S(2)}, u32[]{:S(2)}) async-start(f32[32,8,768]{2,1,0:T(8,128)} %shard_map.67), calls=%async_computation.7 | async-start | bytes 1572864 | tf_op jit(solution)/shard_map/all_to_all | solution.py:335

commit v7 on v6

--- a/solution.py
+++ b/solution.py
@@ -33,8 +33,9 @@
 
 def grad_kernel(count, scale, *refs):
     exps, student_exps = refs[:SPLIT], refs[SPLIT : 2 * SPLIT]
-    student_ref, u_ref, rows_ref, out_ref, diff = refs[2 * SPLIT :]
-    rows = rows_ref.shape[2]
+    student_ref, u_ref, came_ref, out_ref, own_ref, diff = refs[2 * SPLIT :]
+    senders = came_ref.shape[0] // TEAM
+    rows = came_ref.shape[2]
     chunk = diff.shape[0]
     piece = chunk // SPLIT
     me = lax.axis_index("batch") % TEAM
@@ -42,7 +43,10 @@
     wide = [jnp.broadcast_to(u[g : g + 1, :], (LANES, LANES)).T for g in range(chunk // LANES)]
     wide = jnp.concatenate(wide, 0)
     for place in range(TEAM):
-        by = rows_ref[me ^ place] * count
+        by = 1.0 / jnp.sum(came_ref[pl.ds((me ^ place) * senders, senders)], 0)
+        if place == 0:
+            own_ref[...] = by
+        by = by * count
         for first in range(0, rows, LANES):
             v = by[0:1, first : first + LANES]
             inv_total = by[1:2, first : first + LANES]
@@ -56,7 +60,7 @@
     out_ref[...] = (product.T * scale).reshape(out_ref.shape)
 
 
-def partial_grad(expo_t, student_exp_t, student, u, by_sender, count, scale, owners):
+def partial_grad(expo_t, student_exp_t, student, u, came, count, scale, owners):
     part, crops = expo_t.shape
     depth = student.shape[1]
     steps = 2
@@ -74,16 +78,22 @@
             *pieces(),
             pl.BlockSpec(student.shape, lambda i: (0, 0)),
             pl.BlockSpec(u.shape, lambda i: (0, 0)),
-            pl.BlockSpec(by_sender.shape, lambda i: (0, 0, 0)),
-        ],
-        out_specs=pl.BlockSpec((owners, depth // owners, chunk), lambda i: (0, 0, i)),
-        out_shape=jax.ShapeDtypeStruct((owners, depth // owners, part), jnp.float32),
+            pl.BlockSpec(came.shape, lambda i: (0, 0, 0)),
+        ],
+        out_specs=[
+            pl.BlockSpec((owners, depth // owners, chunk), lambda i: (0, 0, i)),
+            pl.BlockSpec(came.shape[1:], lambda i: (0, 0)),
+        ],
+        out_shape=(
+            jax.ShapeDtypeStruct((owners, depth // owners, part), jnp.float32),
+            jax.ShapeDtypeStruct(came.shape[1:], jnp.float32),
+        ),
         scratch_shapes=[pltpu.VMEM((chunk, crops), jnp.bfloat16)],
         compiler_params=pltpu.CompilerParams(vmem_limit_bytes=GRAD_VMEM),
         cost_estimate=pl.CostEstimate(
             flops=2 * part * crops * depth, bytes_accessed=6 * part * crops, transcendentals=0
         ),
-    )(*[expo_t] * SPLIT, *[student_exp_t] * SPLIT, student, u, by_sender)
+    )(*[expo_t] * SPLIT, *[student_exp_t] * SPLIT, student, u, came)
 
 
 def join_kernel(parts_ref, out_ref):
@@ -225,25 +235,12 @@
     return local_call(column_kernel, (came, expo), waited, out_shape, 2 * expo.size)
 
 
-def team_rows_kernel(came_ref, sent_ref, own_ref):
-    own_ref[...] = 1.0 / jnp.sum(came_ref[...], 0)
-    sent_ref[...] = jnp.broadcast_to(own_ref[...][None], sent_ref.shape)
-
-
-def team_rows(came, *waited):
-    out_shape = (
-        jax.ShapeDtypeStruct((TEAM,) + came.shape[1:], jnp.float32),
-        jax.ShapeDtypeStruct(came.shape[1:], jnp.float32),
-    )
-    return local_call(team_rows_kernel, (came,), waited, out_shape, came.size)
-
-
-def team_kernel(own_ref, other_ref, proto_ref, after_ref, expo_ref, student_exp_ref, student_ref, done_ref, proto_t):
+def team_kernel(own_ref, other_ref, proto_ref, u_ref, after_ref, expo_ref, student_exp_ref, student_ref, u_out_ref, proto_t):
     @pl.when(pl.program_id(0) == 0)
     def _():
         start = pl.multiple_of(first_group(proto_ref.shape[1] // LANES) * LANES, LANES)
         proto_t[...] = proto_ref[:, pl.ds(start, HELD * LANES)].astype(jnp.float32).T.astype(jnp.bfloat16)
-        done_ref[...] = jnp.zeros_like(done_ref)
+        u_out_ref[...] = u_ref[...]
 
     def unit(x):
         return (x * lax.rsqrt(jnp.sum(x * x, 1, keepdims=True) + eps)).astype(jnp.bfloat16)
@@ -260,7 +257,7 @@
     student_exp_ref[...] = jnp.exp(ls / student_temp)
 
 
-def team_products(own, other, proto, waited):
+def team_products(own, other, proto, u, waited):
     senders, rows, depth = own.shape
     part = HELD * LANES
     return pl.pallas_call(
@@ -270,19 +267,20 @@
             pl.BlockSpec((1, rows, depth), lambda i: (i, 0, 0)),
             pl.BlockSpec((1, rows, depth), lambda i: (i, 0, 0)),
             pl.BlockSpec(proto.shape, lambda i: (0, 0)),
+            pl.BlockSpec(u.shape, lambda i: (0, 0)),
             pl.BlockSpec(memory_space=pl.ANY),
         ],
         out_specs=[
             pl.BlockSpec((part, rows), lambda i: (0, i)),
             pl.BlockSpec((part, rows), lambda i: (0, i)),
             pl.BlockSpec((rows, depth), lambda i: (i, 0)),
-            pl.BlockSpec((8, LANES), lambda i: (0, 0)),
+            pl.BlockSpec(u.shape, lambda i: (0, 0)),
         ],
         out_shape=(
             jax.ShapeDtypeStruct((part, senders * rows), jnp.bfloat16),
             jax.ShapeDtypeStruct((part, senders * rows), jnp.float32),
             jax.ShapeDtypeStruct((senders * rows, depth), jnp.bfloat16),
-            jax.ShapeDtypeStruct((8, LANES), jnp.float32),
+            jax.ShapeDtypeStruct(u.shape, jnp.float32),
         ),
         scratch_shapes=[pltpu.VMEM((part, depth), jnp.bfloat16)],
         compiler_params=pltpu.CompilerParams(vmem_limit_bytes=TEAM_VMEM),
@@ -291,13 +289,15 @@
             bytes_accessed=10 * 2**20,
             transcendentals=2 * part * senders * rows,
         ),
-    )(own, other, proto, waited)
+    )(own, other, proto, u, waited)
 
 
 def local(teacher, student, prototypes, gain):
     rows, depth = teacher.shape
     nb, npr = lax.axis_size("batch"), lax.axis_size("proto")
-    teams = [[t * TEAM + i for i in range(TEAM)] for t in range(nb // TEAM)]
+    rows_of_chips = [
+        [(t * TEAM + i) * npr + p for i in range(TEAM) for p in range(npr)] for t in range(nb // TEAM)
+    ]
     cols = prototypes.shape[1]
     count = cols * npr
     rows_all = rows * nb
@@ -309,9 +309,9 @@
 
     held = [mine, member(mine, 1), None, member(mine, 3)]
     came = lax.all_to_all(sent, "batch", 0, 0, tiled=True)
-    sent, _ = row_terms(came, expo, npr, held[1], held[3])
+    sent, _ = row_terms(came, expo, npr, held[1])
     came = lax.all_to_all(sent, "proto", 0, 0, tiled=True)
-    sent = column_terms(came, expo, nb)
+    sent = column_terms(came, expo, nb, held[3])
     held[2] = member(mine, 2)
     came = lax.all_to_all(sent, "batch", 0, 0, tiled=True)
     sent, _ = row_terms(came, expo, npr, held[2])
@@ -323,15 +323,13 @@
 
     logits = jnp.dot(unit_rows(student), proto_n, preferred_element_type=jnp.float32)
     local_total = jnp.sum(jnp.exp(logits / student_temp), 1)
-    sent, scale_u = row_terms(came, expo, npr, other, total=local_total[None])
-    came = lax.all_to_all(sent, "proto", 0, 0, tiled=True)
-    *team_values, done = team_products(own, other, proto_n, sent)
-    sent, inverse = team_rows(came, done)
+    sent, scale_u = row_terms(came, expo, TEAM * npr, other, total=local_total[None])
+    came = lax.all_to_all(sent, ("batch", "proto"), 0, 0, tiled=True, axis_index_groups=rows_of_chips)
+    team_values = team_products(own, other, proto_n, scale_u, sent)
+
+    inv_root = 1.0 / rows_all**0.5
+    grad_t, inverse = partial_grad(*team_values, came, float(count), inv_root, nb)
     scale_v = inverse[0]
-    by_sender = lax.all_to_all(sent, "batch", 0, 0, tiled=True, axis_index_groups=teams)
-
-    inv_root = 1.0 / rows_all**0.5
-    grad_t = partial_grad(*team_values, scale_u, by_sender, float(count), inv_root, nb)
     parts = lax.all_to_all(grad_t, "batch", 0, 0, tiled=True)
     grad = pl.pallas_call(
         join_kernel,

time: 172 us -> 170 us (0.988)
  blocking collectives: 22.1 us -> 12.8 us
  waiting for transfers between devices: 55.7 us -> 60.4 us
  starting transfers between devices: 64 us -> 66.1 us
    all_to_all x0 -> x1, waiting for transfers between devices: none -> 10.3 us  [local(): lax.all_to_all(sent, ('batch', 'proto'), 0, 0, tiled=True, axis_index_gro...]
    all_to_all x1 -> x0, blocking collectives: 8.55 us -> none  [local(): lax.all_to_all(sent, 'batch', 0, 0, tiled=True, axis_index_groups=teams)]
    all_to_all x0 -> x1, starting transfers between devices: none -> 6.91 us  [local(): lax.all_to_all(sent, ('batch', 'proto'), 0, 0, tiled=True, axis_index_gro...]
    all_to_all x2 -> x1, starting transfers between devices: 19.2 us -> 14.9 us  [local(): came = lax.all_to_all(sent, 'proto', 0, 0, tiled=True)]
    all_to_all x2 -> x1, waiting for transfers between devices: 10.1 us -> 5.99 us  [local(): came = lax.all_to_all(sent, 'proto', 0, 0, tiled=True)]
    ppermute x3, waiting for transfers between devices: 5.1 us -> 3.3 us  [member(): return lax.ppermute(rows, 'batch', [(i, i ^ flip) for i in range(nb)])]
    pallas_call x6 -> x5, Pallas kernels: 5.71 us -> 5.74 us  [local_call(): pl.pallas_call(body, in_specs=[pl.BlockSpec()] * n + [pl.BlockSpec(memory...]
where the time goes in v7:
time: 170 us; the launch traced here: 169 us
  starting transfers between devices  66.1 us (39%)
  waiting for transfers between devices  60.4 us (36%)
  Pallas kernels  20.9 us (12%)
  blocking collectives  12.8 us (8%)
  local copies, waits for them, and re-layouts  4.26 us (3%)
  matrix products  2.04 us (1%)
    all_to_all x3, starting transfers between devices, local(): came = lax.all_to_all(sent, 'batch', 0, 0, tiled=True)  27 us
    all_to_all x3, waiting for transfers between devices, local(): came = lax.all_to_all(sent, 'batch', 0, 0, tiled=True)  21.3 us
    all_to_all x1, waiting for transfers between devices, local(): parts = lax.all_to_all(grad_t, 'batch', 0, 0, tiled=True)  19.5 us
    all_to_all x1, starting transfers between devices, local(): came = lax.all_to_all(sent, 'proto', 0, 0, tiled=True)  14.9 us
    all_to_all x1, blocking collectives, local(): came = lax.all_to_all(sent, 'proto', 0, 0, tiled=True)  12.8 us
    ppermute x3, starting transfers between devices, member(): return lax.ppermute(rows, 'batch', [(i, i ^ flip) for i in range(nb)])  10.4 us
    all_to_all x1, waiting for transfers between devices, local(): lax.all_to_all(sent, ('batch', 'proto'), 0, 0, tiled=True, axis_index_gro...  10.3 us
    all_to_all x1, starting transfers between devices, local(): lax.all_to_all(sent, ('batch', 'proto'), 0, 0, tiled=True, axis_index_gro...  6.91 us
  transfers between devices with their start and end apart: 10, of which 7 were waited for; matrix products, arithmetic and copies ran while one was open for 4% of the time, Pallas kernels for 6%

profile of v7, /device:TPU:2, one launch (start us, length us, event | category | flops | bytes accessed | tf_op | source)
XLA Modules:
  0.0 168.9 jit_solution(13680401908495202100)
XLA Ops:
  0.6 3.9 %shard_map.59 = (f32[1,256,256]{2,1,0:T(8,128)}, bf16[256,2816]{1,0:T(8,128)(2,1)}, bf16[256,2816]{1,0:T(8,128)(2,1)S(1)}, f32[32,2,1408]{2,1,0:T(2,128)}) custom-call(bf16[256,256]{1,0:T(8,128)(2,1)} %teacher_ref.1, bf16[256,256]{1,0:T(8,128)(2,1)} %student_ref.1, bf16[256,2816]{1,0:T(8,128)(2,1)} %proto_ref.1, f32[22,128]{1,0:T(8,128)} %bitcast.7), custom_call_target="tpu_custom_call" | custom-call | flops 369098752 | bytes 4325376 | tf_op jit(solution)/shard_map/pallas_call | solution.py:145
  4.5 13.2 %all-to-all-start = ((f32[32,2,1408]{2,1,0:T(2,128)}), f32[32,2,1408]{2,1,0:T(2,128)S(1)}, u32[]{:S(2)}, u32[]{:S(2)}) async-start(f32[32,2,1408]{2,1,0:T(2,128)} %get-tuple-element.17), calls=%async_computation | async-start | bytes 720896 | tf_op jit(solution)/shard_map/all_to_all | solution.py:311
  17.8 2.3 %collective-permute-start = (f32[1,256,256]{2,1,0:T(8,128)}, f32[1,256,256]{2,1,0:T(8,128)S(1)}, u32[]{:S(2)}, u32[]{:S(2)}) collective-permute-start(f32[1,256,256]{2,1,0:T(8,128)} %get-tuple-element.18), channel_id=1, source_target_pairs={{0,1},{1,0},{2,3},{3,2},{4,5},{5,4},{6,7},{7,6},{8,9},{9,8},{10,11... | collective-permute-start | bytes 786440 | tf_op jit(solution)/shard_map/ppermute | solution.py:308
  20.0 4.2 %collective-permute-start.1 = (f32[1,256,256]{2,1,0:T(8,128)}, f32[1,256,256]{2,1,0:T(8,128)S(1)}, u32[]{:S(2)}, u32[]{:S(2)}) collective-permute-start(f32[1,256,256]{2,1,0:T(8,128)} %get-tuple-element.18), channel_id=1, source_target_pairs={{0,3},{1,2},{2,1},{3,0},{4,7},{5,6},{6,5},{7,4},{8,11},{9,10},{10,... | collective-permute-start | bytes 786440 | tf_op jit(solution)/shard_map/ppermute | solution.py:308
  24.3 3.3 %collective-permute-done.refs_2_ = f32[1,256,256]{2,1,0:T(8,128)S(1)} collective-permute-done((f32[1,256,256]{2,1,0:T(8,128)}, f32[1,256,256]{2,1,0:T(8,128)S(1)}, u32[]{:S(2)}, u32[]{:S(2)}) %collective-permute-start) | collective-permute-done | bytes 262176 | tf_op jit(solution)/shard_map/ppermute | solution.py:308
  29.9 14.9 %all-to-all-start.1 = ((f32[24,1,256]{2,1,0:T(1,128)}), f32[24,1,256]{2,1,0:T(1,128)S(1)}, u32[]{:S(2)}, u32[]{:S(2)}) async-start(f32[24,1,256]{2,1,0:T(1,128)} %get-tuple-element.19), calls=%async_computation.1 | async-start | bytes 49152 | tf_op jit(solution)/shard_map/all_to_all | solution.py:313
  44.8 4.0 %collective-permute-start.2 = (f32[1,256,256]{2,1,0:T(8,128)}, f32[1,256,256]{2,1,0:T(8,128)S(1)}, u32[]{:S(2)}, u32[]{:S(2)}) collective-permute-start(f32[1,256,256]{2,1,0:T(8,128)} %get-tuple-element.18), channel_id=1, source_target_pairs={{0,2},{1,3},{2,0},{3,1},{4,6},{5,7},{6,4},{7,5},{8,10},{9,11},{10,... | collective-permute-start | bytes 786440 | tf_op jit(solution)/shard_map/ppermute | solution.py:308
  48.8 6.0 %all-to-all-done.1.refs_0_ = f32[24,1,256]{2,1,0:T(1,128)S(1)} async-done(((f32[24,1,256]{2,1,0:T(1,128)}), f32[24,1,256]{2,1,0:T(1,128)S(1)}, u32[]{:S(2)}, u32[]{:S(2)}) %all-to-all-start.1) | async-done | bytes 24608 | tf_op jit(solution)/shard_map/all_to_all | solution.py:313
  55.9 8.2 %all-to-all-start.2 = ((f32[32,2,1408]{2,1,0:T(2,128)}), f32[32,2,1408]{2,1,0:T(2,128)S(1)}, u32[]{:S(2)}, u32[]{:S(2)}) async-start(f32[32,2,1408]{2,1,0:T(2,128)} %shard_map.61), calls=%async_computation.2 | async-start | bytes 720896 | tf_op jit(solution)/shard_map/all_to_all | solution.py:316
  67.1 1.9 %collective-permute-start.3 = (f32[4,256,256]{2,1,0:T(8,128)}, f32[4,256,256]{2,1,0:T(8,128)S(1)}, u32[]{:S(2)}, u32[]{:S(2)}) collective-permute-start(f32[4,256,256]{2,1,0:T(8,128)} %constant_dynamic-update-slice_fusion.own_ref), channel_id=1, source_target_pairs={{0,32},{32,0},{64,96},{96,64},{128,160},{160,128},{192,224},{224,1... | collective-permute-start | bytes 3145736 | tf_op jit(solution)/shard_map/ppermute | solution.py:321
  69.0 8.8 %all-to-all-done.2.refs_0_ = f32[32,2,1408]{2,1,0:T(2,128)S(1)} async-done(((f32[32,2,1408]{2,1,0:T(2,128)}), f32[32,2,1408]{2,1,0:T(2,128)S(1)}, u32[]{:S(2)}, u32[]{:S(2)}) %all-to-all-start.2) | async-done | bytes 360480 | tf_op jit(solution)/shard_map/all_to_all | solution.py:316
  78.8 12.8 %all_to_all.35.refs_0_ = f32[24,1,256]{2,1,0:T(1,128)S(1)} all-to-all(f32[24,1,256]{2,1,0:T(1,128)S(1)} %get-tuple-element.20), channel_id=1, replica_groups=mesh['proto'=24,'batch'=32] {'proto'}, dimensions={0} | all-to-all | bytes 49152 | tf_op jit(solution)/shard_map/all_to_all | solution.py:319
  91.7 1.2 shard_map.63
  92.8 5.6 %all-to-all-start.4 = ((f32[32,2,1408]{2,1,0:T(2,128)}), f32[32,2,1408]{2,1,0:T(2,128)S(1)}, u32[]{:S(2)}, u32[]{:S(2)}) async-start(f32[32,2,1408]{2,1,0:T(2,128)} %shard_map.63), calls=%async_computation.4 | async-start | bytes 720896 | tf_op jit(solution)/shard_map/all_to_all | solution.py:322
  98.5 2.0 %fusion.1 = f32[256]{0:T(256)S(1)} fusion(bf16[256,2816]{1,0:T(8,128)(2,1)} %get-tuple-element.21.proto_ref, bf16[256,256]{1,0:T(8,128)(2,1)S(1)} %copy-done.4, f32[256]{0:T(256)S(1)} %add_rsqrt_fusion), kind=kOutput, calls=%fused_computation.3 | convolution fusion | flops 370736896 | bytes 1574912 | tf_op jit(solution)/shard_map/dot_general | solution.py:324
  100.6 11.4 %all-to-all-done.4.refs_0_ = f32[32,2,1408]{2,1,0:T(2,128)S(1)} async-done(((f32[32,2,1408]{2,1,0:T(2,128)}), f32[32,2,1408]{2,1,0:T(2,128)S(1)}, u32[]{:S(2)}, u32[]{:S(2)}) %all-to-all-start.4) | async-done | bytes 360480 | tf_op jit(solution)/shard_map/all_to_all | solution.py:322
  112.0 1.2 shard_map.64
  113.2 6.9 %all-to-all-start.5 = ((f32[96,2,256]{2,1,0:T(2,128)}), f32[96,2,256]{2,1,0:T(2,128)S(1)}, u32[]{:S(2)}, u32[]{:S(2)}) async-start(f32[96,2,256]{2,1,0:T(2,128)} %get-tuple-element.23.after_ref), calls=%async_computation.5 | async-start | bytes 393216 | tf_op jit(solution)/shard_map/all_to_all | solution.py:327
  120.2 6.1 %shard_map.65 = (bf16[768,1024]{1,0:T(8,128)(2,1)}, f32[768,1024]{1,0:T(8,128)}, bf16[1024,256]{1,0:T(8,128)(2,1)}, f32[22,128]{1,0:T(8,128)}) custom-call(f32[4,256,256]{2,1,0:T(8,128)} %constant_dynamic-update-slice_fusion.own_ref, f32[4,256,256]{2,1,0:T(8,128)} %copy-done, bf16[256,2816]{1,0:T(8,128)(2,1)} %get-tuple-element.21.proto_ref, ...), custom_call_target="tpu_custom_call" | custom-call | flops 805306368 | bytes 10485760 | tf_op jit(solution)/shard_map/pallas_call | solution.py:263
  126.3 10.3 %all-to-all-done.5.refs_10_ = f32[96,2,256]{2,1,0:T(2,128)S(1)} async-done(((f32[96,2,256]{2,1,0:T(2,128)}), f32[96,2,256]{2,1,0:T(2,128)S(1)}, u32[]{:S(2)}, u32[]{:S(2)}) %all-to-all-start.5) | async-done | bytes 196640 | tf_op jit(solution)/shard_map/all_to_all | solution.py:327
  137.2 4.4 %shard_map.66 = (f32[32,8,768]{2,1,0:T(8,128)}, f32[2,256]{1,0:T(2,128)}) custom-call(bf16[768,1024]{1,0:T(8,128)(2,1)} %get-tuple-element.24.refs_0_.refs_1_.refs_2_.refs_3_, bf16[768,1024]{1,0:T(8,128)(2,1)} %get-tuple-element.24.refs_0_.refs_1_.refs_2_.refs_3_, bf16[768,1024]{1,0:T(8,128)(2,1)} %get-tuple-element.24.refs_0_.refs_1_.refs_2_.refs_3_, ...), custom_call_target="tpu_custom_call" | custom-call | flops 402653184 | bytes 4718592 | tf_op jit(solution)/shard_map/pallas_call | solution.py:73
  141.7 4.9 %all-to-all-start.6 = ((f32[32,8,768]{2,1,0:T(8,128)}), f32[32,8,768]{2,1,0:T(8,128)S(1)}, u32[]{:S(2)}, u32[]{:S(2)}) async-start(f32[32,8,768]{2,1,0:T(8,128)} %get-tuple-element.29), calls=%async_computation.6 | async-start | bytes 1572864 | tf_op jit(solution)/shard_map/all_to_all | solution.py:333
  147.2 1.5 multiply_convert_fusion
  148.8 19.5 %all-to-all-done.6.parts_ref = f32[32,8,768]{2,1,0:T(8,128)S(1)} async-done(((f32[32,8,768]{2,1,0:T(8,128)}), f32[32,8,768]{2,1,0:T(8,128)S(1)}, u32[]{:S(2)}, u32[]{:S(2)}) %all-to-all-start.6) | async-done | bytes 786464 | tf_op jit(solution)/shard_map/all_to_all | solution.py:333
  (27 shorter events, 9.6 us)
Async XLA Ops:
  4.5 59.6 %copy-start.5 = (f32[1,256,256]{2,1,0:T(8,128)S(1)}, f32[1,256,256]{2,1,0:T(8,128)}, u32[]{:S(2)}) copy-start(f32[1,256,256]{2,1,0:T(8,128)} %get-tuple-element.18) | copy-start | bytes 786436
  4.5 24.2 %all-to-all-start = ((f32[32,2,1408]{2,1,0:T(2,128)}), f32[32,2,1408]{2,1,0:T(2,128)S(1)}, u32[]{:S(2)}, u32[]{:S(2)}) async-start(f32[32,2,1408]{2,1,0:T(2,128)} %get-tuple-element.17), calls=%async_computation | async-start | bytes 720896 | tf_op jit(solution)/shard_map/all_to_all | solution.py:311
  17.8 9.8 %collective-permute-start = (f32[1,256,256]{2,1,0:T(8,128)}, f32[1,256,256]{2,1,0:T(8,128)S(1)}, u32[]{:S(2)}, u32[]{:S(2)}) collective-permute-start(f32[1,256,256]{2,1,0:T(8,128)} %get-tuple-element.18), channel_id=1, source_target_pairs={{0,1},{1,0},{2,3},{3,2},{4,5},{5,4},{6,7},{7,6},{8,9},{9,8},{10,11... | collective-permute-start | bytes 786440 | tf_op jit(solution)/shard_map/ppermute | solution.py:308
  20.0 28.7 %collective-permute-start.1 = (f32[1,256,256]{2,1,0:T(8,128)}, f32[1,256,256]{2,1,0:T(8,128)S(1)}, u32[]{:S(2)}, u32[]{:S(2)}) collective-permute-start(f32[1,256,256]{2,1,0:T(8,128)} %get-tuple-element.18), channel_id=1, source_target_pairs={{0,3},{1,2},{2,1},{3,0},{4,7},{5,6},{6,5},{7,4},{8,11},{9,10},{10,... | collective-permute-start | bytes 786440 | tf_op jit(solution)/shard_map/ppermute | solution.py:308
  29.9 24.9 %all-to-all-start.1 = ((f32[24,1,256]{2,1,0:T(1,128)}), f32[24,1,256]{2,1,0:T(1,128)S(1)}, u32[]{:S(2)}, u32[]{:S(2)}) async-start(f32[24,1,256]{2,1,0:T(1,128)} %get-tuple-element.19), calls=%async_computation.1 | async-start | bytes 49152 | tf_op jit(solution)/shard_map/all_to_all | solution.py:313
  44.8 20.8 %collective-permute-start.2 = (f32[1,256,256]{2,1,0:T(8,128)}, f32[1,256,256]{2,1,0:T(8,128)S(1)}, u32[]{:S(2)}, u32[]{:S(2)}) collective-permute-start(f32[1,256,256]{2,1,0:T(8,128)} %get-tuple-element.18), channel_id=1, source_target_pairs={{0,2},{1,3},{2,0},{3,1},{4,6},{5,7},{6,4},{7,5},{8,10},{9,11},{10,... | collective-permute-start | bytes 786440 | tf_op jit(solution)/shard_map/ppermute | solution.py:308
  55.9 21.8 %all-to-all-start.2 = ((f32[32,2,1408]{2,1,0:T(2,128)}), f32[32,2,1408]{2,1,0:T(2,128)S(1)}, u32[]{:S(2)}, u32[]{:S(2)}) async-start(f32[32,2,1408]{2,1,0:T(2,128)} %shard_map.61), calls=%async_computation.2 | async-start | bytes 720896 | tf_op jit(solution)/shard_map/all_to_all | solution.py:316
  65.6 32.8 %copy-start.4 = (bf16[256,256]{1,0:T(8,128)(2,1)S(1)}, bf16[256,256]{1,0:T(8,128)(2,1)}, u32[]{:S(2)}) copy-start(bf16[256,256]{1,0:T(8,128)(2,1)} %student_ref.1) | copy-start | bytes 393220
  67.1 33.5 %collective-permute-start.3 = (f32[4,256,256]{2,1,0:T(8,128)}, f32[4,256,256]{2,1,0:T(8,128)S(1)}, u32[]{:S(2)}, u32[]{:S(2)}) collective-permute-start(f32[4,256,256]{2,1,0:T(8,128)} %constant_dynamic-update-slice_fusion.own_ref), channel_id=1, source_target_pairs={{0,32},{32,0},{64,96},{96,64},{128,160},{160,128},{192,224},{224,1... | collective-permute-start | bytes 3145736 | tf_op jit(solution)/shard_map/ppermute | solution.py:321
  92.8 19.2 %all-to-all-start.4 = ((f32[32,2,1408]{2,1,0:T(2,128)}), f32[32,2,1408]{2,1,0:T(2,128)S(1)}, u32[]{:S(2)}, u32[]{:S(2)}) async-start(f32[32,2,1408]{2,1,0:T(2,128)} %shard_map.63), calls=%async_computation.4 | async-start | bytes 720896 | tf_op jit(solution)/shard_map/all_to_all | solution.py:322
  100.6 19.6 %copy-start = (f32[4,256,256]{2,1,0:T(8,128)}, f32[4,256,256]{2,1,0:T(8,128)S(1)}, u32[]{:S(2)}) copy-start(f32[4,256,256]{2,1,0:T(8,128)S(1)} %collective-permute-done.3.refs_3_.other_ref) | copy-start | bytes 3145732
  113.2 6.9 %copy-start.1 = (f32[22,128]{1,0:T(8,128)}, f32[22,128]{1,0:T(8,128)S(1)}, u32[]{:S(2)}) copy-start(f32[22,128]{1,0:T(8,128)S(1)} %get-tuple-element.22.u_ref) | copy-start | bytes 33796
  113.2 23.3 %all-to-all-start.5 = ((f32[96,2,256]{2,1,0:T(2,128)}), f32[96,2,256]{2,1,0:T(2,128)S(1)}, u32[]{:S(2)}, u32[]{:S(2)}) async-start(f32[96,2,256]{2,1,0:T(2,128)} %get-tuple-element.23.after_ref), calls=%async_computation.5 | async-start | bytes 393216 | tf_op jit(solution)/shard_map/all_to_all | solution.py:327
  136.5 0.7 copy-start.3
  137.2 10.0 %copy-start.2 = (f32[22,128]{1,0:T(8,128)S(1)}, f32[22,128]{1,0:T(8,128)}, u32[]{:S(2)}) copy-start(f32[22,128]{1,0:T(8,128)} %copy-done.1) | copy-start | bytes 33796
  141.7 26.6 %all-to-all-start.6 = ((f32[32,8,768]{2,1,0:T(8,128)}), f32[32,8,768]{2,1,0:T(8,128)S(1)}, u32[]{:S(2)}, u32[]{:S(2)}) async-start(f32[32,8,768]{2,1,0:T(8,128)} %get-tuple-element.29), calls=%async_computation.6 | async-start | bytes 1572864 | tf_op jit(solution)/shard_map/all_to_all | solution.py:333

commit v8 on v7

--- a/solution.py
+++ b/solution.py
@@ -107,15 +107,13 @@
         out_ref[:, start : start + HELD * LANES] = total
 
 
-def start_kernel(teacher_ref, student_ref, proto_ref, gain_ref, mine_ref, proto_n_ref, expo_ref, sent_ref, unit, terms):
+def start_kernel(teacher_ref, proto_ref, gain_ref, expo_ref, sent_ref, unit, proto_n, terms):
     step = pl.program_id(0)
     here = proto_ref.shape[1] // LANES
 
     @pl.when(step == 0)
     def _():
         t = teacher_ref[...].astype(jnp.float32)
-        first = lax.axis_index("proto") % 2 == 0
-        mine_ref[0] = jnp.where(first, t, student_ref[...].astype(jnp.float32))
         unit[...] = (t * lax.rsqrt(jnp.sum(t * t, 1, keepdims=True) + eps)).astype(jnp.bfloat16)
 
     for j in range(here):
@@ -123,8 +121,8 @@
         w = proto_ref[:, span].astype(jnp.float32)
         gains = gain_ref[pl.ds(step * here + j, 1), :]
         w = (w * lax.rsqrt(jnp.sum(w * w, 0, keepdims=True) + eps) * gains).astype(jnp.bfloat16)
-        proto_n_ref[:, span] = w
-    e = jnp.exp(jnp.dot(unit[...], proto_n_ref[...], preferred_element_type=jnp.float32) / teacher_temp)
+        proto_n[:, span] = w
+    e = jnp.exp(jnp.dot(unit[...], proto_n[...], preferred_element_type=jnp.float32) / teacher_temp)
     e = e.astype(jnp.bfloat16)
     cols = proto_ref.shape[1]
     expo_ref[:, pl.ds(pl.multiple_of(step * cols, LANES), cols)] = e
@@ -136,7 +134,7 @@
         sent_ref[...] = jnp.broadcast_to(terms[...][None], sent_ref.shape)
 
 
-def start(teacher, student, prototypes, gain, peers):
+def start(teacher, prototypes, gain, peers):
     rows, depth = teacher.shape
     cols = prototypes.shape[1]
     groups = cols // LANES
@@ -147,28 +145,27 @@
         grid=(steps,),
         in_specs=[
             pl.BlockSpec((rows, depth), lambda i: (0, 0)),
-            pl.BlockSpec((rows, depth), lambda i: (0, 0)),
             pl.BlockSpec((depth, chunk), lambda i: (0, i)),
             pl.BlockSpec((groups, LANES), lambda i: (0, 0)),
         ],
         out_specs=[
-            pl.BlockSpec((1, rows, depth), lambda i: (0, 0, 0)),
-            pl.BlockSpec((depth, chunk), lambda i: (0, i)),
             pl.BlockSpec(memory_space=pltpu.VMEM),
             pl.BlockSpec(memory_space=pltpu.VMEM),
         ],
         out_shape=(
-            jax.ShapeDtypeStruct((1, rows, depth), jnp.float32),
-            jax.ShapeDtypeStruct((depth, cols), jnp.bfloat16),
             pltpu.VMEM((rows, cols), jnp.bfloat16),
             pltpu.VMEM((peers, steps, chunk), jnp.float32),
         ),
-        scratch_shapes=[pltpu.VMEM((rows, depth), jnp.bfloat16), pltpu.VMEM((steps, chunk), jnp.float32)],
+        scratch_shapes=[
+            pltpu.VMEM((rows, depth), jnp.bfloat16),
+            pltpu.VMEM((depth, chunk), jnp.bfloat16),
+            pltpu.VMEM((steps, chunk), jnp.float32),
+        ],
         compiler_params=pltpu.CompilerParams(vmem_limit_bytes=60 * 2**20),
         cost_estimate=pl.CostEstimate(
             flops=2 * rows * depth * cols, bytes_accessed=6 * depth * cols, transcendentals=rows * cols
         ),
-    )(teacher, student, prototypes, gain.reshape(groups, LANES))
+    )(teacher, prototypes, gain.reshape(groups, LANES))
 
 
 def local_call(kernel, operands, waited, out_shape, flops):
@@ -212,7 +209,7 @@
     more = () if total is None else (total,)
     rows = expo.shape[0]
     out_shape = (
-        jax.ShapeDtypeStruct((peers, 1 + len(more), rows), jnp.float32),
+        pltpu.VMEM((peers, 1 + len(more), rows), jnp.float32),
         jax.ShapeDtypeStruct((expo.shape[1] // LANES, LANES), jnp.float32),
     )
     return local_call(row_kernel, (came, expo, *more), waited, out_shape, 2 * expo.size)
@@ -231,7 +228,7 @@
 
 
 def column_terms(came, expo, peers, *waited):
-    out_shape = jax.ShapeDtypeStruct((peers, HALVES, expo.shape[1] // HALVES), jnp.float32)
+    out_shape = pltpu.VMEM((peers, HALVES, expo.shape[1] // HALVES), jnp.float32)
     return local_call(column_kernel, (came, expo), waited, out_shape, 2 * expo.size)
 
 
@@ -302,7 +299,14 @@
     count = cols * npr
     rows_all = rows * nb
 
-    mine, proto_n, expo, sent = start(teacher, student, prototypes, gain, nb)
+    expo, sent = start(teacher, prototypes, gain, nb)
+    core = lax.axis_index("proto") % 2
+    mine = jnp.where(core == 0, teacher.astype(jnp.float32), student.astype(jnp.float32))
+    mine = lax.optimization_barrier(mine)[None]
+    wf = prototypes.astype(jnp.float32)
+    proto_n = (wf * lax.rsqrt(jnp.sum(wf * wf, 0, keepdims=True) + eps) * gain[None, :]).astype(
+        jnp.bfloat16
+    )
 
     def member(rows, flip):
         return lax.ppermute(rows, "batch", [(i, i ^ flip) for i in range(nb)])

time: 170 us -> 174 us (1.024)
  blocking collectives: 12.8 us -> 0 us
  waiting for transfers between devices: 60.4 us -> 69.1 us
  starting transfers between devices: 66.1 us -> 73.2 us
  other arithmetic: 1.66 us -> 7.06 us
  local copies, waits for them, and re-layouts: 4.26 us -> 1.77 us
    all_to_all x1 -> x0, blocking collectives: 12.8 us -> none  [local(): came = lax.all_to_all(sent, 'proto', 0, 0, tiled=True)]
    all_to_all x1 -> x2, waiting for transfers between devices: 5.99 us -> 16.6 us  [local(): came = lax.all_to_all(sent, 'proto', 0, 0, tiled=True)]
    all_to_all x3, waiting for transfers between devices: 21.3 us -> 11.4 us  [local(): came = lax.all_to_all(sent, 'batch', 0, 0, tiled=True)]
    ppermute x3, waiting for transfers between devices: 3.3 us -> 11.3 us  [member(): return lax.ppermute(rows, 'batch', [(i, i ^ flip) for i in range(nb)])]
    all_to_all x1 -> x2, starting transfers between devices: 14.9 us -> 18.7 us  [local(): came = lax.all_to_all(sent, 'proto', 0, 0, tiled=True)]
    all_to_all x3, starting transfers between devices: 27 us -> 29.9 us  [local(): came = lax.all_to_all(sent, 'batch', 0, 0, tiled=True)]
    unnamed x15 -> x14, local copies, waits for them, and re-layouts: 2.86 us -> 1.09 us
  transfers between devices with their start and end apart: 10 -> 11, of which waited for: 7 -> 8; matrix products, arithmetic and copies ran while one was open for 4% -> 5% of each run, Pallas kernels for 6% -> 5%
where the time goes in v8:
time: 174 us; the launch traced here: 173 us
  starting transfers between devices  73.2 us (42%)
  waiting for transfers between devices  69.1 us (40%)
  Pallas kernels  20.5 us (12%)
  other arithmetic  7.06 us (4%)
  local copies, waits for them, and re-layouts  1.77 us (1%)
    all_to_all x3, starting transfers between devices, local(): came = lax.all_to_all(sent, 'batch', 0, 0, tiled=True)  29.9 us
    all_to_all x1, waiting for transfers between devices, local(): parts = lax.all_to_all(grad_t, 'batch', 0, 0, tiled=True)  19.5 us
    all_to_all x2, starting transfers between devices, local(): came = lax.all_to_all(sent, 'proto', 0, 0, tiled=True)  18.7 us
    all_to_all x2, waiting for transfers between devices, local(): came = lax.all_to_all(sent, 'proto', 0, 0, tiled=True)  16.6 us
    all_to_all x3, waiting for transfers between devices, local(): came = lax.all_to_all(sent, 'batch', 0, 0, tiled=True)  11.4 us
    ppermute x3, waiting for transfers between devices, member(): return lax.ppermute(rows, 'batch', [(i, i ^ flip) for i in range(nb)])  11.3 us
    ppermute x3, starting transfers between devices, member(): return lax.ppermute(rows, 'batch', [(i, i ^ flip) for i in range(nb)])  10.4 us
    all_to_all x1, waiting for transfers between devices, local(): lax.all_to_all(sent, ('batch', 'proto'), 0, 0, tiled=True, axis_index_gro...  10.3 us
  transfers between devices with their start and end apart: 11, of which 8 were waited for; matrix products, arithmetic and copies ran while one was open for 5% of the time, Pallas kernels for 5%

profile of v8, /device:TPU:2, one launch (start us, length us, event | category | flops | bytes accessed | tf_op | source)
XLA Modules:
  0.0 173.1 jit_solution(9664777338544963374)
XLA Ops:
  0.6 3.5 %shard_map.59 = (bf16[256,2816]{1,0:T(8,128)(2,1)S(1)}, f32[32,2,1408]{2,1,0:T(2,128)}) custom-call(bf16[256,256]{1,0:T(8,128)(2,1)} %teacher_ref.1, bf16[256,2816]{1,0:T(8,128)(2,1)} %proto_ref.1, f32[22,128]{1,0:T(8,128)} %bitcast.12), custom_call_target="tpu_custom_call" | custom-call | flops 369098752 | bytes 4325376 | tf_op jit(solution)/shard_map/pallas_call | solution.py:143
  4.1 13.1 %all-to-all-start = ((f32[32,2,1408]{2,1,0:T(2,128)}), f32[32,2,1408]{2,1,0:T(2,128)S(1)}, u32[]{:S(2)}, u32[]{:S(2)}) async-start(f32[32,2,1408]{2,1,0:T(2,128)} %get-tuple-element.15), calls=%async_computation | async-start | bytes 720896 | tf_op jit(solution)/shard_map/all_to_all | solution.py:315
  18.3 2.3 %collective-permute-start = (f32[1,256,256]{2,1,0:T(8,128)S(1)}, f32[1,256,256]{2,1,0:T(8,128)S(1)}, u32[]{:S(2)}, u32[]{:S(2)}) collective-permute-start(f32[1,256,256]{2,1,0:T(8,128)S(1)} %bitcast.8), channel_id=1, source_target_pairs={{0,1},{1,0},{2,3},{3,2},{4,5},{5,4},{6,7},{7,6},{8,9},{9,8},{10,11... | collective-permute-start | bytes 786440 | tf_op jit(solution)/shard_map/ppermute | solution.py:312
  20.6 4.2 %collective-permute-start.1 = (f32[1,256,256]{2,1,0:T(8,128)S(1)}, f32[1,256,256]{2,1,0:T(8,128)S(1)}, u32[]{:S(2)}, u32[]{:S(2)}) collective-permute-start(f32[1,256,256]{2,1,0:T(8,128)S(1)} %bitcast.9), channel_id=1, source_target_pairs={{0,3},{1,2},{2,1},{3,0},{4,7},{5,6},{6,5},{7,4},{8,11},{9,10},{10,... | collective-permute-start | bytes 786440 | tf_op jit(solution)/shard_map/ppermute | solution.py:312
  24.8 2.7 %collective-permute-done.refs_2_ = f32[1,256,256]{2,1,0:T(8,128)S(1)} collective-permute-done((f32[1,256,256]{2,1,0:T(8,128)S(1)}, f32[1,256,256]{2,1,0:T(8,128)S(1)}, u32[]{:S(2)}, u32[]{:S(2)}) %collective-permute-start) | collective-permute-done | bytes 262176 | tf_op jit(solution)/shard_map/ppermute | solution.py:312
  29.3 14.9 %all-to-all-start.1 = ((f32[24,1,256]{2,1,0:T(1,128)}), f32[24,1,256]{2,1,0:T(1,128)S(1)}, u32[]{:S(2)}, u32[]{:S(2)}) async-start(f32[24,1,256]{2,1,0:T(1,128)} %get-tuple-element.16), calls=%async_computation.1 | async-start | bytes 49152 | tf_op jit(solution)/shard_map/all_to_all | solution.py:317
  44.2 10.0 %all-to-all-done.1.refs_0_ = f32[24,1,256]{2,1,0:T(1,128)S(1)} async-done(((f32[24,1,256]{2,1,0:T(1,128)}), f32[24,1,256]{2,1,0:T(1,128)S(1)}, u32[]{:S(2)}, u32[]{:S(2)}) %all-to-all-start.1) | async-done | bytes 24608 | tf_op jit(solution)/shard_map/all_to_all | solution.py:317
  55.4 8.7 %all-to-all-start.2 = ((f32[32,2,1408]{2,1,0:T(2,128)}), f32[32,2,1408]{2,1,0:T(2,128)S(1)}, u32[]{:S(2)}, u32[]{:S(2)}) async-start(f32[32,2,1408]{2,1,0:T(2,128)} %shard_map.61), calls=%async_computation.2 | async-start | bytes 720896 | tf_op jit(solution)/shard_map/all_to_all | solution.py:320
  64.1 4.0 %collective-permute-start.2 = (f32[1,256,256]{2,1,0:T(8,128)S(1)}, f32[1,256,256]{2,1,0:T(8,128)S(1)}, u32[]{:S(2)}, u32[]{:S(2)}) collective-permute-start(f32[1,256,256]{2,1,0:T(8,128)S(1)} %bitcast.10), channel_id=1, source_target_pairs={{0,2},{1,3},{2,0},{3,1},{4,6},{5,7},{6,4},{7,5},{8,10},{9,11},{10,... | collective-permute-start | bytes 786440 | tf_op jit(solution)/shard_map/ppermute | solution.py:312
  68.1 1.7 fusion.1
  69.8 8.5 %collective-permute-done.2.refs_2_ = f32[1,256,256]{2,1,0:T(8,128)S(1)} collective-permute-done((f32[1,256,256]{2,1,0:T(8,128)S(1)}, f32[1,256,256]{2,1,0:T(8,128)S(1)}, u32[]{:S(2)}, u32[]{:S(2)}) %collective-permute-start.2) | collective-permute-done | bytes 262176 | tf_op jit(solution)/shard_map/ppermute | solution.py:312
  79.4 3.8 %all-to-all-start.3 = ((f32[24,1,256]{2,1,0:T(1,128)}), f32[24,1,256]{2,1,0:T(1,128)S(1)}, u32[]{:S(2)}, u32[]{:S(2)}) async-start(f32[24,1,256]{2,1,0:T(1,128)} %get-tuple-element.17), calls=%async_computation.3 | async-start | bytes 49152 | tf_op jit(solution)/shard_map/all_to_all | solution.py:323
  84.3 2.2 %collective-permute-start.3 = (f32[4,256,256]{2,1,0:T(8,128)}, f32[4,256,256]{2,1,0:T(8,128)S(1)}, u32[]{:S(2)}, u32[]{:S(2)}) collective-permute-start(f32[4,256,256]{2,1,0:T(8,128)} %pad_maximum_fusion.own_ref), channel_id=1, source_target_pairs={{0,32},{32,0},{64,96},{96,64},{128,160},{160,128},{192,224},{224,1... | collective-permute-start | bytes 3145736 | tf_op jit(solution)/shard_map/ppermute | solution.py:325
  86.6 6.6 %all-to-all-done.3.refs_0_ = f32[24,1,256]{2,1,0:T(1,128)S(1)} async-done(((f32[24,1,256]{2,1,0:T(1,128)}), f32[24,1,256]{2,1,0:T(1,128)S(1)}, u32[]{:S(2)}, u32[]{:S(2)}) %all-to-all-start.3) | async-done | bytes 24608 | tf_op jit(solution)/shard_map/all_to_all | solution.py:323
  94.3 8.2 %all-to-all-start.4 = ((f32[32,2,1408]{2,1,0:T(2,128)}), f32[32,2,1408]{2,1,0:T(2,128)S(1)}, u32[]{:S(2)}, u32[]{:S(2)}) async-start(f32[32,2,1408]{2,1,0:T(2,128)} %shard_map.63), calls=%async_computation.4 | async-start | bytes 720896 | tf_op jit(solution)/shard_map/all_to_all | solution.py:326
  102.5 1.7 fusion.3.proto_ref
  105.3 10.8 %all-to-all-done.4.refs_0_ = f32[32,2,1408]{2,1,0:T(2,128)S(1)} async-done(((f32[32,2,1408]{2,1,0:T(2,128)}), f32[32,2,1408]{2,1,0:T(2,128)S(1)}, u32[]{:S(2)}, u32[]{:S(2)}) %all-to-all-start.4) | async-done | bytes 360480 | tf_op jit(solution)/shard_map/all_to_all | solution.py:326
  117.3 6.9 %all-to-all-start.5 = ((f32[96,2,256]{2,1,0:T(2,128)}), f32[96,2,256]{2,1,0:T(2,128)S(1)}, u32[]{:S(2)}, u32[]{:S(2)}) async-start(f32[96,2,256]{2,1,0:T(2,128)} %get-tuple-element.19.after_ref), calls=%async_computation.5 | async-start | bytes 393216 | tf_op jit(solution)/shard_map/all_to_all | solution.py:331
  124.3 6.0 %shard_map.65 = (bf16[768,1024]{1,0:T(8,128)(2,1)}, f32[768,1024]{1,0:T(8,128)}, bf16[1024,256]{1,0:T(8,128)(2,1)}, f32[22,128]{1,0:T(8,128)}) custom-call(f32[4,256,256]{2,1,0:T(8,128)} %pad_maximum_fusion.own_ref, f32[4,256,256]{2,1,0:T(8,128)} %copy-done, bf16[256,2816]{1,0:T(8,128)(2,1)} %copy-done.3, f32[22,128]{1,0:T(8,128)} %copy-done.1, ...), custom_call_target="tpu_custom_call" | custom-call | flops 805306368 | bytes 10485760 | tf_op jit(solution)/shard_map/pallas_call | solution.py:260
  130.3 10.3 %all-to-all-done.5.refs_10_ = f32[96,2,256]{2,1,0:T(2,128)S(1)} async-done(((f32[96,2,256]{2,1,0:T(2,128)}), f32[96,2,256]{2,1,0:T(2,128)S(1)}, u32[]{:S(2)}, u32[]{:S(2)}) %all-to-all-start.5) | async-done | bytes 196640 | tf_op jit(solution)/shard_map/all_to_all | solution.py:331
  141.4 4.5 %shard_map.66 = (f32[32,8,768]{2,1,0:T(8,128)}, f32[2,256]{1,0:T(2,128)}) custom-call(bf16[768,1024]{1,0:T(8,128)(2,1)} %get-tuple-element.20.refs_0_.refs_1_.refs_2_.refs_3_, bf16[768,1024]{1,0:T(8,128)(2,1)} %get-tuple-element.20.refs_0_.refs_1_.refs_2_.refs_3_, bf16[768,1024]{1,0:T(8,128)(2,1)} %get-tuple-element.20.refs_0_.refs_1_.refs_2_.refs_3_, ...), custom_call_target="tpu_custom_call" | custom-call | flops 402653184 | bytes 4718592 | tf_op jit(solution)/shard_map/pallas_call | solution.py:73
  145.9 4.9 %all-to-all-start.6 = ((f32[32,8,768]{2,1,0:T(8,128)}), f32[32,8,768]{2,1,0:T(8,128)S(1)}, u32[]{:S(2)}, u32[]{:S(2)}) async-start(f32[32,8,768]{2,1,0:T(8,128)} %get-tuple-element.25), calls=%async_computation.6 | async-start | bytes 1572864 | tf_op jit(solution)/shard_map/all_to_all | solution.py:337
  151.4 1.5 multiply_convert_fusion
  152.9 19.5 %all-to-all-done.6.parts_ref = f32[32,8,768]{2,1,0:T(8,128)S(1)} async-done(((f32[32,8,768]{2,1,0:T(8,128)}), f32[32,8,768]{2,1,0:T(8,128)S(1)}, u32[]{:S(2)}, u32[]{:S(2)}) %all-to-all-start.6) | async-done | bytes 786464 | tf_op jit(solution)/shard_map/all_to_all | solution.py:337
  (30 shorter events, 11.8 us)
Async XLA Ops:
  4.1 24.0 %all-to-all-start = ((f32[32,2,1408]{2,1,0:T(2,128)}), f32[32,2,1408]{2,1,0:T(2,128)S(1)}, u32[]{:S(2)}, u32[]{:S(2)}) async-start(f32[32,2,1408]{2,1,0:T(2,128)} %get-tuple-element.15), calls=%async_computation | async-start | bytes 720896 | tf_op jit(solution)/shard_map/all_to_all | solution.py:315
  18.3 9.2 %collective-permute-start = (f32[1,256,256]{2,1,0:T(8,128)S(1)}, f32[1,256,256]{2,1,0:T(8,128)S(1)}, u32[]{:S(2)}, u32[]{:S(2)}) collective-permute-start(f32[1,256,256]{2,1,0:T(8,128)S(1)} %bitcast.8), channel_id=1, source_target_pairs={{0,1},{1,0},{2,3},{3,2},{4,5},{5,4},{6,7},{7,6},{8,9},{9,8},{10,11... | collective-permute-start | bytes 786440 | tf_op jit(solution)/shard_map/ppermute | solution.py:312
  20.6 23.6 %collective-permute-start.1 = (f32[1,256,256]{2,1,0:T(8,128)S(1)}, f32[1,256,256]{2,1,0:T(8,128)S(1)}, u32[]{:S(2)}, u32[]{:S(2)}) collective-permute-start(f32[1,256,256]{2,1,0:T(8,128)S(1)} %bitcast.9), channel_id=1, source_target_pairs={{0,3},{1,2},{2,1},{3,0},{4,7},{5,6},{6,5},{7,4},{8,11},{9,10},{10,... | collective-permute-start | bytes 786440 | tf_op jit(solution)/shard_map/ppermute | solution.py:312
  29.3 24.9 %all-to-all-start.1 = ((f32[24,1,256]{2,1,0:T(1,128)}), f32[24,1,256]{2,1,0:T(1,128)S(1)}, u32[]{:S(2)}, u32[]{:S(2)}) async-start(f32[24,1,256]{2,1,0:T(1,128)} %get-tuple-element.16), calls=%async_computation.1 | async-start | bytes 49152 | tf_op jit(solution)/shard_map/all_to_all | solution.py:317
  55.4 22.9 %all-to-all-start.2 = ((f32[32,2,1408]{2,1,0:T(2,128)}), f32[32,2,1408]{2,1,0:T(2,128)S(1)}, u32[]{:S(2)}, u32[]{:S(2)}) async-start(f32[32,2,1408]{2,1,0:T(2,128)} %shard_map.61), calls=%async_computation.2 | async-start | bytes 720896 | tf_op jit(solution)/shard_map/all_to_all | solution.py:320
  64.1 14.2 %collective-permute-start.2 = (f32[1,256,256]{2,1,0:T(8,128)S(1)}, f32[1,256,256]{2,1,0:T(8,128)S(1)}, u32[]{:S(2)}, u32[]{:S(2)}) collective-permute-start(f32[1,256,256]{2,1,0:T(8,128)S(1)} %bitcast.10), channel_id=1, source_target_pairs={{0,2},{1,3},{2,0},{3,1},{4,6},{5,7},{6,4},{7,5},{8,10},{9,11},{10,... | collective-permute-start | bytes 786440 | tf_op jit(solution)/shard_map/ppermute | solution.py:312
  69.7 32.8 %copy-start.6 = (f32[2816]{0:T(1024)S(1)}, f32[2816]{0:T(1024)}, u32[]{:S(2)}) copy-start(f32[2816]{0:T(1024)} %param.7) | copy-start | bytes 33796
  79.4 13.7 %all-to-all-start.3 = ((f32[24,1,256]{2,1,0:T(1,128)}), f32[24,1,256]{2,1,0:T(1,128)S(1)}, u32[]{:S(2)}, u32[]{:S(2)}) async-start(f32[24,1,256]{2,1,0:T(1,128)} %get-tuple-element.17), calls=%async_computation.3 | async-start | bytes 49152 | tf_op jit(solution)/shard_map/all_to_all | solution.py:323
  84.3 19.9 %copy-start.5 = (bf16[256,256]{1,0:T(8,128)(2,1)S(1)}, bf16[256,256]{1,0:T(8,128)(2,1)}, u32[]{:S(2)}) copy-start(bf16[256,256]{1,0:T(8,128)(2,1)} %param.5) | copy-start | bytes 393220
  84.3 21.0 %collective-permute-start.3 = (f32[4,256,256]{2,1,0:T(8,128)}, f32[4,256,256]{2,1,0:T(8,128)S(1)}, u32[]{:S(2)}, u32[]{:S(2)}) collective-permute-start(f32[4,256,256]{2,1,0:T(8,128)} %pad_maximum_fusion.own_ref), channel_id=1, source_target_pairs={{0,32},{32,0},{64,96},{96,64},{128,160},{160,128},{192,224},{224,1... | collective-permute-start | bytes 3145736 | tf_op jit(solution)/shard_map/ppermute | solution.py:325
  94.3 21.8 %all-to-all-start.4 = ((f32[32,2,1408]{2,1,0:T(2,128)}), f32[32,2,1408]{2,1,0:T(2,128)S(1)}, u32[]{:S(2)}, u32[]{:S(2)}) async-start(f32[32,2,1408]{2,1,0:T(2,128)} %shard_map.63), calls=%async_computation.4 | async-start | bytes 720896 | tf_op jit(solution)/shard_map/all_to_all | solution.py:326
  104.2 1.1 copy-start.3
  105.3 19.0 %copy-start = (f32[4,256,256]{2,1,0:T(8,128)}, f32[4,256,256]{2,1,0:T(8,128)S(1)}, u32[]{:S(2)}) copy-start(f32[4,256,256]{2,1,0:T(8,128)S(1)} %collective-permute-done.3.refs_3_.other_ref) | copy-start | bytes 3145732
  117.3 7.0 %copy-start.1 = (f32[22,128]{1,0:T(8,128)}, f32[22,128]{1,0:T(8,128)S(1)}, u32[]{:S(2)}) copy-start(f32[22,128]{1,0:T(8,128)S(1)} %get-tuple-element.18.u_ref) | copy-start | bytes 33796
  117.3 23.3 %all-to-all-start.5 = ((f32[96,2,256]{2,1,0:T(2,128)}), f32[96,2,256]{2,1,0:T(2,128)S(1)}, u32[]{:S(2)}, u32[]{:S(2)}) async-start(f32[96,2,256]{2,1,0:T(2,128)} %get-tuple-element.19.after_ref), calls=%async_computation.5 | async-start | bytes 393216 | tf_op jit(solution)/shard_map/all_to_all | solution.py:331
  140.7 0.7 copy-start.4
  141.4 10.0 %copy-start.2 = (f32[22,128]{1,0:T(8,128)S(1)}, f32[22,128]{1,0:T(8,128)}, u32[]{:S(2)}) copy-start(f32[22,128]{1,0:T(8,128)} %copy-done.1) | copy-start | bytes 33796
  145.9 26.6 %all-to-all-start.6 = ((f32[32,8,768]{2,1,0:T(8,128)}), f32[32,8,768]{2,1,0:T(8,128)S(1)}, u32[]{:S(2)}, u32[]{:S(2)}) async-start(f32[32,8,768]{2,1,0:T(8,128)} %get-tuple-element.25), calls=%async_computation.6 | async-start | bytes 1572864 | tf_op jit(solution)/shard_map/all_to_all | solution.py:337

commit v9 on v7

--- a/solution.py
+++ b/solution.py
@@ -33,7 +33,7 @@
 
 def grad_kernel(count, scale, *refs):
     exps, student_exps = refs[:SPLIT], refs[SPLIT : 2 * SPLIT]
-    student_ref, u_ref, came_ref, out_ref, own_ref, diff = refs[2 * SPLIT :]
+    student_ref, u_ref, came_ref, totals_ref, out_ref, own_ref, diff = refs[2 * SPLIT :]
     senders = came_ref.shape[0] // TEAM
     rows = came_ref.shape[2]
     chunk = diff.shape[0]
@@ -47,9 +47,10 @@
         if place == 0:
             own_ref[...] = by
         by = by * count
+        inv_totals = count / totals_ref[me ^ place]
         for first in range(0, rows, LANES):
-            v = by[0:1, first : first + LANES]
-            inv_total = by[1:2, first : first + LANES]
+            v = by[:, first : first + LANES]
+            inv_total = inv_totals[first // LANES : first // LANES + 1, :]
             span = slice(place * rows + first, place * rows + first + LANES)
             for i in range(SPLIT):
                 part = slice(i * piece, (i + 1) * piece)
@@ -60,7 +61,7 @@
     out_ref[...] = (product.T * scale).reshape(out_ref.shape)
 
 
-def partial_grad(expo_t, student_exp_t, student, u, came, count, scale, owners):
+def partial_grad(expo_t, student_exp_t, student, u, came, totals, count, scale, owners):
     part, crops = expo_t.shape
     depth = student.shape[1]
     steps = 2
@@ -79,6 +80,7 @@
             pl.BlockSpec(student.shape, lambda i: (0, 0)),
             pl.BlockSpec(u.shape, lambda i: (0, 0)),
             pl.BlockSpec(came.shape, lambda i: (0, 0, 0)),
+            pl.BlockSpec(totals.shape, lambda i: (0, 0, 0)),
         ],
         out_specs=[
             pl.BlockSpec((owners, depth // owners, chunk), lambda i: (0, 0, i)),
@@ -93,7 +95,7 @@
         cost_estimate=pl.CostEstimate(
             flops=2 * part * crops * depth, bytes_accessed=6 * part * crops, transcendentals=0
         ),
-    )(*[expo_t] * SPLIT, *[student_exp_t] * SPLIT, student, u, came)
+    )(*[expo_t] * SPLIT, *[student_exp_t] * SPLIT, student, u, came, totals)
 
 
 def join_kernel(parts_ref, out_ref):
@@ -186,52 +188,66 @@
     )(*operands, *waited)
 
 
-def row_kernel(came_ref, expo_ref, *refs):
-    total_ref, (sent_ref, u_ref) = (refs[0] if len(refs) == 3 else None), refs[-2:]
-    u = 1.0 / jnp.sum(came_ref[...], 0)
-    half = u.shape[1] // LANES
-    for j in range(u_ref.shape[0]):
+def row_kernel(has_total, came_ref, expo_ref, *refs):
+    total_ref = refs[0] if has_total else None
+    sent_ref, u_ref, *team_ref = refs[1:] if has_total else refs
+    groups = u_ref.shape[0]
+    half = groups // HALVES
+    u = 1.0 / jnp.sum(came_ref[:, :, : half * LANES], 0)
+    for j in range(groups):
         u_ref[j : j + 1, :] = u[j // half : j // half + 1, j % half * LANES : (j % half + 1) * LANES]
+    if team_ref:
+        first = lax.axis_index("batch") // TEAM * TEAM
+        team_ref[0][...] = came_ref[pl.ds(first, TEAM), :, half * LANES :]
     rows = expo_ref.shape[0]
     block = 64
     sums = []
     for first in range(0, rows, block):
         acc = jnp.zeros((block, LANES), jnp.float32)
-        for j in range(u_ref.shape[0]):
+        for j in range(groups):
             e = expo_ref[first : first + block, j * LANES : (j + 1) * LANES].astype(jnp.float32)
             acc += e * u_ref[j : j + 1, :]
         sums.append(acc)
     r = jnp.sum(jnp.concatenate(sums, 0).T, 0, keepdims=True)
     peers = sent_ref.shape[0]
     sent_ref[:, 0:1, :] = jnp.broadcast_to(r[None], (peers, 1, rows))
-    if total_ref is not None:
+    if has_total:
         sent_ref[:, 1:2, :] = jnp.broadcast_to(total_ref[...][None], (peers, 1, rows))
 
 
 def row_terms(came, expo, peers, *waited, total=None):
     more = () if total is None else (total,)
-    rows = expo.shape[0]
+    rows, cols = expo.shape
+    extra = came.shape[2] - cols // HALVES
     out_shape = (
         jax.ShapeDtypeStruct((peers, 1 + len(more), rows), jnp.float32),
-        jax.ShapeDtypeStruct((expo.shape[1] // LANES, LANES), jnp.float32),
+        jax.ShapeDtypeStruct((cols // LANES, LANES), jnp.float32),
     )
-    return local_call(row_kernel, (came, expo, *more), waited, out_shape, 2 * expo.size)
+    if extra:
+        out_shape += (jax.ShapeDtypeStruct((TEAM, HALVES, extra), jnp.float32),)
+    kernel = functools.partial(row_kernel, bool(more))
+    return local_call(kernel, (came, expo, *more), waited, out_shape, 2 * expo.size)
 
 
 def column_kernel(came_ref, expo_ref, sent_ref):
     rows = expo_ref.shape[0]
-    v = 1.0 / jnp.sum(came_ref[...], 0)
-    v = jnp.broadcast_to(v, (LANES, rows)).T
-    peers, halves, cols = sent_ref.shape
+    got = jnp.sum(came_ref[...], 0)
+    v = jnp.broadcast_to(1.0 / got[0:1], (LANES, rows)).T
+    peers, halves, width = sent_ref.shape
+    cols = expo_ref.shape[1] // halves
     for h in range(halves):
         for first in range(0, cols, LANES):
             e = expo_ref[:, h * cols + first : h * cols + first + LANES].astype(jnp.float32)
             sent_ref[0, h : h + 1, first : first + LANES] = jnp.sum(e * v, 0, keepdims=True)
-    sent_ref[1:] = jnp.broadcast_to(sent_ref[0:1], (peers - 1, halves, cols))
+    if width > cols:
+        for h in range(halves):
+            sent_ref[0, h : h + 1, cols:] = got[1:2, h * (width - cols) : (h + 1) * (width - cols)]
+    sent_ref[1:] = jnp.broadcast_to(sent_ref[0:1], (peers - 1, halves, width))
 
 
 def column_terms(came, expo, peers, *waited):
-    out_shape = jax.ShapeDtypeStruct((peers, HALVES, expo.shape[1] // HALVES), jnp.float32)
+    extra = (came.shape[1] - 1) * came.shape[2]
+    out_shape = jax.ShapeDtypeStruct((peers, HALVES, (expo.shape[1] + extra) // HALVES), jnp.float32)
     return local_call(column_kernel, (came, expo), waited, out_shape, 2 * expo.size)
 
 
@@ -304,6 +320,9 @@
 
     mine, proto_n, expo, sent = start(teacher, student, prototypes, gain, nb)
 
+    logits = jnp.dot(unit_rows(student), proto_n, preferred_element_type=jnp.float32)
+    local_total = jnp.sum(jnp.exp(logits / student_temp), 1)
+
     def member(rows, flip):
         return lax.ppermute(rows, "batch", [(i, i ^ flip) for i in range(nb)])
 
@@ -314,21 +333,19 @@
     sent = column_terms(came, expo, nb, held[3])
     held[2] = member(mine, 2)
     came = lax.all_to_all(sent, "batch", 0, 0, tiled=True)
-    sent, _ = row_terms(came, expo, npr, held[2])
+    sent, _ = row_terms(came, expo, npr, held[2], total=local_total[None])
     own = jnp.concatenate(held)
     came = lax.all_to_all(sent, "proto", 0, 0, tiled=True)
     sent = column_terms(came, expo, nb)
     other = lax.ppermute(own, "proto", [(i, i ^ 1) for i in range(npr)])
     came = lax.all_to_all(sent, "batch", 0, 0, tiled=True)
 
-    logits = jnp.dot(unit_rows(student), proto_n, preferred_element_type=jnp.float32)
-    local_total = jnp.sum(jnp.exp(logits / student_temp), 1)
-    sent, scale_u = row_terms(came, expo, TEAM * npr, other, total=local_total[None])
+    sent, scale_u, totals = row_terms(came, expo, TEAM * npr, other)
     came = lax.all_to_all(sent, ("batch", "proto"), 0, 0, tiled=True, axis_index_groups=rows_of_chips)
     team_values = team_products(own, other, proto_n, scale_u, sent)
 
     inv_root = 1.0 / rows_all**0.5
-    grad_t, inverse = partial_grad(*team_values, came, float(count), inv_root, nb)
+    grad_t, inverse = partial_grad(*team_values, came, totals, float(count), inv_root, nb)
     scale_v = inverse[0]
     parts = lax.all_to_all(grad_t, "batch", 0, 0, tiled=True)
     grad = pl.pallas_call(

time: 170 us -> 170 us (level)
    all_to_all x1, waiting for transfers between devices: 5.99 us -> 9.96 us  [local(): came = lax.all_to_all(sent, 'proto', 0, 0, tiled=True)]
    all_to_all x1, waiting for transfers between devices: 10.3 us -> 7.22 us  [local(): lax.all_to_all(sent, ('batch', 'proto'), 0, 0, tiled=True, axis_index_gro...]
    ppermute x3, waiting for transfers between devices: 3.3 us -> 0.88 us  [member(): return lax.ppermute(rows, 'batch', [(i, i ^ flip) for i in range(nb)])]
  transfers between devices with their start and end apart: 10 -> 10, of which waited for: 7 -> 6; matrix products, arithmetic and copies ran while one was open for 4% -> 5% of each run, Pallas kernels for 6% -> 6%
where the time goes in v9:
time: 170 us; the launch traced here: 169 us
  starting transfers between devices  65.7 us (39%)
  waiting for transfers between devices  59.1 us (35%)
  Pallas kernels  20.8 us (12%)
  blocking collectives  13.3 us (8%)
  local copies, waits for them, and re-layouts  4.12 us (2%)
  other arithmetic  3.24 us (2%)
  matrix products  2.04 us (1%)
    all_to_all x3, starting transfers between devices, local(): came = lax.all_to_all(sent, 'batch', 0, 0, tiled=True)  28 us
    all_to_all x3, waiting for transfers between devices, local(): came = lax.all_to_all(sent, 'batch', 0, 0, tiled=True)  21 us
    all_to_all x1, waiting for transfers between devices, local(): parts = lax.all_to_all(grad_t, 'batch', 0, 0, tiled=True)  20.1 us
    all_to_all x1, starting transfers between devices, local(): came = lax.all_to_all(sent, 'proto', 0, 0, tiled=True)  14.2 us
    all_to_all x1, blocking collectives, local(): came = lax.all_to_all(sent, 'proto', 0, 0, tiled=True)  13.3 us
    all_to_all x1, waiting for transfers between devices, local(): came = lax.all_to_all(sent, 'proto', 0, 0, tiled=True)  9.96 us
    ppermute x3, starting transfers between devices, member(): return lax.ppermute(rows, 'batch', [(i, i ^ flip) for i in range(nb)])  9.82 us
    all_to_all x1, waiting for transfers between devices, local(): lax.all_to_all(sent, ('batch', 'proto'), 0, 0, tiled=True, axis_index_gro...  7.22 us
  transfers between devices with their start and end apart: 10, of which 6 were waited for; matrix products, arithmetic and copies ran while one was open for 5% of the time, Pallas kernels for 6%

profile of v9, /device:TPU:2, one launch (start us, length us, event | category | flops | bytes accessed | tf_op | source)
XLA Modules:
  0.0 169.1 jit_solution(10633716471633262134)
XLA Ops:
  0.6 3.9 %shard_map.59 = (f32[1,256,256]{2,1,0:T(8,128)}, bf16[256,2816]{1,0:T(8,128)(2,1)}, bf16[256,2816]{1,0:T(8,128)(2,1)S(1)}, f32[32,2,1408]{2,1,0:T(2,128)}) custom-call(bf16[256,256]{1,0:T(8,128)(2,1)} %teacher_ref.1, bf16[256,256]{1,0:T(8,128)(2,1)} %student_ref.1, bf16[256,2816]{1,0:T(8,128)(2,1)} %proto_ref.1, f32[22,128]{1,0:T(8,128)} %bitcast.7), custom_call_target="tpu_custom_call" | custom-call | flops 369098752 | bytes 4325376 | tf_op jit(solution)/shard_map/pallas_call | solution.py:147
  4.5 13.2 %all-to-all-start = ((f32[32,2,1408]{2,1,0:T(2,128)}), f32[32,2,1408]{2,1,0:T(2,128)S(1)}, u32[]{:S(2)}, u32[]{:S(2)}) async-start(f32[32,2,1408]{2,1,0:T(2,128)} %get-tuple-element.18), calls=%async_computation | async-start | bytes 720896 | tf_op jit(solution)/shard_map/all_to_all | solution.py:330
  17.8 2.3 %collective-permute-start = (f32[1,256,256]{2,1,0:T(8,128)}, f32[1,256,256]{2,1,0:T(8,128)S(1)}, u32[]{:S(2)}, u32[]{:S(2)}) collective-permute-start(f32[1,256,256]{2,1,0:T(8,128)} %get-tuple-element.19), channel_id=1, source_target_pairs={{0,1},{1,0},{2,3},{3,2},{4,5},{5,4},{6,7},{7,6},{8,9},{9,8},{10,11... | collective-permute-start | bytes 786440 | tf_op jit(solution)/shard_map/ppermute | solution.py:327
  20.0 4.2 %collective-permute-start.1 = (f32[1,256,256]{2,1,0:T(8,128)}, f32[1,256,256]{2,1,0:T(8,128)S(1)}, u32[]{:S(2)}, u32[]{:S(2)}) collective-permute-start(f32[1,256,256]{2,1,0:T(8,128)} %get-tuple-element.19), channel_id=1, source_target_pairs={{0,3},{1,2},{2,1},{3,0},{4,7},{5,6},{6,5},{7,4},{8,11},{9,10},{10,... | collective-permute-start | bytes 786440 | tf_op jit(solution)/shard_map/ppermute | solution.py:327
  24.2 3.4 %collective-permute-start.2 = (f32[1,256,256]{2,1,0:T(8,128)}, f32[1,256,256]{2,1,0:T(8,128)S(1)}, u32[]{:S(2)}, u32[]{:S(2)}) collective-permute-start(f32[1,256,256]{2,1,0:T(8,128)} %get-tuple-element.19), channel_id=1, source_target_pairs={{0,2},{1,3},{2,0},{3,1},{4,6},{5,7},{6,4},{7,5},{8,10},{9,11},{10,... | collective-permute-start | bytes 786440 | tf_op jit(solution)/shard_map/ppermute | solution.py:327
  30.7 14.2 %all-to-all-start.1 = ((f32[24,1,256]{2,1,0:T(1,128)}), f32[24,1,256]{2,1,0:T(1,128)S(1)}, u32[]{:S(2)}, u32[]{:S(2)}) async-start(f32[24,1,256]{2,1,0:T(1,128)} %get-tuple-element.20), calls=%async_computation.1 | async-start | bytes 49152 | tf_op jit(solution)/shard_map/all_to_all | solution.py:332
  44.9 10.0 %all-to-all-done.1.refs_0_ = f32[24,1,256]{2,1,0:T(1,128)S(1)} async-done(((f32[24,1,256]{2,1,0:T(1,128)}), f32[24,1,256]{2,1,0:T(1,128)S(1)}, u32[]{:S(2)}, u32[]{:S(2)}) %all-to-all-start.1) | async-done | bytes 24608 | tf_op jit(solution)/shard_map/all_to_all | solution.py:332
  54.9 1.2 shard_map.61
  56.1 9.3 %all-to-all-start.2 = ((f32[32,2,1408]{2,1,0:T(2,128)}), f32[32,2,1408]{2,1,0:T(2,128)S(1)}, u32[]{:S(2)}, u32[]{:S(2)}) async-start(f32[32,2,1408]{2,1,0:T(2,128)} %shard_map.61), calls=%async_computation.2 | async-start | bytes 720896 | tf_op jit(solution)/shard_map/all_to_all | solution.py:335
  68.2 1.9 %collective-permute-start.3 = (f32[4,256,256]{2,1,0:T(8,128)}, f32[4,256,256]{2,1,0:T(8,128)S(1)}, u32[]{:S(2)}, u32[]{:S(2)}) collective-permute-start(f32[4,256,256]{2,1,0:T(8,128)} %constant_dynamic-update-slice_fusion.own_ref), channel_id=1, source_target_pairs={{0,32},{32,0},{64,96},{96,64},{128,160},{160,128},{192,224},{224,1... | collective-permute-start | bytes 3145736 | tf_op jit(solution)/shard_map/ppermute | solution.py:340
  70.1 2.0 %fusion.1 = f32[256]{0:T(256)S(1)} fusion(bf16[256,2816]{1,0:T(8,128)(2,1)} %get-tuple-element.21.proto_ref, bf16[256,256]{1,0:T(8,128)(2,1)S(1)} %copy-done.4, f32[256]{0:T(256)S(1)} %add_rsqrt_fusion), kind=kOutput, calls=%fused_computation.3 | convolution fusion | flops 370736896 | bytes 1574912 | tf_op jit(solution)/shard_map/dot_general | solution.py:323
  72.2 6.8 %all-to-all-done.2.refs_0_ = f32[32,2,1408]{2,1,0:T(2,128)S(1)} async-done(((f32[32,2,1408]{2,1,0:T(2,128)}), f32[32,2,1408]{2,1,0:T(2,128)S(1)}, u32[]{:S(2)}, u32[]{:S(2)}) %all-to-all-start.2) | async-done | bytes 360480 | tf_op jit(solution)/shard_map/all_to_all | solution.py:335
  80.0 13.3 %all_to_all.35.refs_0_ = f32[24,2,256]{2,1,0:T(2,128)S(1)} all-to-all(f32[24,2,256]{2,1,0:T(2,128)S(1)} %get-tuple-element.22), channel_id=1, replica_groups=mesh['proto'=24,'batch'=32] {'proto'}, dimensions={0} | all-to-all | bytes 98304 | tf_op jit(solution)/shard_map/all_to_all | solution.py:338
  93.2 1.2 shard_map.63
  94.4 5.6 %all-to-all-start.4 = ((f32[32,2,1536]{2,1,0:T(2,128)}), f32[32,2,1536]{2,1,0:T(2,128)S(1)}, u32[]{:S(2)}, u32[]{:S(2)}) async-start(f32[32,2,1536]{2,1,0:T(2,128)} %shard_map.63), calls=%async_computation.4 | async-start | bytes 786432 | tf_op jit(solution)/shard_map/all_to_all | solution.py:341
  100.0 14.2 %all-to-all-done.4.refs_0_ = f32[32,2,1536]{2,1,0:T(2,128)S(1)} async-done(((f32[32,2,1536]{2,1,0:T(2,128)}), f32[32,2,1536]{2,1,0:T(2,128)S(1)}, u32[]{:S(2)}, u32[]{:S(2)}) %all-to-all-start.4) | async-done | bytes 393248 | tf_op jit(solution)/shard_map/all_to_all | solution.py:341
  114.2 1.2 shard_map.64
  116.0 6.8 %all-to-all-start.5 = ((f32[96,1,256]{2,1,0:T(1,128)}), f32[96,1,256]{2,1,0:T(1,128)S(1)}, u32[]{:S(2)}, u32[]{:S(2)}) async-start(f32[96,1,256]{2,1,0:T(1,128)} %get-tuple-element.24.after_ref), calls=%async_computation.5 | async-start | bytes 196608 | tf_op jit(solution)/shard_map/all_to_all | solution.py:344
  122.8 6.0 %shard_map.65 = (bf16[768,1024]{1,0:T(8,128)(2,1)}, f32[768,1024]{1,0:T(8,128)}, bf16[1024,256]{1,0:T(8,128)(2,1)}, f32[22,128]{1,0:T(8,128)}) custom-call(f32[4,256,256]{2,1,0:T(8,128)} %constant_dynamic-update-slice_fusion.own_ref, f32[4,256,256]{2,1,0:T(8,128)} %copy-done, bf16[256,2816]{1,0:T(8,128)(2,1)} %get-tuple-element.21.proto_ref, ...), custom_call_target="tpu_custom_call" | custom-call | flops 805306368 | bytes 10485760 | tf_op jit(solution)/shard_map/pallas_call | solution.py:279
  128.9 7.2 %all-to-all-done.5.refs_10_ = f32[96,1,256]{2,1,0:T(1,128)S(1)} async-done(((f32[96,1,256]{2,1,0:T(1,128)}), f32[96,1,256]{2,1,0:T(1,128)S(1)}, u32[]{:S(2)}, u32[]{:S(2)}) %all-to-all-start.5) | async-done | bytes 98336 | tf_op jit(solution)/shard_map/all_to_all | solution.py:344
  136.7 4.5 %shard_map.66 = (f32[32,8,768]{2,1,0:T(8,128)}, f32[1,256]{1,0:T(1,128)}) custom-call(bf16[768,1024]{1,0:T(8,128)(2,1)} %get-tuple-element.25.refs_0_.refs_1_.refs_2_.refs_3_, bf16[768,1024]{1,0:T(8,128)(2,1)} %get-tuple-element.25.refs_0_.refs_1_.refs_2_.refs_3_, bf16[768,1024]{1,0:T(8,128)(2,1)} %get-tuple-element.25.refs_0_.refs_1_.refs_2_.refs_3_, ...), custom_call_target="tpu_custom_call" | custom-call | flops 402653184 | bytes 4718592 | tf_op jit(solution)/shard_map/pallas_call | solution.py:74
  141.2 4.9 %all-to-all-start.6 = ((f32[32,8,768]{2,1,0:T(8,128)}), f32[32,8,768]{2,1,0:T(8,128)S(1)}, u32[]{:S(2)}, u32[]{:S(2)}) async-start(f32[32,8,768]{2,1,0:T(8,128)} %get-tuple-element.31), calls=%async_computation.6 | async-start | bytes 1572864 | tf_op jit(solution)/shard_map/all_to_all | solution.py:350
  146.1 2.2 %multiply_convert_fusion = bf16[256,2816]{1,0:T(8,128)(2,1)} fusion(bf16[256,2816]{1,0:T(8,128)(2,1)S(1)} %get-tuple-element.17.refs_1_, f32[256]{0:T(256)} %bitcast.8, f32[2816]{0:T(1024)S(1)} %bitcast.5), kind=kLoop, calls=%fused_computation.2 | loop fusion | flops 3604480 | bytes 2895872 | tf_op jit(solution)/shard_map/convert_element_type | solution.py:359
  148.3 20.1 %all-to-all-done.6.parts_ref = f32[32,8,768]{2,1,0:T(8,128)S(1)} async-done(((f32[32,8,768]{2,1,0:T(8,128)}), f32[32,8,768]{2,1,0:T(8,128)S(1)}, u32[]{:S(2)}, u32[]{:S(2)}) %all-to-all-start.6) | async-done | bytes 786464 | tf_op jit(solution)/shard_map/all_to_all | solution.py:350
  (28 shorter events, 8.9 us)
Async XLA Ops:
  4.5 60.8 %copy-start.6 = (f32[1,256,256]{2,1,0:T(8,128)S(1)}, f32[1,256,256]{2,1,0:T(8,128)}, u32[]{:S(2)}) copy-start(f32[1,256,256]{2,1,0:T(8,128)} %get-tuple-element.19) | copy-start | bytes 786436
  4.5 25.0 %all-to-all-start = ((f32[32,2,1408]{2,1,0:T(2,128)}), f32[32,2,1408]{2,1,0:T(2,128)S(1)}, u32[]{:S(2)}, u32[]{:S(2)}) async-start(f32[32,2,1408]{2,1,0:T(2,128)} %get-tuple-element.18), calls=%async_computation | async-start | bytes 720896 | tf_op jit(solution)/shard_map/all_to_all | solution.py:330
  17.8 11.7 %collective-permute-start = (f32[1,256,256]{2,1,0:T(8,128)}, f32[1,256,256]{2,1,0:T(8,128)S(1)}, u32[]{:S(2)}, u32[]{:S(2)}) collective-permute-start(f32[1,256,256]{2,1,0:T(8,128)} %get-tuple-element.19), channel_id=1, source_target_pairs={{0,1},{1,0},{2,3},{3,2},{4,5},{5,4},{6,7},{7,6},{8,9},{9,8},{10,11... | collective-permute-start | bytes 786440 | tf_op jit(solution)/shard_map/ppermute | solution.py:327
  20.0 24.9 %collective-permute-start.1 = (f32[1,256,256]{2,1,0:T(8,128)}, f32[1,256,256]{2,1,0:T(8,128)S(1)}, u32[]{:S(2)}, u32[]{:S(2)}) collective-permute-start(f32[1,256,256]{2,1,0:T(8,128)} %get-tuple-element.19), channel_id=1, source_target_pairs={{0,3},{1,2},{2,1},{3,0},{4,7},{5,6},{6,5},{7,4},{8,11},{9,10},{10,... | collective-permute-start | bytes 786440 | tf_op jit(solution)/shard_map/ppermute | solution.py:327
  24.2 42.5 %collective-permute-start.2 = (f32[1,256,256]{2,1,0:T(8,128)}, f32[1,256,256]{2,1,0:T(8,128)S(1)}, u32[]{:S(2)}, u32[]{:S(2)}) collective-permute-start(f32[1,256,256]{2,1,0:T(8,128)} %get-tuple-element.19), channel_id=1, source_target_pairs={{0,2},{1,3},{2,0},{3,1},{4,6},{5,7},{6,4},{7,5},{8,10},{9,11},{10,... | collective-permute-start | bytes 786440 | tf_op jit(solution)/shard_map/ppermute | solution.py:327
  30.7 39.5 %copy-start.4 = (bf16[256,256]{1,0:T(8,128)(2,1)S(1)}, bf16[256,256]{1,0:T(8,128)(2,1)}, u32[]{:S(2)}) copy-start(bf16[256,256]{1,0:T(8,128)(2,1)} %student_ref.1) | copy-start | bytes 393220
  30.7 24.2 %all-to-all-start.1 = ((f32[24,1,256]{2,1,0:T(1,128)}), f32[24,1,256]{2,1,0:T(1,128)S(1)}, u32[]{:S(2)}, u32[]{:S(2)}) async-start(f32[24,1,256]{2,1,0:T(1,128)} %get-tuple-element.20), calls=%async_computation.1 | async-start | bytes 49152 | tf_op jit(solution)/shard_map/all_to_all | solution.py:332
  56.1 22.9 %all-to-all-start.2 = ((f32[32,2,1408]{2,1,0:T(2,128)}), f32[32,2,1408]{2,1,0:T(2,128)S(1)}, u32[]{:S(2)}, u32[]{:S(2)}) async-start(f32[32,2,1408]{2,1,0:T(2,128)} %shard_map.61), calls=%async_computation.2 | async-start | bytes 720896 | tf_op jit(solution)/shard_map/all_to_all | solution.py:335
  68.2 31.8 %collective-permute-start.3 = (f32[4,256,256]{2,1,0:T(8,128)}, f32[4,256,256]{2,1,0:T(8,128)S(1)}, u32[]{:S(2)}, u32[]{:S(2)}) collective-permute-start(f32[4,256,256]{2,1,0:T(8,128)} %constant_dynamic-update-slice_fusion.own_ref), channel_id=1, source_target_pairs={{0,32},{32,0},{64,96},{96,64},{128,160},{160,128},{192,224},{224,1... | collective-permute-start | bytes 3145736 | tf_op jit(solution)/shard_map/ppermute | solution.py:340
  94.4 19.8 %all-to-all-start.4 = ((f32[32,2,1536]{2,1,0:T(2,128)}), f32[32,2,1536]{2,1,0:T(2,128)S(1)}, u32[]{:S(2)}, u32[]{:S(2)}) async-start(f32[32,2,1536]{2,1,0:T(2,128)} %shard_map.63), calls=%async_computation.4 | async-start | bytes 786432 | tf_op jit(solution)/shard_map/all_to_all | solution.py:341
  100.0 22.9 %copy-start = (f32[4,256,256]{2,1,0:T(8,128)}, f32[4,256,256]{2,1,0:T(8,128)S(1)}, u32[]{:S(2)}) copy-start(f32[4,256,256]{2,1,0:T(8,128)S(1)} %collective-permute-done.3.refs_2_.other_ref) | copy-start | bytes 3145732
  115.4 0.6 copy-start.1
  116.0 20.1 %copy-start.3 = (f32[4,2,128]{2,1,0:T(2,128)}, f32[4,2,128]{2,1,0:T(2,128)S(1)}, u32[]{:S(2)}) copy-start(f32[4,2,128]{2,1,0:T(2,128)S(1)} %get-tuple-element.29.refs_11_) | copy-start | bytes 12292
  116.0 20.1 %all-to-all-start.5 = ((f32[96,1,256]{2,1,0:T(1,128)}), f32[96,1,256]{2,1,0:T(1,128)S(1)}, u32[]{:S(2)}, u32[]{:S(2)}) async-start(f32[96,1,256]{2,1,0:T(1,128)} %get-tuple-element.24.after_ref), calls=%async_computation.5 | async-start | bytes 196608 | tf_op jit(solution)/shard_map/all_to_all | solution.py:344
  136.1 0.6 copy-start.5
  136.7 9.4 %copy-start.2 = (f32[22,128]{1,0:T(8,128)S(1)}, f32[22,128]{1,0:T(8,128)}, u32[]{:S(2)}) copy-start(f32[22,128]{1,0:T(8,128)} %copy-done.1) | copy-start | bytes 33796
  141.2 27.2 %all-to-all-start.6 = ((f32[32,8,768]{2,1,0:T(8,128)}), f32[32,8,768]{2,1,0:T(8,128)S(1)}, u32[]{:S(2)}, u32[]{:S(2)}) async-start(f32[32,8,768]{2,1,0:T(8,128)} %get-tuple-element.31), calls=%async_computation.6 | async-start | bytes 1572864 | tf_op jit(solution)/shard_map/all_to_all | solution.py:350

commit v10 on v9

--- a/solution.py
+++ b/solution.py
@@ -9,7 +9,7 @@
 
 ITERS = 3
 SMALL, VMEM = 16 * 2**20, 61 * 2**20
-TEAM_VMEM, GRAD_VMEM = 56 * 2**20, 61 * 2**20
+TEAM_VMEM, GRAD_VMEM = 50 * 2**20, 61 * 2**20
 LANES = 128
 HELD = 6
 SPLIT = 4

time: 170 us -> 169 us (level)
    unnamed x17 -> x15, local copies, waits for them, and re-layouts: 3.39 us -> 4.25 us
where the time goes in v10:
time: 169 us
  starting transfers between devices  65.7 us (39%)
  waiting for transfers between devices  57.9 us (34%)
  Pallas kernels  20.6 us (12%)
  blocking collectives  13.3 us (8%)
  local copies, waits for them, and re-layouts  4.96 us (3%)
  other arithmetic  3.23 us (2%)
  matrix products  2.04 us (1%)
    all_to_all x3, starting transfers between devices, local(): came = lax.all_to_all(sent, 'batch', 0, 0, tiled=True)  28 us
    all_to_all x3, waiting for transfers between devices, local(): came = lax.all_to_all(sent, 'batch', 0, 0, tiled=True)  20.9 us
    all_to_all x1, waiting for transfers between devices, local(): parts = lax.all_to_all(grad_t, 'batch', 0, 0, tiled=True)  20.1 us
    all_to_all x1, starting transfers between devices, local(): came = lax.all_to_all(sent, 'proto', 0, 0, tiled=True)  14.2 us
    all_to_all x1, blocking collectives, local(): came = lax.all_to_all(sent, 'proto', 0, 0, tiled=True)  13.3 us
    all_to_all x1, waiting for transfers between devices, local(): came = lax.all_to_all(sent, 'proto', 0, 0, tiled=True)  9.96 us
    ppermute x3, starting transfers between devices, member(): return lax.ppermute(rows, 'batch', [(i, i ^ flip) for i in range(nb)])  9.82 us
    all_to_all x1, starting transfers between devices, local(): lax.all_to_all(sent, ('batch', 'proto'), 0, 0, tiled=True, axis_index_gro...  6.82 us
  transfers between devices with their start and end apart: 10, of which 6 were waited for; matrix products, arithmetic and copies ran while one was open for 5% of the time, Pallas kernels for 6%

profile of v10, /device:TPU:2, one launch (start us, length us, event | category | flops | bytes accessed | tf_op | source)
XLA Modules:
  0.0 168.5 jit_solution(6994880142627215787)
XLA Ops:
  0.6 3.9 %shard_map.59 = (f32[1,256,256]{2,1,0:T(8,128)}, bf16[256,2816]{1,0:T(8,128)(2,1)}, bf16[256,2816]{1,0:T(8,128)(2,1)S(1)}, f32[32,2,1408]{2,1,0:T(2,128)}) custom-call(bf16[256,256]{1,0:T(8,128)(2,1)} %teacher_ref.1, bf16[256,256]{1,0:T(8,128)(2,1)} %student_ref.1, bf16[256,2816]{1,0:T(8,128)(2,1)} %proto_ref.1, f32[22,128]{1,0:T(8,128)} %bitcast.7), custom_call_target="tpu_custom_call" | custom-call | flops 369098752 | bytes 4325376 | tf_op jit(solution)/shard_map/pallas_call | solution.py:147
  4.5 13.2 %all-to-all-start = ((f32[32,2,1408]{2,1,0:T(2,128)}), f32[32,2,1408]{2,1,0:T(2,128)S(1)}, u32[]{:S(2)}, u32[]{:S(2)}) async-start(f32[32,2,1408]{2,1,0:T(2,128)} %get-tuple-element.18), calls=%async_computation | async-start | bytes 720896 | tf_op jit(solution)/shard_map/all_to_all | solution.py:330
  17.8 2.3 %collective-permute-start = (f32[1,256,256]{2,1,0:T(8,128)}, f32[1,256,256]{2,1,0:T(8,128)S(1)}, u32[]{:S(2)}, u32[]{:S(2)}) collective-permute-start(f32[1,256,256]{2,1,0:T(8,128)} %get-tuple-element.19), channel_id=1, source_target_pairs={{0,1},{1,0},{2,3},{3,2},{4,5},{5,4},{6,7},{7,6},{8,9},{9,8},{10,11... | collective-permute-start | bytes 786440 | tf_op jit(solution)/shard_map/ppermute | solution.py:327
  20.0 4.2 %collective-permute-start.1 = (f32[1,256,256]{2,1,0:T(8,128)}, f32[1,256,256]{2,1,0:T(8,128)S(1)}, u32[]{:S(2)}, u32[]{:S(2)}) collective-permute-start(f32[1,256,256]{2,1,0:T(8,128)} %get-tuple-element.19), channel_id=1, source_target_pairs={{0,3},{1,2},{2,1},{3,0},{4,7},{5,6},{6,5},{7,4},{8,11},{9,10},{10,... | collective-permute-start | bytes 786440 | tf_op jit(solution)/shard_map/ppermute | solution.py:327
  24.3 3.4 %collective-permute-start.2 = (f32[1,256,256]{2,1,0:T(8,128)}, f32[1,256,256]{2,1,0:T(8,128)S(1)}, u32[]{:S(2)}, u32[]{:S(2)}) collective-permute-start(f32[1,256,256]{2,1,0:T(8,128)} %get-tuple-element.19), channel_id=1, source_target_pairs={{0,2},{1,3},{2,0},{3,1},{4,6},{5,7},{6,4},{7,5},{8,10},{9,11},{10,... | collective-permute-start | bytes 786440 | tf_op jit(solution)/shard_map/ppermute | solution.py:327
  30.7 14.2 %all-to-all-start.1 = ((f32[24,1,256]{2,1,0:T(1,128)}), f32[24,1,256]{2,1,0:T(1,128)S(1)}, u32[]{:S(2)}, u32[]{:S(2)}) async-start(f32[24,1,256]{2,1,0:T(1,128)} %get-tuple-element.20), calls=%async_computation.1 | async-start | bytes 49152 | tf_op jit(solution)/shard_map/all_to_all | solution.py:332
  44.9 10.0 %all-to-all-done.1.refs_0_ = f32[24,1,256]{2,1,0:T(1,128)S(1)} async-done(((f32[24,1,256]{2,1,0:T(1,128)}), f32[24,1,256]{2,1,0:T(1,128)S(1)}, u32[]{:S(2)}, u32[]{:S(2)}) %all-to-all-start.1) | async-done | bytes 24608 | tf_op jit(solution)/shard_map/all_to_all | solution.py:332
  54.9 1.2 shard_map.61
  56.1 9.3 %all-to-all-start.2 = ((f32[32,2,1408]{2,1,0:T(2,128)}), f32[32,2,1408]{2,1,0:T(2,128)S(1)}, u32[]{:S(2)}, u32[]{:S(2)}) async-start(f32[32,2,1408]{2,1,0:T(2,128)} %shard_map.61), calls=%async_computation.2 | async-start | bytes 720896 | tf_op jit(solution)/shard_map/all_to_all | solution.py:335
  68.3 1.9 %collective-permute-start.3 = (f32[4,256,256]{2,1,0:T(8,128)}, f32[4,256,256]{2,1,0:T(8,128)S(1)}, u32[]{:S(2)}, u32[]{:S(2)}) collective-permute-start(f32[4,256,256]{2,1,0:T(8,128)} %constant_dynamic-update-slice_fusion.own_ref), channel_id=1, source_target_pairs={{0,32},{32,0},{64,96},{96,64},{128,160},{160,128},{192,224},{224,1... | collective-permute-start | bytes 3145736 | tf_op jit(solution)/shard_map/ppermute | solution.py:340
  70.2 2.0 %fusion.1 = f32[256]{0:T(256)S(1)} fusion(bf16[256,2816]{1,0:T(8,128)(2,1)} %get-tuple-element.21.proto_ref, bf16[256,256]{1,0:T(8,128)(2,1)S(1)} %copy-done.3, f32[256]{0:T(256)S(1)} %add_rsqrt_fusion), kind=kOutput, calls=%fused_computation.3 | convolution fusion | flops 370736896 | bytes 1574912 | tf_op jit(solution)/shard_map/dot_general | solution.py:323
  72.2 6.7 %all-to-all-done.2.refs_0_ = f32[32,2,1408]{2,1,0:T(2,128)S(1)} async-done(((f32[32,2,1408]{2,1,0:T(2,128)}), f32[32,2,1408]{2,1,0:T(2,128)S(1)}, u32[]{:S(2)}, u32[]{:S(2)}) %all-to-all-start.2) | async-done | bytes 360480 | tf_op jit(solution)/shard_map/all_to_all | solution.py:335
  80.0 13.3 %all_to_all.35.refs_0_ = f32[24,2,256]{2,1,0:T(2,128)S(1)} all-to-all(f32[24,2,256]{2,1,0:T(2,128)S(1)} %get-tuple-element.22), channel_id=1, replica_groups=mesh['proto'=24,'batch'=32] {'proto'}, dimensions={0} | all-to-all | bytes 98304 | tf_op jit(solution)/shard_map/all_to_all | solution.py:338
  93.2 1.2 shard_map.63
  94.4 5.6 %all-to-all-start.4 = ((f32[32,2,1536]{2,1,0:T(2,128)}), f32[32,2,1536]{2,1,0:T(2,128)S(1)}, u32[]{:S(2)}, u32[]{:S(2)}) async-start(f32[32,2,1536]{2,1,0:T(2,128)} %shard_map.63), calls=%async_computation.4 | async-start | bytes 786432 | tf_op jit(solution)/shard_map/all_to_all | solution.py:341
  100.0 14.2 %all-to-all-done.4.refs_0_ = f32[32,2,1536]{2,1,0:T(2,128)S(1)} async-done(((f32[32,2,1536]{2,1,0:T(2,128)}), f32[32,2,1536]{2,1,0:T(2,128)S(1)}, u32[]{:S(2)}, u32[]{:S(2)}) %all-to-all-start.4) | async-done | bytes 393248 | tf_op jit(solution)/shard_map/all_to_all | solution.py:341
  114.2 1.2 shard_map.64
  115.4 6.8 %all-to-all-start.5 = ((f32[96,1,256]{2,1,0:T(1,128)}), f32[96,1,256]{2,1,0:T(1,128)S(1)}, u32[]{:S(2)}, u32[]{:S(2)}) async-start(f32[96,1,256]{2,1,0:T(1,128)} %get-tuple-element.24.after_ref), calls=%async_computation.5 | async-start | bytes 196608 | tf_op jit(solution)/shard_map/all_to_all | solution.py:344
  122.3 5.9 %shard_map.65 = (bf16[768,1024]{1,0:T(8,128)(2,1)}, f32[768,1024]{1,0:T(8,128)}, bf16[1024,256]{1,0:T(8,128)(2,1)S(1)}, f32[22,128]{1,0:T(8,128)S(1)}) custom-call(f32[4,256,256]{2,1,0:T(8,128)} %constant_dynamic-update-slice_fusion.own_ref, f32[4,256,256]{2,1,0:T(8,128)S(1)} %collective-permute-done.3.refs_2_.other_ref, ...), custom_call_target="tpu_custom_call" | custom-call | flops 805306368 | bytes 10485760 | tf_op jit(solution)/shard_map/pallas_call | solution.py:279
  129.5 6.0 %all-to-all-done.5.refs_10_ = f32[96,1,256]{2,1,0:T(1,128)S(1)} async-done(((f32[96,1,256]{2,1,0:T(1,128)}), f32[96,1,256]{2,1,0:T(1,128)S(1)}, u32[]{:S(2)}, u32[]{:S(2)}) %all-to-all-start.5) | async-done | bytes 98336 | tf_op jit(solution)/shard_map/all_to_all | solution.py:344
  136.2 4.4 %shard_map.66 = (f32[32,8,768]{2,1,0:T(8,128)}, f32[1,256]{1,0:T(1,128)}) custom-call(bf16[768,1024]{1,0:T(8,128)(2,1)} %get-tuple-element.25.refs_0_.refs_1_.refs_2_.refs_3_, bf16[768,1024]{1,0:T(8,128)(2,1)} %get-tuple-element.25.refs_0_.refs_1_.refs_2_.refs_3_, bf16[768,1024]{1,0:T(8,128)(2,1)} %get-tuple-element.25.refs_0_.refs_1_.refs_2_.refs_3_, ...), custom_call_target="tpu_custom_call" | custom-call | flops 402653184 | bytes 4718592 | tf_op jit(solution)/shard_map/pallas_call | solution.py:74
  140.6 4.9 %all-to-all-start.6 = ((f32[32,8,768]{2,1,0:T(8,128)}), f32[32,8,768]{2,1,0:T(8,128)S(1)}, u32[]{:S(2)}, u32[]{:S(2)}) async-start(f32[32,8,768]{2,1,0:T(8,128)} %get-tuple-element.31), calls=%async_computation.6 | async-start | bytes 1572864 | tf_op jit(solution)/shard_map/all_to_all | solution.py:350
  145.5 2.2 %multiply_convert_fusion = bf16[256,2816]{1,0:T(8,128)(2,1)} fusion(bf16[256,2816]{1,0:T(8,128)(2,1)S(1)} %get-tuple-element.17.refs_1_, f32[256]{0:T(256)} %bitcast.8, f32[2816]{0:T(1024)S(1)} %bitcast.5), kind=kLoop, calls=%fused_computation.2 | loop fusion | flops 3604480 | bytes 2895872 | tf_op jit(solution)/shard_map/convert_element_type | solution.py:359
  147.7 20.1 %all-to-all-done.6.parts_ref = f32[32,8,768]{2,1,0:T(8,128)S(1)} async-done(((f32[32,8,768]{2,1,0:T(8,128)}), f32[32,8,768]{2,1,0:T(8,128)S(1)}, u32[]{:S(2)}, u32[]{:S(2)}) %all-to-all-start.6) | async-done | bytes 786464 | tf_op jit(solution)/shard_map/all_to_all | solution.py:350
  (26 shorter events, 9.7 us)
Async XLA Ops:
  4.5 60.8 %copy-start.5 = (f32[1,256,256]{2,1,0:T(8,128)S(1)}, f32[1,256,256]{2,1,0:T(8,128)}, u32[]{:S(2)}) copy-start(f32[1,256,256]{2,1,0:T(8,128)} %get-tuple-element.19) | copy-start | bytes 786436
  4.5 25.0 %all-to-all-start = ((f32[32,2,1408]{2,1,0:T(2,128)}), f32[32,2,1408]{2,1,0:T(2,128)S(1)}, u32[]{:S(2)}, u32[]{:S(2)}) async-start(f32[32,2,1408]{2,1,0:T(2,128)} %get-tuple-element.18), calls=%async_computation | async-start | bytes 720896 | tf_op jit(solution)/shard_map/all_to_all | solution.py:330
  17.8 11.7 %collective-permute-start = (f32[1,256,256]{2,1,0:T(8,128)}, f32[1,256,256]{2,1,0:T(8,128)S(1)}, u32[]{:S(2)}, u32[]{:S(2)}) collective-permute-start(f32[1,256,256]{2,1,0:T(8,128)} %get-tuple-element.19), channel_id=1, source_target_pairs={{0,1},{1,0},{2,3},{3,2},{4,5},{5,4},{6,7},{7,6},{8,9},{9,8},{10,11... | collective-permute-start | bytes 786440 | tf_op jit(solution)/shard_map/ppermute | solution.py:327
  20.0 24.9 %collective-permute-start.1 = (f32[1,256,256]{2,1,0:T(8,128)}, f32[1,256,256]{2,1,0:T(8,128)S(1)}, u32[]{:S(2)}, u32[]{:S(2)}) collective-permute-start(f32[1,256,256]{2,1,0:T(8,128)} %get-tuple-element.19), channel_id=1, source_target_pairs={{0,3},{1,2},{2,1},{3,0},{4,7},{5,6},{6,5},{7,4},{8,11},{9,10},{10,... | collective-permute-start | bytes 786440 | tf_op jit(solution)/shard_map/ppermute | solution.py:327
  24.3 42.6 %collective-permute-start.2 = (f32[1,256,256]{2,1,0:T(8,128)}, f32[1,256,256]{2,1,0:T(8,128)S(1)}, u32[]{:S(2)}, u32[]{:S(2)}) collective-permute-start(f32[1,256,256]{2,1,0:T(8,128)} %get-tuple-element.19), channel_id=1, source_target_pairs={{0,2},{1,3},{2,0},{3,1},{4,6},{5,7},{6,4},{7,5},{8,10},{9,11},{10,... | collective-permute-start | bytes 786440 | tf_op jit(solution)/shard_map/ppermute | solution.py:327
  30.7 39.5 %copy-start.3 = (bf16[256,256]{1,0:T(8,128)(2,1)S(1)}, bf16[256,256]{1,0:T(8,128)(2,1)}, u32[]{:S(2)}) copy-start(bf16[256,256]{1,0:T(8,128)(2,1)} %student_ref.1) | copy-start | bytes 393220
  30.7 24.2 %all-to-all-start.1 = ((f32[24,1,256]{2,1,0:T(1,128)}), f32[24,1,256]{2,1,0:T(1,128)S(1)}, u32[]{:S(2)}, u32[]{:S(2)}) async-start(f32[24,1,256]{2,1,0:T(1,128)} %get-tuple-element.20), calls=%async_computation.1 | async-start | bytes 49152 | tf_op jit(solution)/shard_map/all_to_all | solution.py:332
  56.1 22.9 %all-to-all-start.2 = ((f32[32,2,1408]{2,1,0:T(2,128)}), f32[32,2,1408]{2,1,0:T(2,128)S(1)}, u32[]{:S(2)}, u32[]{:S(2)}) async-start(f32[32,2,1408]{2,1,0:T(2,128)} %shard_map.61), calls=%async_computation.2 | async-start | bytes 720896 | tf_op jit(solution)/shard_map/all_to_all | solution.py:335
  68.3 31.7 %collective-permute-start.3 = (f32[4,256,256]{2,1,0:T(8,128)}, f32[4,256,256]{2,1,0:T(8,128)S(1)}, u32[]{:S(2)}, u32[]{:S(2)}) collective-permute-start(f32[4,256,256]{2,1,0:T(8,128)} %constant_dynamic-update-slice_fusion.own_ref), channel_id=1, source_target_pairs={{0,32},{32,0},{64,96},{96,64},{128,160},{160,128},{192,224},{224,1... | collective-permute-start | bytes 3145736 | tf_op jit(solution)/shard_map/ppermute | solution.py:340
  94.4 19.8 %all-to-all-start.4 = ((f32[32,2,1536]{2,1,0:T(2,128)}), f32[32,2,1536]{2,1,0:T(2,128)S(1)}, u32[]{:S(2)}, u32[]{:S(2)}) async-start(f32[32,2,1536]{2,1,0:T(2,128)} %shard_map.63), calls=%async_computation.4 | async-start | bytes 786432 | tf_op jit(solution)/shard_map/all_to_all | solution.py:341
  115.4 20.1 %copy-start.2 = (f32[4,2,128]{2,1,0:T(2,128)}, f32[4,2,128]{2,1,0:T(2,128)S(1)}, u32[]{:S(2)}) copy-start(f32[4,2,128]{2,1,0:T(2,128)S(1)} %get-tuple-element.29.refs_11_) | copy-start | bytes 12292
  115.4 20.1 %all-to-all-start.5 = ((f32[96,1,256]{2,1,0:T(1,128)}), f32[96,1,256]{2,1,0:T(1,128)S(1)}, u32[]{:S(2)}, u32[]{:S(2)}) async-start(f32[96,1,256]{2,1,0:T(1,128)} %get-tuple-element.24.after_ref), calls=%async_computation.5 | async-start | bytes 196608 | tf_op jit(solution)/shard_map/all_to_all | solution.py:344
  128.1 0.8 copy-start
  128.9 0.6 copy-start.1
  135.5 0.7 copy-start.4
  140.6 27.2 %all-to-all-start.6 = ((f32[32,8,768]{2,1,0:T(8,128)}), f32[32,8,768]{2,1,0:T(8,128)S(1)}, u32[]{:S(2)}, u32[]{:S(2)}) async-start(f32[32,8,768]{2,1,0:T(8,128)} %get-tuple-element.31), calls=%async_computation.6 | async-start | bytes 1572864 | tf_op jit(solution)/shard_map/all_to_all | solution.py:350

commit v11 on v10

--- a/solution.py
+++ b/solution.py
@@ -9,7 +9,7 @@
 
 ITERS = 3
 SMALL, VMEM = 16 * 2**20, 61 * 2**20
-TEAM_VMEM, GRAD_VMEM = 50 * 2**20, 61 * 2**20
+TEAM_VMEM, GRAD_VMEM = 50 * 2**20, 52 * 2**20
 LANES = 128
 HELD = 6
 SPLIT = 4

time: 169 us -> 168 us (level)
  waiting for transfers between devices: 57.9 us -> 60 us
  local copies, waits for them, and re-layouts: 4.96 us -> 2.94 us
    unnamed x15 -> x7, local copies, waits for them, and re-layouts: 4.25 us -> 2.21 us
where the time goes in v11:
time: 168 us; the launch traced here: 167 us
  starting transfers between devices  65.7 us (39%)
  waiting for transfers between devices  60 us (36%)
  Pallas kernels  20.2 us (12%)
  blocking collectives  13.3 us (8%)
  local copies, waits for them, and re-layouts  2.94 us (2%)
  other arithmetic  2.56 us (2%)
  matrix products  2.04 us (1%)
    all_to_all x3, starting transfers between devices, local(): came = lax.all_to_all(sent, 'batch', 0, 0, tiled=True)  28 us
    all_to_all x3, waiting for transfers between devices, local(): came = lax.all_to_all(sent, 'batch', 0, 0, tiled=True)  20.9 us
    all_to_all x1, waiting for transfers between devices, local(): parts = lax.all_to_all(grad_t, 'batch', 0, 0, tiled=True)  20.8 us
    all_to_all x1, starting transfers between devices, local(): came = lax.all_to_all(sent, 'proto', 0, 0, tiled=True)  14.2 us
    all_to_all x1, blocking collectives, local(): came = lax.all_to_all(sent, 'proto', 0, 0, tiled=True)  13.3 us
    all_to_all x1, waiting for transfers between devices, local(): came = lax.all_to_all(sent, 'proto', 0, 0, tiled=True)  9.96 us
    ppermute x3, starting transfers between devices, member(): return lax.ppermute(rows, 'batch', [(i, i ^ flip) for i in range(nb)])  9.82 us
    all_to_all x1, waiting for transfers between devices, local(): lax.all_to_all(sent, ('batch', 'proto'), 0, 0, tiled=True, axis_index_gro...  7.42 us
  transfers between devices with their start and end apart: 10, of which 6 were waited for; matrix products, arithmetic and copies ran while one was open for 5% of the time, Pallas kernels for 6%

profile of v11, /device:TPU:2, one launch (start us, length us, event | category | flops | bytes accessed | tf_op | source)
XLA Modules:
  0.0 167.4 jit_solution(6020920458524441329)
XLA Ops:
  0.6 3.9 %shard_map.59 = (f32[1,256,256]{2,1,0:T(8,128)}, bf16[256,2816]{1,0:T(8,128)(2,1)}, bf16[256,2816]{1,0:T(8,128)(2,1)S(1)}, f32[32,2,1408]{2,1,0:T(2,128)}) custom-call(bf16[256,256]{1,0:T(8,128)(2,1)} %teacher_ref.1, bf16[256,256]{1,0:T(8,128)(2,1)} %student_ref.1, bf16[256,2816]{1,0:T(8,128)(2,1)} %proto_ref.1, f32[22,128]{1,0:T(8,128)} %bitcast.8), custom_call_target="tpu_custom_call" | custom-call | flops 369098752 | bytes 4325376 | tf_op jit(solution)/shard_map/pallas_call | solution.py:147
  4.6 13.2 %all-to-all-start = ((f32[32,2,1408]{2,1,0:T(2,128)}), f32[32,2,1408]{2,1,0:T(2,128)S(1)}, u32[]{:S(2)}, u32[]{:S(2)}) async-start(f32[32,2,1408]{2,1,0:T(2,128)} %get-tuple-element.18), calls=%async_computation | async-start | bytes 720896 | tf_op jit(solution)/shard_map/all_to_all | solution.py:330
  17.8 2.3 %collective-permute-start = (f32[1,256,256]{2,1,0:T(8,128)}, f32[1,256,256]{2,1,0:T(8,128)S(1)}, u32[]{:S(2)}, u32[]{:S(2)}) collective-permute-start(f32[1,256,256]{2,1,0:T(8,128)} %get-tuple-element.19), channel_id=1, source_target_pairs={{0,1},{1,0},{2,3},{3,2},{4,5},{5,4},{6,7},{7,6},{8,9},{9,8},{10,11... | collective-permute-start | bytes 786440 | tf_op jit(solution)/shard_map/ppermute | solution.py:327
  20.1 4.2 %collective-permute-start.1 = (f32[1,256,256]{2,1,0:T(8,128)}, f32[1,256,256]{2,1,0:T(8,128)S(1)}, u32[]{:S(2)}, u32[]{:S(2)}) collective-permute-start(f32[1,256,256]{2,1,0:T(8,128)} %get-tuple-element.19), channel_id=1, source_target_pairs={{0,3},{1,2},{2,1},{3,0},{4,7},{5,6},{6,5},{7,4},{8,11},{9,10},{10,... | collective-permute-start | bytes 786440 | tf_op jit(solution)/shard_map/ppermute | solution.py:327
  24.3 3.4 %collective-permute-start.2 = (f32[1,256,256]{2,1,0:T(8,128)}, f32[1,256,256]{2,1,0:T(8,128)S(1)}, u32[]{:S(2)}, u32[]{:S(2)}) collective-permute-start(f32[1,256,256]{2,1,0:T(8,128)} %get-tuple-element.19), channel_id=1, source_target_pairs={{0,2},{1,3},{2,0},{3,1},{4,6},{5,7},{6,4},{7,5},{8,10},{9,11},{10,... | collective-permute-start | bytes 786440 | tf_op jit(solution)/shard_map/ppermute | solution.py:327
  30.7 14.2 %all-to-all-start.1 = ((f32[24,1,256]{2,1,0:T(1,128)}), f32[24,1,256]{2,1,0:T(1,128)S(1)}, u32[]{:S(2)}, u32[]{:S(2)}) async-start(f32[24,1,256]{2,1,0:T(1,128)} %get-tuple-element.20), calls=%async_computation.1 | async-start | bytes 49152 | tf_op jit(solution)/shard_map/all_to_all | solution.py:332
  45.0 10.0 %all-to-all-done.1.refs_0_ = f32[24,1,256]{2,1,0:T(1,128)S(1)} async-done(((f32[24,1,256]{2,1,0:T(1,128)}), f32[24,1,256]{2,1,0:T(1,128)S(1)}, u32[]{:S(2)}, u32[]{:S(2)}) %all-to-all-start.1) | async-done | bytes 24608 | tf_op jit(solution)/shard_map/all_to_all | solution.py:332
  54.9 1.2 shard_map.61
  56.1 9.3 %all-to-all-start.2 = ((f32[32,2,1408]{2,1,0:T(2,128)}), f32[32,2,1408]{2,1,0:T(2,128)S(1)}, u32[]{:S(2)}, u32[]{:S(2)}) async-start(f32[32,2,1408]{2,1,0:T(2,128)} %shard_map.61), calls=%async_computation.2 | async-start | bytes 720896 | tf_op jit(solution)/shard_map/all_to_all | solution.py:335
  68.3 1.9 %collective-permute-start.3 = (f32[4,256,256]{2,1,0:T(8,128)}, f32[4,256,256]{2,1,0:T(8,128)S(1)}, u32[]{:S(2)}, u32[]{:S(2)}) collective-permute-start(f32[4,256,256]{2,1,0:T(8,128)} %constant_dynamic-update-slice_fusion.own_ref), channel_id=1, source_target_pairs={{0,32},{32,0},{64,96},{96,64},{128,160},{160,128},{192,224},{224,1... | collective-permute-start | bytes 3145736 | tf_op jit(solution)/shard_map/ppermute | solution.py:340
  70.2 2.0 %fusion.1 = f32[256]{0:T(256)S(1)} fusion(bf16[256,2816]{1,0:T(8,128)(2,1)} %get-tuple-element.21.proto_ref, bf16[256,256]{1,0:T(8,128)(2,1)S(1)} %copy-done, f32[256]{0:T(256)S(1)} %add_rsqrt_fusion), kind=kOutput, calls=%fused_computation.3 | convolution fusion | flops 370736896 | bytes 1574912 | tf_op jit(solution)/shard_map/dot_general | solution.py:323
  72.3 6.7 %all-to-all-done.2.refs_0_ = f32[32,2,1408]{2,1,0:T(2,128)S(1)} async-done(((f32[32,2,1408]{2,1,0:T(2,128)}), f32[32,2,1408]{2,1,0:T(2,128)S(1)}, u32[]{:S(2)}, u32[]{:S(2)}) %all-to-all-start.2) | async-done | bytes 360480 | tf_op jit(solution)/shard_map/all_to_all | solution.py:335
  80.0 13.3 %all_to_all.35.refs_0_ = f32[24,2,256]{2,1,0:T(2,128)S(1)} all-to-all(f32[24,2,256]{2,1,0:T(2,128)S(1)} %get-tuple-element.22), channel_id=1, replica_groups=mesh['proto'=24,'batch'=32] {'proto'}, dimensions={0} | all-to-all | bytes 98304 | tf_op jit(solution)/shard_map/all_to_all | solution.py:338
  93.3 1.2 shard_map.63
  94.4 5.6 %all-to-all-start.4 = ((f32[32,2,1536]{2,1,0:T(2,128)}), f32[32,2,1536]{2,1,0:T(2,128)S(1)}, u32[]{:S(2)}, u32[]{:S(2)}) async-start(f32[32,2,1536]{2,1,0:T(2,128)} %shard_map.63), calls=%async_computation.4 | async-start | bytes 786432 | tf_op jit(solution)/shard_map/all_to_all | solution.py:341
  100.0 14.2 %all-to-all-done.4.refs_0_ = f32[32,2,1536]{2,1,0:T(2,128)S(1)} async-done(((f32[32,2,1536]{2,1,0:T(2,128)}), f32[32,2,1536]{2,1,0:T(2,128)S(1)}, u32[]{:S(2)}, u32[]{:S(2)}) %all-to-all-start.4) | async-done | bytes 393248 | tf_op jit(solution)/shard_map/all_to_all | solution.py:341
  114.2 1.2 shard_map.64
  115.4 6.8 %all-to-all-start.5 = ((f32[96,1,256]{2,1,0:T(1,128)}), f32[96,1,256]{2,1,0:T(1,128)S(1)}, u32[]{:S(2)}, u32[]{:S(2)}) async-start(f32[96,1,256]{2,1,0:T(1,128)} %get-tuple-element.24.after_ref), calls=%async_computation.5 | async-start | bytes 196608 | tf_op jit(solution)/shard_map/all_to_all | solution.py:344
  122.3 5.8 %shard_map.65 = (bf16[768,1024]{1,0:T(8,128)(2,1)}, f32[768,1024]{1,0:T(8,128)}, bf16[1024,256]{1,0:T(8,128)(2,1)S(1)}, f32[22,128]{1,0:T(8,128)S(1)}) custom-call(f32[4,256,256]{2,1,0:T(8,128)} %constant_dynamic-update-slice_fusion.own_ref, f32[4,256,256]{2,1,0:T(8,128)S(1)} %collective-permute-done.3.refs_2_.other_ref, ...), custom_call_target="tpu_custom_call" | custom-call | flops 805306368 | bytes 10485760 | tf_op jit(solution)/shard_map/pallas_call | solution.py:279
  128.1 7.4 %all-to-all-done.5.refs_10_ = f32[96,1,256]{2,1,0:T(1,128)S(1)} async-done(((f32[96,1,256]{2,1,0:T(1,128)}), f32[96,1,256]{2,1,0:T(1,128)S(1)}, u32[]{:S(2)}, u32[]{:S(2)}) %all-to-all-start.5) | async-done | bytes 98336 | tf_op jit(solution)/shard_map/all_to_all | solution.py:344
  135.5 4.0 %shard_map.66 = (f32[32,8,768]{2,1,0:T(8,128)}, f32[1,256]{1,0:T(1,128)S(1)}) custom-call(bf16[768,1024]{1,0:T(8,128)(2,1)} %get-tuple-element.25.refs_0_.refs_1_.refs_2_.refs_3_, bf16[768,1024]{1,0:T(8,128)(2,1)} %get-tuple-element.25.refs_0_.refs_1_.refs_2_.refs_3_, bf16[768,1024]{1,0:T(8,128)(2,1)} %get-tuple-element.25.refs_0_.refs_1_.refs_2_.refs_3_, ...), custom_call_target="tpu_custom_call" | custom-call | flops 402653184 | bytes 4718592 | tf_op jit(solution)/shard_map/pallas_call | solution.py:74
  139.5 4.8 %all-to-all-start.6 = ((f32[32,8,768]{2,1,0:T(8,128)}), f32[32,8,768]{2,1,0:T(8,128)S(1)}, u32[]{:S(2)}, u32[]{:S(2)}) async-start(f32[32,8,768]{2,1,0:T(8,128)} %get-tuple-element.31), calls=%async_computation.6 | async-start | bytes 1572864 | tf_op jit(solution)/shard_map/all_to_all | solution.py:350
  144.4 1.5 multiply_convert_fusion
  145.9 20.8 %all-to-all-done.6.parts_ref = f32[32,8,768]{2,1,0:T(8,128)S(1)} async-done(((f32[32,8,768]{2,1,0:T(8,128)}), f32[32,8,768]{2,1,0:T(8,128)S(1)}, u32[]{:S(2)}, u32[]{:S(2)}) %all-to-all-start.6) | async-done | bytes 786464 | tf_op jit(solution)/shard_map/all_to_all | solution.py:350
  (18 shorter events, 7.7 us)
Async XLA Ops:
  4.6 60.8 %copy-start.1 = (f32[1,256,256]{2,1,0:T(8,128)S(1)}, f32[1,256,256]{2,1,0:T(8,128)}, u32[]{:S(2)}) copy-start(f32[1,256,256]{2,1,0:T(8,128)} %get-tuple-element.19) | copy-start | bytes 786436
  4.6 25.0 %all-to-all-start = ((f32[32,2,1408]{2,1,0:T(2,128)}), f32[32,2,1408]{2,1,0:T(2,128)S(1)}, u32[]{:S(2)}, u32[]{:S(2)}) async-start(f32[32,2,1408]{2,1,0:T(2,128)} %get-tuple-element.18), calls=%async_computation | async-start | bytes 720896 | tf_op jit(solution)/shard_map/all_to_all | solution.py:330
  17.8 11.7 %collective-permute-start = (f32[1,256,256]{2,1,0:T(8,128)}, f32[1,256,256]{2,1,0:T(8,128)S(1)}, u32[]{:S(2)}, u32[]{:S(2)}) collective-permute-start(f32[1,256,256]{2,1,0:T(8,128)} %get-tuple-element.19), channel_id=1, source_target_pairs={{0,1},{1,0},{2,3},{3,2},{4,5},{5,4},{6,7},{7,6},{8,9},{9,8},{10,11... | collective-permute-start | bytes 786440 | tf_op jit(solution)/shard_map/ppermute | solution.py:327
  20.1 24.9 %collective-permute-start.1 = (f32[1,256,256]{2,1,0:T(8,128)}, f32[1,256,256]{2,1,0:T(8,128)S(1)}, u32[]{:S(2)}, u32[]{:S(2)}) collective-permute-start(f32[1,256,256]{2,1,0:T(8,128)} %get-tuple-element.19), channel_id=1, source_target_pairs={{0,3},{1,2},{2,1},{3,0},{4,7},{5,6},{6,5},{7,4},{8,11},{9,10},{10,... | collective-permute-start | bytes 786440 | tf_op jit(solution)/shard_map/ppermute | solution.py:327
  24.3 42.5 %collective-permute-start.2 = (f32[1,256,256]{2,1,0:T(8,128)}, f32[1,256,256]{2,1,0:T(8,128)S(1)}, u32[]{:S(2)}, u32[]{:S(2)}) collective-permute-start(f32[1,256,256]{2,1,0:T(8,128)} %get-tuple-element.19), channel_id=1, source_target_pairs={{0,2},{1,3},{2,0},{3,1},{4,6},{5,7},{6,4},{7,5},{8,10},{9,11},{10,... | collective-permute-start | bytes 786440 | tf_op jit(solution)/shard_map/ppermute | solution.py:327
  30.7 39.5 %copy-start = (bf16[256,256]{1,0:T(8,128)(2,1)S(1)}, bf16[256,256]{1,0:T(8,128)(2,1)}, u32[]{:S(2)}) copy-start(bf16[256,256]{1,0:T(8,128)(2,1)} %student_ref.1) | copy-start | bytes 393220
  30.7 24.2 %all-to-all-start.1 = ((f32[24,1,256]{2,1,0:T(1,128)}), f32[24,1,256]{2,1,0:T(1,128)S(1)}, u32[]{:S(2)}, u32[]{:S(2)}) async-start(f32[24,1,256]{2,1,0:T(1,128)} %get-tuple-element.20), calls=%async_computation.1 | async-start | bytes 49152 | tf_op jit(solution)/shard_map/all_to_all | solution.py:332
  56.1 22.9 %all-to-all-start.2 = ((f32[32,2,1408]{2,1,0:T(2,128)}), f32[32,2,1408]{2,1,0:T(2,128)S(1)}, u32[]{:S(2)}, u32[]{:S(2)}) async-start(f32[32,2,1408]{2,1,0:T(2,128)} %shard_map.61), calls=%async_computation.2 | async-start | bytes 720896 | tf_op jit(solution)/shard_map/all_to_all | solution.py:335
  68.3 31.7 %collective-permute-start.3 = (f32[4,256,256]{2,1,0:T(8,128)}, f32[4,256,256]{2,1,0:T(8,128)S(1)}, u32[]{:S(2)}, u32[]{:S(2)}) collective-permute-start(f32[4,256,256]{2,1,0:T(8,128)} %constant_dynamic-update-slice_fusion.own_ref), channel_id=1, source_target_pairs={{0,32},{32,0},{64,96},{96,64},{128,160},{160,128},{192,224},{224,1... | collective-permute-start | bytes 3145736 | tf_op jit(solution)/shard_map/ppermute | solution.py:340
  94.4 19.8 %all-to-all-start.4 = ((f32[32,2,1536]{2,1,0:T(2,128)}), f32[32,2,1536]{2,1,0:T(2,128)S(1)}, u32[]{:S(2)}, u32[]{:S(2)}) async-start(f32[32,2,1536]{2,1,0:T(2,128)} %shard_map.63), calls=%async_computation.4 | async-start | bytes 786432 | tf_op jit(solution)/shard_map/all_to_all | solution.py:341
  115.4 20.1 %all-to-all-start.5 = ((f32[96,1,256]{2,1,0:T(1,128)}), f32[96,1,256]{2,1,0:T(1,128)S(1)}, u32[]{:S(2)}, u32[]{:S(2)}) async-start(f32[96,1,256]{2,1,0:T(1,128)} %get-tuple-element.24.after_ref), calls=%async_computation.5 | async-start | bytes 196608 | tf_op jit(solution)/shard_map/all_to_all | solution.py:344
  139.5 27.2 %all-to-all-start.6 = ((f32[32,8,768]{2,1,0:T(8,128)}), f32[32,8,768]{2,1,0:T(8,128)S(1)}, u32[]{:S(2)}, u32[]{:S(2)}) async-start(f32[32,8,768]{2,1,0:T(8,128)} %get-tuple-element.31), calls=%async_computation.6 | async-start | bytes 1572864 | tf_op jit(solution)/shard_map/all_to_all | solution.py:350
